TPU v7x, 128 devices: a whole 4x4x4 slice. The times are simulated.
128 devices in a mesh: dom: 128 (over y, x, z, core).
Axes of the slice: x: 4, y: 4, z: 4, core: 2. Of those that a mesh axis runs over, the one named last changes fastest.
Arguments:
- positions: float32 [204800, 3, 128], P('dom'), may hold values from 0 to 1
- velocity: float32 [204800, 3, 128], P('dom'), may hold values from -6 to 6
- mass: float32 [204800, 128], P('dom'), may hold values from 0.004 to 0.016
- smoothing: float32 [204800, 128], P('dom'), may hold values from 0.35 to 0.7
- energy: float32 [204800, 128], P('dom'), may hold values from 0.5 to 2
- density_old: float32 [204800, 128], P('dom'), may hold values from 0.3 to 3
- counts: int32 [204800], P('dom'), may hold values from 64 to 128
- active: int32 [2048], P('dom'), may hold values from 0 to 204799, as said below
- neighbours: int32 [2048, 27], P('dom'), may hold values from 0 to 204799, as said below
Outputs:
- hydro: float32 [2048, 5, 128], P('dom')
Inputs may be any that keep to these rules, and one draw needn't show every extreme that they name: `active`: Distinct. The entries at positions k * 16 to (k + 1) * 16 - 1 are cells of device k; cells k * 1600 to (k + 1) * 1600 - 1 belong to device k. Domains lie in a box with helical periodic boundaries: the +z, +y and +x neighbours of device d's domain are devices d + 1, d + 4 and d + 16, modulo the number of devices. A device's active cells run along the high x-y edge of its domain, the last of its 16 rows being the high corner cell. So in row a of device d, slot k names a cell of device (d + 16 bx + 4 by + bz) modulo the number of devices, where bx = 1 if k // 9 == 2 else 0, by = 1 if (k // 3) % 3 == 2 else 0, and bz = 1 if k % 3 == 2 and a is the device's last row, else 0. Slot 13 of row a is active[a]. Entries may repeat.
All inputs are finite; a program needn't handle non-finite values.
Results may differ from a plain program's by a relative error of at most 0.0003.
Values sent between devices are 32-bit elements; how exact they have to be, the bound alone decides.
A program may use at most 64 MiB of HBM per device.

v0:
```python
import math

import jax
import jax.numpy as jnp
from jax import lax
from jax.sharding import PartitionSpec as P

kernel_norm = 8.0 / math.pi
gas_factor = 2.0 / 3.0


def from_behind(value, axis, steps):
    count = lax.axis_size(axis)
    pairs = [(source, (source + steps) % count) for source in range(count)]
    return lax.ppermute(value, axis, pairs)


def kernel_value(dist_sq, smooth):
    ratio = jnp.sqrt(dist_sq) / smooth
    inner = 1.0 - 6.0 * ratio**2 + 6.0 * ratio**3
    outer = 2.0 * jnp.maximum(1.0 - ratio, 0.0) ** 3
    return kernel_norm / smooth**3 * jnp.where(ratio < 0.5, inner, outer)


def kernel_slope(dist_sq, smooth):
    ratio = jnp.sqrt(dist_sq) / smooth
    inner = -12.0 + 18.0 * ratio
    outer = -6.0 * jnp.maximum(1.0 - ratio, 0.0) ** 2 / jnp.maximum(ratio, 0.5)
    return kernel_norm / smooth**5 * jnp.where(ratio < 0.5, inner, outer)


def slot_shift(slot):
    return jnp.stack([slot // 9 - 1, slot // 3 % 3 - 1, slot % 3 - 1]).astype(jnp.float32)


def slot_codes(rows):
    codes = []
    for row in range(rows):
        for slot in range(27):
            bit_x = 1 if slot // 9 == 2 else 0
            bit_y = 1 if slot // 3 % 3 == 2 else 0
            bit_z = 1 if slot % 3 == 2 and row == rows - 1 else 0
            codes.append(4 * bit_x + 2 * bit_y + bit_z)
    return codes


def positions_of(codes, wanted):
    return [place for place, code in enumerate(codes) if code == wanted]


def shards(positions, velocity, mass, smoothing, energy, density_old, counts, active, neighbours):
    cells_dev = positions.shape[0]
    slots_dev = active.shape[0]
    devices = lax.axis_size("dom")
    me_index = lax.axis_index("dom")
    first_cell = me_index * cells_dev
    valid = (jnp.arange(128, dtype=jnp.int32)[None, :] < counts[:, None]).astype(jnp.float32)
    weighed = mass * valid
    own_cells = active - first_cell
    flat_cells = neighbours.reshape(-1)
    codes = slot_codes(slots_dev)
    home_slots = positions_of(codes, 0)
    lists = [positions_of(codes, code) for code in range(1, 8)]
    steps_by = [16 * (code >> 2) + 4 * (code >> 1 & 1) + (code & 1) for code in range(1, 8)]
    order = list(home_slots)
    for entries in lists:
        order = order + entries
    backward = [0] * len(order)
    for place, entry in enumerate(order):
        backward[entry] = place
    slot_major = [backward[row * 27 + slot] for slot in range(27) for row in range(slots_dev)]
    inverse = jnp.asarray(slot_major, dtype=jnp.int32)
    home_index = flat_cells[jnp.asarray(home_slots, dtype=jnp.int32)] - first_cell
    served = []
    for place in range(7):
        target = (me_index + steps_by[place]) % devices
        asked = flat_cells[jnp.asarray(lists[place], dtype=jnp.int32)] - target * cells_dev
        served.append(from_behind(asked, "dom", steps_by[place]))

    def arrange(pieces):
        joined = jnp.concatenate(pieces, axis=0)[inverse]
        return joined.reshape((27, slots_dev, joined.shape[1]))

    flat_pos = positions.reshape(cells_dev, 384)
    static_table = jnp.concatenate([flat_pos, weighed], axis=1)
    moving_table = jnp.concatenate([velocity.reshape(cells_dev, 384), smoothing, energy], axis=1)
    pieces = [static_table[home_index]]
    for place in range(7):
        pieces.append(from_behind(static_table[served[place]], "dom", -steps_by[place]))
    near_static = arrange(pieces)
    pos_own = flat_pos[own_cells].reshape(slots_dev, 3, 128)
    smooth_own = smoothing[own_cells]
    valid_own = valid[own_cells]
    slot_ids = jnp.arange(27, dtype=jnp.int32)

    def density_step(total, items):
        slot, near = items
        pos_near = near[:, 0:384].reshape(slots_dev, 3, 128) + slot_shift(slot)[None, :, None]
        gap = pos_own[:, :, :, None] - pos_near[:, :, None, :]
        dist_sq = jnp.sum(gap * gap, axis=1)
        weight = kernel_value(dist_sq, smooth_own[:, :, None])
        return (total + jnp.sum(near[:, None, 384:512] * weight, axis=2), None)

    fresh, _ = lax.scan(
        density_step, jnp.zeros((slots_dev, 128), jnp.float32), (slot_ids, near_static)
    )
    fresh = jnp.where(valid_own > 0, fresh, density_old[own_cells])
    table = density_old.at[own_cells].set(fresh)
    dynamic_table = jnp.concatenate([moving_table, table], axis=1)
    pieces = [dynamic_table[home_index]]
    for place in range(7):
        pieces.append(from_behind(dynamic_table[served[place]], "dom", -steps_by[place]))
    near_moving = arrange(pieces)
    rho_near = near_moving[:, :, 640:768]
    vel_own = velocity[own_cells]
    energy_own = energy[own_cells]
    press_own = gas_factor * fresh * energy_own / (fresh * fresh)

    def force_step(carry, items):
        accel_sum, rate_sum = carry
        slot, near, moving, rho_part = items
        pos_near = near[:, 0:384].reshape(slots_dev, 3, 128) + slot_shift(slot)[None, :, None]
        mass_near = near[:, 384:512]
        vel_near = moving[:, 0:384].reshape(slots_dev, 3, 128)
        smooth_near = moving[:, 384:512]
        energy_near = moving[:, 512:640]
        gap = pos_own[:, :, :, None] - pos_near[:, :, None, :]
        dist_sq = jnp.sum(gap * gap, axis=1)
        slope_own = kernel_slope(dist_sq, smooth_own[:, :, None])
        slope_near = kernel_slope(dist_sq, smooth_near[:, None, :])
        press_near = gas_factor * rho_part * energy_near / (rho_part * rho_part)
        coeff = mass_near[:, None, :] * (
            press_own[:, :, None] * slope_own + press_near[:, None, :] * slope_near
        )
        accel_part = jnp.sum(coeff[:, None, :, :] * gap, axis=3)
        vel_gap = vel_own[:, :, :, None] - vel_near[:, :, None, :]
        inner = jnp.sum(vel_gap * gap, axis=1)
        rate_part = jnp.sum(mass_near[:, None, :] * slope_own * inner, axis=2)
        return ((accel_sum + accel_part, rate_sum + rate_part), None)

    start = (jnp.zeros((slots_dev, 3, 128), jnp.float32), jnp.zeros((slots_dev, 128), jnp.float32))
    (accel_sum, rate_sum), _ = lax.scan(
        force_step, start, (slot_ids, near_static, near_moving[:, :, 0:640], rho_near)
    )
    stacked = jnp.concatenate(
        [fresh[:, None, :], -accel_sum, (press_own * rate_sum)[:, None, :]], axis=1
    )
    return stacked * valid_own[:, None, :]


def solution(mesh):
    placed = (
        P("dom", None, None),
        P("dom", None, None),
        P("dom", None),
        P("dom", None),
        P("dom", None),
        P("dom", None),
        P("dom"),
        P("dom"),
        P("dom", None),
    )
    return jax.shard_map(
        shards, mesh=mesh, in_specs=placed, out_specs=P("dom", None, None), check_vma=False
    )
```

profile of v0, /device:TPU:1, one launch (start us, length us, event | category | flops | bytes accessed | tf_op | source)
XLA Modules:
  0.0 676.4 jit_solution(5791912850241298322)
XLA Ops:
  0.0 2.1 copy.58
  4.8 4.5 collective-permute-start.2
  11.3 2.8 collective-permute-start.6
  17.5 4.9 collective-permute-start.4
  23.6 3.3 collective-permute-start.12
  27.0 2.4 copy.33
  29.5 2.1 copy.34
  37.0 1.7 gather_fusion.16
  38.8 2.4 pad_maximum_fusion.1
  41.2 2.8 collective-permute-start.8
  45.9 2.0 collective-permute-done.8
  47.9 4.0 collective-permute-start.13
  53.0 1.7 collective-permute-start.5
  56.9 4.0 collective-permute-start.3
  64.0 2.1 collective-permute-start.11
  66.1 2.3 gather_fusion.17
  70.0 1.7 gather_fusion
  71.7 1.7 gather_fusion.18
  73.4 1.7 gather_fusion.19
  75.1 2.5 copy.36
  77.6 2.1 copy.37
  79.8 3.0 concatenate.32
  82.8 2.3 gather_fusion.15
  85.1 201.6 %while.33 = (s32[]{:T(128)}, f32[16,128]{1,0:T(8,128)S(1)}, f32[27,16,512]{2,1,0:T(8,128)}, f32[16,128,1]{1,0,2:T(8,128)S(1)}, f32[16,384]{1,0:T(8,128)S(1)}, /*...) while((s32[]{:T(128)}, f32[16,128]{1,0:T(8,128)S(1)}, ...), condition=%wide.region_3.4_spmd.clone, body=%wide.region_0.3_spmd.clone.sunk | while | flops 6563879 | bytes 2499033 | solution.py:104
  287.7 3.9 pad_maximum_fusion
  291.6 3.2 gather_fusion.22
  294.9 3.2 gather_fusion.24
  298.1 6.2 collective-permute-start.15
  304.8 3.1 gather_fusion.26
  310.3 6.1 collective-permute-start.20
  316.4 3.0 gather_fusion.23
  319.4 3.0 gather_fusion.21
  323.4 2.8 collective-permute-start.14
  326.2 3.0 gather_fusion.25
  331.0 3.6 gather_fusion.20
  335.4 1.9 gather_fusion.27
  338.1 337.7 %while.34 = (s32[]{:T(128)}, f32[16,3,128]{2,1,0:T(4,128)S(1)}, f32[16,128]{1,0:T(8,128)S(1)}, f32[27,16,512]{2,1,0:T(8,128)}, f32[16,128]{1,0:T(8,128)S(1)}, /*...) while((s32[]{:T(128)}, f32[16,3,128]{2,1,0:T(4,128)S(1)}, ...), condition=%wide.region_10.11_spmd.clone, body=%wide.region_5.10_spmd.clone.sunk | while | flops 17858600 | bytes 8225290 | solution.py:142
  346.4 2.9 fusion.23
  358.9 2.9 fusion.23
  371.4 2.9 fusion.23
  383.9 2.9 fusion.23
  396.4 2.9 fusion.23
  408.9 2.9 fusion.23
  421.4 2.9 fusion.23
  433.9 2.9 fusion.23
  446.4 2.9 fusion.23
  458.9 2.9 fusion.23
  471.5 2.9 fusion.23
  484.0 2.9 fusion.23
  496.5 2.9 fusion.23
  509.0 2.9 fusion.23
  521.5 2.9 fusion.23
  534.0 2.9 fusion.23
  546.5 2.9 fusion.23
  559.0 2.9 fusion.23
  571.5 2.9 fusion.23
  584.0 2.9 fusion.23
  596.5 2.9 fusion.23
  609.0 2.9 fusion.23
  621.5 2.9 fusion.23
  634.0 2.9 fusion.23
  646.6 2.9 fusion.23
  659.1 2.9 fusion.23
  671.6 2.9 fusion.23
  (930 shorter events, 299.7 us)
Async XLA Ops:
  0.0 16.9 %copy-start.11 = (s32[2]{0:T(128)S(1)}, s32[2]{0:T(128)}, u32[]{:S(2)}) copy-start(s32[2]{0:T(128)} %constant.438) | copy-start | bytes 28
  4.8 50.6 %collective-permute-start.2 = (s32[94]{0:T(128)S(1)}, s32[94]{0:T(128)S(1)}, u32[]{:S(2)}, u32[]{:S(2)}) collective-permute-start(s32[94]{0:T(128)S(1)} %broadcast_subtract_fusion.5), channel_id=1, source_target_pairs={{0,4},{1,5},{2,6},{3,7},{4,8},{5,9},{6,10},{7,11},{8,12},{9,13},{1... | collective-permute-start | bytes 1136 | tf_op jit(solution)/shard_map/ppermute | solution.py:15
  11.3 44.2 %collective-permute-start.6 = (s32[94]{0:T(128)S(1)}, s32[94]{0:T(128)S(1)}, u32[]{:S(2)}, u32[]{:S(2)}) collective-permute-start(s32[94]{0:T(128)S(1)} %broadcast_subtract_fusion.3), channel_id=1, source_target_pairs={{0,16},{1,17},{2,18},{3,19},{4,20},{5,21},{6,22},{7,23},{8,24},{9,... | collective-permute-start | bytes 1136 | tf_op jit(solution)/shard_map/ppermute | solution.py:15
  15.6 39.8 %collective-permute-start.10 = (s32[47]{0:T(128)S(1)}, s32[47]{0:T(128)S(1)}, u32[]{:S(2)}, u32[]{:S(2)}) collective-permute-start(s32[47]{0:T(128)S(1)} %broadcast_subtract_fusion.1), channel_id=1, source_target_pairs={{0,20},{1,21},{2,22},{3,23},{4,24},{5,25},{6,26},{7,27},{8,28},{9,... | collective-permute-start | bytes 572 | tf_op jit(solution)/shard_map/ppermute | solution.py:15
  17.5 28.3 %collective-permute-start.4 = (s32[2]{0:T(128)S(1)}, s32[2]{0:T(128)S(1)}, u32[]{:S(2)}, u32[]{:S(2)}) collective-permute-start(s32[2]{0:T(128)S(1)} %broadcast_subtract_fusion.4), channel_id=1, source_target_pairs={{0,5},{1,6},{2,7},{3,8},{4,9},{5,10},{6,11},{7,12},{8,13},{9,14},{... | collective-permute-start | bytes 32 | tf_op jit(solution)/shard_map/ppermute | solution.py:15
  23.6 17.6 %collective-permute-start.12 = (s32[1]{0:T(128)}, s32[1]{0:T(128)}, u32[]{:S(2)}, u32[]{:S(2)}) collective-permute-start(s32[1]{0:T(128)} %sub.247), channel_id=1, source_target_pairs={{0,21},{1,22},{2,23},{3,24},{4,25},{5,26},{6,27},{7,28},{8,29},{9,... | collective-permute-start | bytes 20 | tf_op jit(solution)/shard_map/ppermute | solution.py:15
  29.4 2.2 copy-start.6
  29.4 3.4 copy-start.5
  29.4 4.6 copy-start.10
  29.4 5.2 copy-start.9
  29.5 5.9 copy-start.8
  31.6 5.4 copy-start.12
  38.7 7.0 %copy-start = (f32[1600,384]{1,0:T(8,128)S(1)}, f32[1600,384]{1,0:T(8,128)}, u32[]{:S(2)}) copy-start(f32[1600,384]{1,0:T(8,128)} %copy.34) | copy-start | bytes 7372804
  38.8 7.0 %copy-start.2 = (f32[1600,128]{1,0:T(8,128)S(1)}, f32[1600,128]{1,0:T(8,128)}, u32[]{:S(2)}) copy-start(f32[1600,128]{1,0:T(8,128)} %fusion.12) | copy-start | bytes 2457604
  41.2 6.6 collective-permute-start.8
  45.8 20.3 %copy-start.7 = (s32[432]{0:T(512)S(1)}, s32[432]{0:T(512)}, u32[]{:S(2)}) copy-start(s32[432]{0:T(512)} %constant.442) | copy-start | bytes 5188
  45.8 7.2 %collective-permute-start = (s32[4]{0:T(128)S(1)}, s32[4]{0:T(128)S(1)}, u32[]{:S(2)}, u32[]{:S(2)}) collective-permute-start(s32[4]{0:T(128)S(1)} %broadcast_subtract_fusion.6), channel_id=1, source_target_pairs={{0,1},{1,2},{2,3},{3,4},{4,5},{5,6},{6,7},{7,8},{8,9},{9,10},{10,1... | collective-permute-start | bytes 56 | tf_op jit(solution)/shard_map/ppermute | solution.py:15
  47.9 15.0 %collective-permute-start.13 = (f32[1,512]{1,0:T(1,128)S(1)}, f32[1,512]{1,0:T(1,128)S(1)}, u32[]{:S(2)}, u32[]{:S(2)}) collective-permute-start(f32[1,512]{1,0:T(1,128)S(1)} %fusion.15), channel_id=1, source_target_pairs={{0,107},{1,108},{2,109},{3,110},{4,111},{5,112},{6,113},{7,114},{8... | collective-permute-start | bytes 6152 | tf_op jit(solution)/shard_map/ppermute | solution.py:15
  53.0 11.0 %collective-permute-start.5 = (f32[2,512]{1,0:T(2,128)S(1)}, f32[2,512]{1,0:T(2,128)S(1)}, u32[]{:S(2)}, u32[]{:S(2)}) collective-permute-start(f32[2,512]{1,0:T(2,128)S(1)} %gather_fusion.8), channel_id=1, source_target_pairs={{0,123},{1,124},{2,125},{3,126},{4,127},{5,0},{6,1},{7,2},{8,3},{9... | collective-permute-start | bytes 12296 | tf_op jit(solution)/shard_map/ppermute | solution.py:15
  55.4 24.4 %collective-permute-start.9 = (f32[2,512]{1,0:T(2,128)S(1)}, f32[2,512]{1,0:T(2,128)S(1)}, u32[]{:S(2)}, u32[]{:S(2)}) collective-permute-start(f32[2,512]{1,0:T(2,128)S(1)} %gather_fusion.12), channel_id=1, source_target_pairs={{0,111},{1,112},{2,113},{3,114},{4,115},{5,116},{6,117},{7,118},{8... | collective-permute-start | bytes 12296 | tf_op jit(solution)/shard_map/ppermute | solution.py:15
  56.9 22.9 %collective-permute-start.3 = (f32[94,512]{1,0:T(8,128)}, f32[94,512]{1,0:T(8,128)}, u32[]{:S(2)}, u32[]{:S(2)}) collective-permute-start(f32[94,512]{1,0:T(8,128)} %gather_fusion.6), channel_id=1, source_target_pairs={{0,124},{1,125},{2,126},{3,127},{4,0},{5,1},{6,2},{7,3},{8,4},{9,5... | collective-permute-start | bytes 577544 | tf_op jit(solution)/shard_map/ppermute | solution.py:15
  62.3 17.5 %collective-permute-start.7 = (f32[94,512]{1,0:T(8,128)}, f32[94,512]{1,0:T(8,128)}, u32[]{:S(2)}, u32[]{:S(2)}) collective-permute-start(f32[94,512]{1,0:T(8,128)} %gather_fusion.10), channel_id=1, source_target_pairs={{0,112},{1,113},{2,114},{3,115},{4,116},{5,117},{6,118},{7,119},{8... | collective-permute-start | bytes 577544 | tf_op jit(solution)/shard_map/ppermute | solution.py:15
  62.9 16.9 %collective-permute-start.1 = (f32[4,512]{1,0:T(4,128)S(1)}, f32[4,512]{1,0:T(4,128)S(1)}, u32[]{:S(2)}, u32[]{:S(2)}) collective-permute-start(f32[4,512]{1,0:T(4,128)S(1)} %gather_fusion.4), channel_id=1, source_target_pairs={{0,127},{1,0},{2,1},{3,2},{4,3},{5,4},{6,5},{7,6},{8,7},{9,8},{10,... | collective-permute-start | bytes 24584 | tf_op jit(solution)/shard_map/ppermute | solution.py:15
  64.0 15.8 %collective-permute-start.11 = (f32[47,512]{1,0:T(8,128)S(1)}, f32[47,512]{1,0:T(8,128)}, u32[]{:S(2)}, u32[]{:S(2)}) collective-permute-start(f32[47,512]{1,0:T(8,128)S(1)} %gather_fusion.14), channel_id=1, source_target_pairs={{0,108},{1,109},{2,110},{3,111},{4,112},{5,113},{6,114},{7,115},{8... | collective-permute-start | bytes 288776 | tf_op jit(solution)/shard_map/ppermute | solution.py:15
  77.6 2.2 copy-start.4
  82.8 203.9 %copy-start.3 = (f32[1600,128]{1,0:T(8,128)S(1)}, f32[1600,128]{1,0:T(8,128)}, u32[]{:S(2)}) copy-start(f32[1600,128]{1,0:T(8,128)} %copy.58) | copy-start | bytes 2457604
  85.1 202.6 %copy-start.1 = (f32[1600,384]{1,0:T(8,128)S(1)}, f32[1600,384]{1,0:T(8,128)}, u32[]{:S(2)}) copy-start(f32[1600,384]{1,0:T(8,128)} %copy.37) | copy-start | bytes 7372804
  298.1 36.9 %collective-permute-start.15 = (f32[94,768]{1,0:T(8,128)S(1)}, f32[94,768]{1,0:T(8,128)S(1)}, u32[]{:S(2)}, u32[]{:S(2)}) collective-permute-start(f32[94,768]{1,0:T(8,128)S(1)} %gather_fusion.22), channel_id=1, source_target_pairs={{0,124},{1,125},{2,126},{3,127},{4,0},{5,1},{6,2},{7,3},{8,4},{9,5... | collective-permute-start | bytes 866312 | tf_op jit(solution)/shard_map/ppermute | solution.py:15
  304.3 30.7 %collective-permute-start.17 = (f32[94,768]{1,0:T(8,128)S(1)}, f32[94,768]{1,0:T(8,128)S(1)}, u32[]{:S(2)}, u32[]{:S(2)}) collective-permute-start(f32[94,768]{1,0:T(8,128)S(1)} %gather_fusion.24), channel_id=1, source_target_pairs={{0,112},{1,113},{2,114},{3,115},{4,116},{5,117},{6,118},{7,119},{8... | collective-permute-start | bytes 866312 | tf_op jit(solution)/shard_map/ppermute | solution.py:15
  307.9 27.0 %collective-permute-start.19 = (f32[47,768]{1,0:T(8,128)S(1)}, f32[47,768]{1,0:T(8,128)S(1)}, u32[]{:S(2)}, u32[]{:S(2)}) collective-permute-start(f32[47,768]{1,0:T(8,128)S(1)} %gather_fusion.26), channel_id=1, source_target_pairs={{0,108},{1,109},{2,110},{3,111},{4,112},{5,113},{6,114},{7,115},{8... | collective-permute-start | bytes 433160 | tf_op jit(solution)/shard_map/ppermute | solution.py:15
  310.3 13.1 %collective-permute-start.20 = (f32[1,768]{1,0:T(1,128)S(1)}, f32[1,768]{1,0:T(1,128)S(1)}, u32[]{:S(2)}, u32[]{:S(2)}) collective-permute-start(f32[1,768]{1,0:T(1,128)S(1)} %constant_dynamic-slice_fusion), channel_id=1, source_target_pairs={{0,107},{1,108},{2,109},{3,110},{4,111},{5,112},{6,113},{7,114},{8... | collective-permute-start | bytes 9224 | tf_op jit(solution)/shard_map/ppermute | solution.py:15
  322.4 6.8 %collective-permute-start.16 = (f32[2,768]{1,0:T(2,128)S(1)}, f32[2,768]{1,0:T(2,128)S(1)}, u32[]{:S(2)}, u32[]{:S(2)}) collective-permute-start(f32[2,768]{1,0:T(2,128)S(1)} %gather_fusion.23), channel_id=1, source_target_pairs={{0,123},{1,124},{2,125},{3,126},{4,127},{5,0},{6,1},{7,2},{8,3},{9... | collective-permute-start | bytes 18440 | tf_op jit(solution)/shard_map/ppermute | solution.py:15
  323.4 11.5 %collective-permute-start.14 = (f32[4,768]{1,0:T(4,128)S(1)}, f32[4,768]{1,0:T(4,128)S(1)}, u32[]{:S(2)}, u32[]{:S(2)}) collective-permute-start(f32[4,768]{1,0:T(4,128)S(1)} %gather_fusion.21), channel_id=1, source_target_pairs={{0,127},{1,0},{2,1},{3,2},{4,3},{5,4},{6,5},{7,6},{8,7},{9,8},{10,... | collective-permute-start | bytes 36872 | tf_op jit(solution)/shard_map/ppermute | solution.py:15
  329.2 5.7 collective-permute-start.18
where the time goes:
time: 685 us; the launch traced here: 676 us
  other arithmetic  280 us (41%)
  loops' own time  191 us (28%)
  local copies, waits for them, and re-layouts  149 us (22%)
  starting transfers between devices  51.3 us (7%)
    another operation x1, loops' own time, shards(): lax.scan(density_step, jnp.zeros((slots_dev, 128), jnp.float32), (slot_id...  96.1 us
    another operation x1, loops' own time, shards(): lax.scan(force_step, start, (slot_ids, near_static, near_moving[:, :, 0:6...  95.1 us
    reduce_sum x27, other arithmetic, force_step(): inner = jnp.sum(vel_gap * gap, axis=1)  79.4 us
    ppermute x21, starting transfers between devices, from_behind(): return lax.ppermute(value, axis, pairs)  51.3 us
    squeeze x54, local copies, waits for them, and re-layouts, shards(): lax.scan(density_step, jnp.zeros((slots_dev, 128), jnp.float32), (slot_id...  41.2 us
    mul x27, other arithmetic, force_step(): mass_near[:, None, :]  38.2 us
    dynamic_slice x54, local copies, waits for them, and re-layouts, shards(): lax.scan(density_step, jnp.zeros((slots_dev, 128), jnp.float32), (slot_id...  35.6 us
    reduce_sum x27, other arithmetic, density_step(): return (total + jnp.sum(near[:, None, 384:512] * weight, axis=2), None)  33.4 us
  transfers between devices with their start and end apart: 21, of which 2 were waited for; matrix products, arithmetic and copies ran while one was open for 8% of the time, Pallas kernels for 0%

commit v1 on v0

v1 whole, which is shorter than its diff:
```python
import math

import jax
import jax.numpy as jnp
import numpy as np
from jax import lax
from jax.experimental import pallas as pl
from jax.experimental.pallas import tpu as pltpu
from jax.sharding import PartitionSpec as P

MESH = pl.DeviceIdType.MESH
NORM = 8.0 / math.pi
GAS = 2.0 / 3.0
TINY = 1e-14
LIMIT = 56 * 1024 * 1024

STEPS = (16, 4, 20, 1, 5, 17, 21)
WIDE = ((2, 8), (0, 6), (0, 7), (1, 2), (1, 5))
EDGE = ((6, 8), (5, 6), (5, 7), (4, 2), (4, 5), (3, 0), (3, 1), (3, 3), (3, 4))
HOME = (0, 1, 3, 4)
SPAN = 47


def shift_tiles():
    tiles = np.zeros((27, 8, 128), np.float32)
    for slot in range(27):
        tiles[slot, 1] = slot // 9 - 1.5
        tiles[slot, 2] = slot // 3 % 3 - 1.5
        tiles[slot, 3] = slot % 3 - 1.5
    return tiles


def greet(me, devices):
    barrier = pltpu.get_barrier_semaphore()
    for steps in STEPS:
        for other in (me + steps, me + devices - steps):
            pl.semaphore_signal(barrier, inc=1, device_id=(lax.rem(other, devices),), device_id_type=MESH)
    pl.semaphore_wait(barrier, 2 * len(STEPS))


def gather_kernel(
    devices, req_ref, req_send, counts_ref, pos_ref, vel_ref, mass_ref, smooth_ref,
    near_ref, asked_ref, send_ref, edge_ref, lists_ref, ask_out, ask_in, send_sem, recv_sem, local_sem,
):
    me = lax.axis_index("dom")
    cells = mass_ref.shape[0]
    first = me * cells
    lane = lax.broadcasted_iota(jnp.int32, (1, 128), 1)

    def fill(dst, place, cell):
        cell = jnp.clip(cell - first, 0, cells - 1)
        keep = lane < counts_ref[cell]
        dst[place, 0:1, :] = jnp.where(keep, mass_ref[pl.ds(cell, 1), :], 0.0)
        for axis in range(3):
            dst[place, 1 + axis : 2 + axis, :] = pos_ref[axis, pl.ds(cell, 1), :]
            dst[place, 4 + axis : 5 + axis, :] = vel_ref[axis, pl.ds(cell, 1), :]
        dst[place, 7:8, :] = smooth_ref[pl.ds(cell, 1), :]

    greet(me, devices)
    asks = []
    for place, steps in enumerate(STEPS):
        ask = pltpu.make_async_remote_copy(
            req_send, asked_ref.at[place], ask_out.at[place], ask_in.at[place],
            device_id=(lax.rem(me + steps, devices),), device_id_type=MESH,
        )
        ask.start()
        asks.append(ask)

    def home_step(entry, carry):
        for block in HOME:
            fill(near_ref, block * 48 + entry, req_ref[block, entry])
        return carry

    lax.fori_loop(0, SPAN, home_step, 0)
    for ask in asks:
        ask.wait()
    listed = pltpu.make_async_copy(asked_ref, lists_ref, local_sem)
    listed.start()
    listed.wait()
    copies = []

    def requester(place):
        return (lax.rem(me + devices - STEPS[place], devices),)

    def serve(group, start):
        def step(entry, carry):
            for place, block in group:
                fill(send_ref, block * 48 + entry, lists_ref[place, block, entry])
            return carry

        lax.fori_loop(0, SPAN, step, 0)
        for number, (place, block) in enumerate(group):
            rows = pl.ds(block * 48, SPAN)
            copy = pltpu.make_async_remote_copy(
                send_ref.at[rows], near_ref.at[rows], send_sem.at[start + number], recv_sem.at[start + number],
                device_id=requester(place), device_id_type=MESH,
            )
            copy.start()
            copies.append(copy)

    serve(WIDE[:3], 0)
    serve(WIDE[3:], 3)
    for number, (place, block) in enumerate(EDGE):
        fill(edge_ref, number, lists_ref[place, block, SPAN])
        copy = pltpu.make_async_remote_copy(
            edge_ref.at[number], near_ref.at[block * 48 + SPAN], send_sem.at[5 + number], recv_sem.at[5 + number],
            device_id=requester(place), device_id_type=MESH,
        )
        copy.start()
        copies.append(copy)
    for copy in copies:
        copy.wait()


def pieces(value):
    one = value.astype(jnp.bfloat16).astype(jnp.float32)
    rest = value - one
    two = rest.astype(jnp.bfloat16).astype(jnp.float32)
    return one, two, rest - two


def row_ids():
    return lax.broadcasted_iota(jnp.int32, (8, 128), 0)


def own_side(tile):
    rows = row_ids()
    near = tile - 0.5
    square = near * near
    norm = square[1:2] + square[2:3] + square[3:4]
    left = jnp.where(rows == 0, norm, jnp.where(rows < 4, -2.0 * near, jnp.where(rows == 4, 1.0, 0.0)))
    one, two, three = pieces(left)
    return jnp.concatenate([one, one, one, two, two, three], axis=0).T.astype(jnp.bfloat16)


def near_side(moved):
    rows = row_ids()
    square = moved * moved
    norm = square[1:2] + square[2:3] + square[3:4]
    right = jnp.where(rows == 0, 1.0, jnp.where(rows == 4, norm, moved))
    one, two, three = pieces(right)
    return jnp.concatenate([one, two, three, one, two, one], axis=0).astype(jnp.bfloat16)


def column(row):
    return jnp.broadcast_to(row, (128, 128)).T


def density_kernel(
    req_ref, lists_ref, counts_ref, active_ref, near_ref, shift_ref, energy_ref, old_ref,
    fresh_ref, mine_ref, edge_ref, table_ref, inv_ref,
):
    cells = old_ref.shape[0]
    first = lax.axis_index("dom") * cells
    lane = lax.broadcasted_iota(jnp.int32, (1, 128), 1)
    table_ref[...] = GAS * energy_ref[...] / old_ref[...]

    def row_step(row, carry):
        own = near_ref[13 * 16 + row]
        left = own_side(own)
        inverse = 1.0 / own[7:8]
        inv_ref[...] = column(inverse)

        def slot_step(slot, sums):
            tile = near_ref[slot * 16 + row]
            dist = jnp.dot(left, near_side(tile + shift_ref[slot]), preferred_element_type=jnp.float32)
            mass = tile[0:1]
            totals = []
            for part in range(8):
                square = jnp.maximum(dist[part * 16 : part * 16 + 16], TINY)
                ratio = square * lax.rsqrt(square) * inv_ref[part * 16 : part * 16 + 16, :]
                outer = 1.0 - jnp.minimum(ratio, 1.0)
                inner = 1.0 - jnp.minimum(ratio + ratio, 1.0)
                weight = (outer + outer) * (outer * outer) - inner * (inner * inner)
                totals.append(sums[part] + weight * mass)
            return tuple(totals)

        zero = jnp.zeros((16, 128), jnp.float32)
        sums = lax.fori_loop(0, 27, slot_step, (zero,) * 8, unroll=3)
        total = jnp.sum(jnp.concatenate(sums, axis=0).T, axis=0, keepdims=True)
        cell = active_ref[row] - first
        fresh = jnp.where(
            lane < counts_ref[cell], total * (NORM * inverse * inverse * inverse), old_ref[pl.ds(cell, 1), :]
        )
        fresh_ref[row] = fresh
        table_ref[pl.ds(cell, 1), :] = GAS * energy_ref[pl.ds(cell, 1), :] / fresh
        return carry

    lax.fori_loop(0, 16, row_step, 0)

    def collect(entry, carry):
        for block in HOME:
            mine_ref[block * 48 + entry] = table_ref[pl.ds(req_ref[block, entry] - first, 1), :]
        for place, block in WIDE:
            mine_ref[block * 48 + entry] = table_ref[pl.ds(lists_ref[place, block, entry] - first, 1), :]
        return carry

    lax.fori_loop(0, SPAN, collect, 0)
    for number, (place, block) in enumerate(EDGE):
        mine_ref[block * 48 + SPAN] = jnp.zeros((1, 128), jnp.float32)
        edge_ref[number] = table_ref[pl.ds(lists_ref[place, block, SPAN] - first, 1), :]


def pass_kernel(devices, mine_ref, edge_ref, near_ref, send_sem, recv_sem, local_sem):
    me = lax.axis_index("dom")
    greet(me, devices)
    copies = []

    def requester(place):
        return (lax.rem(me + devices - STEPS[place], devices),)

    for number, (place, block) in enumerate(WIDE):
        rows = pl.ds(block * 48, SPAN)
        copies.append(
            pltpu.make_async_remote_copy(
                mine_ref.at[rows], near_ref.at[rows], send_sem.at[number], recv_sem.at[number],
                device_id=requester(place), device_id_type=MESH,
            )
        )
    for number, (place, block) in enumerate(EDGE):
        copies.append(
            pltpu.make_async_remote_copy(
                edge_ref.at[number], near_ref.at[block * 48 + SPAN], send_sem.at[5 + number], recv_sem.at[5 + number],
                device_id=requester(place), device_id_type=MESH,
            )
        )
    for number, block in enumerate(HOME):
        rows = pl.ds(block * 48, SPAN)
        copies.append(pltpu.make_async_copy(mine_ref.at[rows], near_ref.at[rows], local_sem.at[number]))
    for copy in copies:
        copy.start()
    for copy in copies:
        copy.wait()


def slope(ratio):
    low = jnp.minimum(ratio, 1.0)
    high = jnp.minimum(ratio + ratio, 1.0)
    return (high - low) * (2.0 - (low + high))


def split(value):
    high = value.astype(jnp.bfloat16)
    return high, (value - high.astype(jnp.float32)).astype(jnp.bfloat16)


def split_rows(value):
    high = value.astype(jnp.bfloat16).astype(jnp.float32)
    both = jnp.concatenate([high, value - high], axis=0).astype(jnp.bfloat16)
    return jnp.concatenate([both, both], axis=1)


def pair_sum(rows, pairs):
    return lax.dot_general(rows, pairs, (((1,), (1,)), ((), ())), preferred_element_type=jnp.float32)


def force_kernel(
    counts_ref, active_ref, near_ref, press_ref, shift_ref, fresh_ref, hydro_ref, inv_ref,
):
    cells = counts_ref.shape[0]
    first = lax.axis_index("dom") * cells
    lane = lax.broadcasted_iota(jnp.int32, (1, 128), 1)
    rows = row_ids()

    def row_step(row, carry):
        own = near_ref[13 * 16 + row]
        left = own_side(own)
        inverse = 1.0 / own[7:8]
        inv_ref[...] = column(inverse)

        def slot_step(slot, sums):
            tile = near_ref[slot * 16 + row]
            moved = tile + shift_ref[slot]
            dist = jnp.dot(left, near_side(moved), preferred_element_type=jnp.float32)
            near_inv = 1.0 / tile[7:8]
            near_sq = near_inv * near_inv
            near_rows = jnp.broadcast_to(near_inv, (16, 128))
            work = moved[1:2] * tile[4:5] + moved[2:3] * tile[5:6] + moved[3:4] * tile[6:7]
            terms = tile[0:1] * jnp.where(rows == 0, 1.0, jnp.where(rows == 7, work, moved))
            press = terms * (press_ref[slot * 16 + row] * (near_sq * near_sq))
            own_pairs, own_rest, near_pairs, near_rest = [], [], [], []
            for part in range(8):
                square = jnp.maximum(dist[part * 16 : part * 16 + 16], TINY)
                root = lax.rsqrt(square)
                gap = square * root
                high, low = split(slope(gap * inv_ref[part * 16 : part * 16 + 16, :]) * root)
                own_pairs.append(high)
                own_rest.append(low)
                high, low = split(slope(gap * near_rows) * root)
                near_pairs.append(high)
                near_rest.append(low)
            def joined(high, low):
                return jnp.concatenate([jnp.concatenate(high, axis=0), jnp.concatenate(low, axis=0)], axis=1)

            return (
                sums[0] + pair_sum(split_rows(terms), joined(own_pairs, own_rest)),
                sums[1] + pair_sum(split_rows(press), joined(near_pairs, near_rest)),
            )

        zero = jnp.zeros((16, 128), jnp.float32)
        sums = lax.fori_loop(0, 27, slot_step, (zero, zero), unroll=3)
        by_own = sums[0][0:8] + sums[0][8:16]
        by_near = sums[1][0:8] + sums[1][8:16]
        place = own - 0.5
        inv_sq = inverse * inverse
        factor = (-6.0 * NORM) * (inv_sq * inv_sq) * press_ref[13 * 16 + row]
        accel = []
        rate = by_own[7:8]
        for axis in range(3):
            at = place[1 + axis : 2 + axis]
            speed = own[4 + axis : 5 + axis]
            pull = at * by_own[0:1] - by_own[1 + axis : 2 + axis]
            push = at * by_near[0:1] - by_near[1 + axis : 2 + axis]
            accel.append(-(factor * pull + (-6.0 * NORM) * push))
            rate = rate + speed * pull - at * by_own[4 + axis : 5 + axis]
        cell = active_ref[row] - first
        keep = lane < counts_ref[cell]
        values = jnp.concatenate([fresh_ref[row]] + accel + [factor * rate], axis=0)
        hydro_ref[row] = jnp.where(keep, values, 0.0)
        return carry

    lax.fori_loop(0, 16, row_step, 0)


def shards(positions, velocity, mass, smoothing, energy, density_old, counts, active, neighbours):
    devices = lax.axis_size("dom")
    vmem = pl.BlockSpec(memory_space=pltpu.VMEM)
    smem = pl.BlockSpec(memory_space=pltpu.SMEM)
    pos = jnp.transpose(positions, (1, 0, 2))
    vel = jnp.transpose(velocity, (1, 0, 2))
    requests = jnp.pad(neighbours.T.reshape(9, 48), ((0, 7), (0, 80)))
    shifts = jnp.asarray(shift_tiles())
    f32 = jnp.float32

    near, asked = pl.pallas_call(
        lambda *refs: gather_kernel(devices, *refs),
        out_shape=(jax.ShapeDtypeStruct((432, 8, 128), f32), jax.ShapeDtypeStruct((7, 16, 128), jnp.int32)),
        in_specs=[smem, vmem, smem, vmem, vmem, vmem, vmem],
        out_specs=(vmem, vmem),
        scratch_shapes=[
            pltpu.VMEM((432, 8, 128), f32),
            pltpu.VMEM((9, 8, 128), f32),
            pltpu.SMEM((7, 16, 128), jnp.int32),
            pltpu.SemaphoreType.DMA((7,)),
            pltpu.SemaphoreType.DMA((7,)),
            pltpu.SemaphoreType.DMA((14,)),
            pltpu.SemaphoreType.DMA((14,)),
            pltpu.SemaphoreType.DMA,
        ],
        compiler_params=pltpu.CompilerParams(collective_id=0, has_side_effects=True, vmem_limit_bytes=LIMIT),
    )(requests, requests, counts, pos, vel, mass, smoothing)

    fresh, mine, edge = pl.pallas_call(
        density_kernel,
        out_shape=(
            jax.ShapeDtypeStruct((16, 1, 128), f32),
            jax.ShapeDtypeStruct((432, 1, 128), f32),
            jax.ShapeDtypeStruct((9, 1, 128), f32),
        ),
        in_specs=[smem, smem, smem, smem, vmem, vmem, vmem, vmem],
        out_specs=(vmem, vmem, vmem),
        scratch_shapes=[pltpu.VMEM((1600, 128), f32), pltpu.VMEM((128, 128), f32)],
        compiler_params=pltpu.CompilerParams(vmem_limit_bytes=LIMIT),
    )(requests, asked, counts, active, near, shifts, energy, density_old)

    press = pl.pallas_call(
        lambda *refs: pass_kernel(devices, *refs),
        out_shape=jax.ShapeDtypeStruct((432, 1, 128), f32),
        in_specs=[vmem, vmem],
        out_specs=vmem,
        scratch_shapes=[
            pltpu.SemaphoreType.DMA((14,)),
            pltpu.SemaphoreType.DMA((14,)),
            pltpu.SemaphoreType.DMA((4,)),
        ],
        compiler_params=pltpu.CompilerParams(collective_id=1, has_side_effects=True, vmem_limit_bytes=LIMIT),
    )(mine, edge)

    return pl.pallas_call(
        force_kernel,
        out_shape=jax.ShapeDtypeStruct((16, 5, 128), f32),
        in_specs=[smem, smem, vmem, vmem, vmem, vmem],
        out_specs=vmem,
        scratch_shapes=[pltpu.VMEM((128, 128), f32)],
        compiler_params=pltpu.CompilerParams(vmem_limit_bytes=LIMIT),
    )(counts, active, near, press, shifts, fresh)


def solution(mesh):
    placed = (
        P("dom", None, None),
        P("dom", None, None),
        P("dom", None),
        P("dom", None),
        P("dom", None),
        P("dom", None),
        P("dom"),
        P("dom"),
        P("dom", None),
    )
    return jax.shard_map(
        shards, mesh=mesh, in_specs=placed, out_specs=P("dom", None, None), check_vma=False
    )
```

time: 685 us -> 215 us (0.31); the launches traced: 676 us -> 214 us
  other arithmetic: 280 us -> 0 us
  Pallas kernels: 0 us -> 211 us
  loops' own time: 191 us -> 0 us
  local copies, waits for them, and re-layouts: 149 us -> 2.93 us
  starting transfers between devices: 51.3 us -> 0 us
    pallas_call x0 -> x4, Pallas kernels: none -> 211 us  [the longest x1 110 us: shards(): pl.pallas_call(force_kernel, out_shape=jax.ShapeDtypeStruct((16, 5, 128),...]
    reduce_sum x135 -> x0, other arithmetic: 201 us -> none  [the longest x27 79.4 us: force_step(): inner = jnp.sum(vel_gap * gap, axis=1)]
    another operation x2 -> x0, loops' own time: 191 us -> none  [the longest x1 96.1 us: shards(): lax.scan(density_step, jnp.zeros((slots_dev, 128), jnp.float32), (slot_id...]
    gather x31 -> x0, local copies, waits for them, and re-layouts: 51.6 us -> none  [the longest x7 19.2 us: shards(): dynamic_table[served[place]]]
    ppermute x21 -> x0, starting transfers between devices: 51.3 us -> none  [from_behind(): return lax.ppermute(value, axis, pairs)]
    squeeze x81 -> x0, local copies, waits for them, and re-layouts: 41.5 us -> none  [the longest x54 41.2 us: shards(): lax.scan(density_step, jnp.zeros((slots_dev, 128), jnp.float32), (slot_id...]
    mul x30 -> x0, other arithmetic: 40 us -> none  [the longest x27 38.2 us: force_step(): mass_near[:, None, :]]
    dynamic_slice x54 -> x0, local copies, waits for them, and re-layouts: 35.6 us -> none  [shards(): lax.scan(density_step, jnp.zeros((slots_dev, 128), jnp.float32), (slot_id...]
  transfers between devices with their start and end apart: 21 -> 0, of which waited for: 2 -> 0; matrix products, arithmetic and copies ran while one was open for 8% -> 0% of each run, Pallas kernels for 0% -> 0%
where the time goes in v1:
time: 215 us; the launch traced here: 214 us
  Pallas kernels  211 us (98%)
  local copies, waits for them, and re-layouts  2.93 us (1%)
    pallas_call x1, Pallas kernels, shards(): pl.pallas_call(force_kernel, out_shape=jax.ShapeDtypeStruct((16, 5, 128),...  110 us
    pallas_call x1, Pallas kernels, shards(): pl.pallas_call(density_kernel, out_shape=(jax.ShapeDtypeStruct((16, 1, 12...  46.2 us
    pallas_call x1, Pallas kernels, shards(): pl.pallas_call(lambda *refs: gather_kernel(devices, *refs), out_shape=(ja...  40.5 us
    pallas_call x1, Pallas kernels, shards(): pl.pallas_call(lambda *refs: pass_kernel(devices, *refs), out_shape=jax.S...  14.8 us

profile of v1, /device:TPU:1, one launch (start us, length us, event | category | flops | bytes accessed | tf_op | source)
XLA Modules:
  0.0 214.4 jit_solution(4976932494944226209)
XLA Ops:
  0.0 0.8 copy.13
  0.8 0.1 reshape.3
  0.9 0.6 pad.4.refs_0_.refs_1_.req_ref
  1.5 40.5 %shard_map.100 = (f32[432,8,128]{2,1,0:T(8,128)}, s32[7,16,128]{2,1,0:T(8,128)}) custom-call(s32[16,128]{1,0:T(8,128)} %pad.4.refs_0_.refs_1_.req_ref, s32[16,128]{1,0:T(8,128)} %pad.4.refs_0_.refs_1_.req_ref, s32[1600]{0:T(1024)} %counts_ref.3, f32[3,1600,128]{2,1,0:T(8,128)} %bitcast.3, f32[3,1600,128]{2,1,0:T(8,128)} %bitcast.4, f32[1600,128]{1,0:T(8,128)} %refs_5_.1, ...), custom_call_target="tpu_custom_call" | custom-call | tf_op jit(solution)/shard_map/pallas_call | solution.py:335
  42.0 46.2 %shard_map.101 = (f32[16,1,128]{2,1,0:T(1,128)}, f32[432,1,128]{2,1,0:T(1,128)}, f32[9,1,128]{2,1,0:T(1,128)}) custom-call(s32[16,128]{1,0:T(8,128)} %pad.4.refs_0_.refs_1_.req_ref, s32[7,16,128]{2,1,0:T(8,128)} %get-tuple-element.11.lists_ref, s32[1600]{0:T(1024)} %counts_ref.3, s32[16]{0:T(128)} %active_ref.3, f32[432,8,128]{2,1,0:T(8,128)} %get-tuple-element.10.near_ref, ...), custom_call_target="tpu_custom_call" | custom-call | tf_op jit(solution)/shard_map/pallas_call | solution.py:353
  88.2 14.8 %shard_map.102.press_ref = f32[432,1,128]{2,1,0:T(1,128)} custom-call(f32[432,1,128]{2,1,0:T(1,128)} %get-tuple-element.12.refs_0_, f32[9,1,128]{2,1,0:T(1,128)} %get-tuple-element.13.refs_1_), custom_call_target="tpu_custom_call" | custom-call | tf_op jit(solution)/shard_map/pallas_call | solution.py:366
  103.0 109.9 %shard_map.103 = f32[16,5,128]{2,1,0:T(8,128)} custom-call(s32[1600]{0:T(1024)} %counts_ref.3, s32[16]{0:T(128)} %active_ref.3, f32[432,8,128]{2,1,0:T(8,128)} %get-tuple-element.10.near_ref, f32[432,1,128]{2,1,0:T(1,128)} %shard_map.102.press_ref, f32[27,8,128]{2,1,0:T(8,128)} %constant.4.clone.shift_ref, f32[16,1,128]{2,1,0:T(1,128)} %get-tuple-element.14.fresh_ref), custom_call_target="tpu_custom_call" | custom-call | tf_op jit(solution)/shard_map/pallas_call | solution.py:379
  212.9 1.5 copy.14

commit v2 on v1

v2 whole, which is shorter than its diff:
```python
import math

import jax
import jax.numpy as jnp
import numpy as np
from jax import lax
from jax.experimental import pallas as pl
from jax.experimental.pallas import tpu as pltpu
from jax.sharding import PartitionSpec as P

MESH = pl.DeviceIdType.MESH
NORM = 8.0 / math.pi
GAS = 2.0 / 3.0
TINY = 1e-14
LIMIT = 56 * 1024 * 1024

STEPS = (16, 4, 20, 1, 5, 17, 21)
WIDE = ((2, 8), (0, 6), (0, 7), (1, 2), (1, 5))
EDGE = ((6, 8), (5, 6), (5, 7), (4, 2), (4, 5), (3, 0), (3, 1), (3, 3), (3, 4))
HOME = (0, 1, 3, 4)
SPAN = 47


def shift_tiles():
    tiles = np.zeros((27, 8, 128), np.float32)
    for slot in range(27):
        tiles[slot, 1] = slot // 9 - 1
        tiles[slot, 2] = slot // 3 % 3 - 1
        tiles[slot, 3] = slot % 3 - 1
    return tiles


def greet(me, devices):
    barrier = pltpu.get_barrier_semaphore()
    for steps in STEPS:
        for other in (me + steps, me + devices - steps):
            pl.semaphore_signal(barrier, inc=1, device_id=(lax.rem(other, devices),), device_id_type=MESH)
    pl.semaphore_wait(barrier, 2 * len(STEPS))


def gather_kernel(
    devices, req_ref, req_send, counts_ref, pos_ref, vel_ref, mass_ref, smooth_ref,
    near_ref, asked_ref, send_ref, edge_ref, lists_ref, ask_out, ask_in, send_sem, recv_sem, local_sem,
):
    me = lax.axis_index("dom")
    cells = mass_ref.shape[0]
    first = me * cells
    lane = lax.broadcasted_iota(jnp.int32, (1, 128), 1)

    def fill(dst, place, cell):
        cell = jnp.clip(cell - first, 0, cells - 1)
        keep = lane < counts_ref[cell]
        dst[place, 0:1, :] = jnp.where(keep, mass_ref[pl.ds(cell, 1), :], 0.0)
        for axis in range(3):
            dst[place, 1 + axis : 2 + axis, :] = pos_ref[axis, pl.ds(cell, 1), :]
            dst[place, 4 + axis : 5 + axis, :] = vel_ref[axis, pl.ds(cell, 1), :]
        dst[place, 7:8, :] = smooth_ref[pl.ds(cell, 1), :]

    greet(me, devices)
    asks = []
    for place, steps in enumerate(STEPS):
        ask = pltpu.make_async_remote_copy(
            req_send, asked_ref.at[place], ask_out.at[place], ask_in.at[place],
            device_id=(lax.rem(me + steps, devices),), device_id_type=MESH,
        )
        ask.start()
        asks.append(ask)

    def home_step(entry, carry):
        for block in HOME:
            fill(near_ref, block * 48 + entry, req_ref[block, entry])
        return carry

    lax.fori_loop(0, SPAN, home_step, 0)
    for ask in asks:
        ask.wait()
    listed = pltpu.make_async_copy(asked_ref, lists_ref, local_sem)
    listed.start()
    listed.wait()
    copies = []

    def requester(place):
        return (lax.rem(me + devices - STEPS[place], devices),)

    def serve(group, start):
        def step(entry, carry):
            for place, block in group:
                fill(send_ref, block * 48 + entry, lists_ref[place, block, entry])
            return carry

        lax.fori_loop(0, SPAN, step, 0)
        for number, (place, block) in enumerate(group):
            rows = pl.ds(block * 48, SPAN)
            copy = pltpu.make_async_remote_copy(
                send_ref.at[rows], near_ref.at[rows], send_sem.at[start + number], recv_sem.at[start + number],
                device_id=requester(place), device_id_type=MESH,
            )
            copy.start()
            copies.append(copy)

    serve(WIDE[:3], 0)
    serve(WIDE[3:], 3)
    for number, (place, block) in enumerate(EDGE):
        fill(edge_ref, number, lists_ref[place, block, SPAN])
        copy = pltpu.make_async_remote_copy(
            edge_ref.at[number], near_ref.at[block * 48 + SPAN], send_sem.at[5 + number], recv_sem.at[5 + number],
            device_id=requester(place), device_id_type=MESH,
        )
        copy.start()
        copies.append(copy)
    for copy in copies:
        copy.wait()


def rows_of(ref, slot, feature):
    return ref[pl.ds(slot * 128 + feature, 16, stride=8), :]


def pick(values, index):
    return jnp.take_along_axis(values, index, axis=1, mode="promise_in_bounds")


def eye():
    return lax.broadcasted_iota(jnp.int32, (128, 128), 0) == lax.broadcasted_iota(jnp.int32, (128, 128), 1)


def column(row):
    return jnp.broadcast_to(jnp.sum(jnp.where(eye(), row, 0.0), axis=1, keepdims=True), (128, 128))


def row_sums(pairs):
    total = jnp.sum(pairs, axis=1, keepdims=True)
    return jnp.sum(jnp.where(eye(), total, 0.0), axis=0, keepdims=True)


def list_jobs(offs_ref, jobs_ref):
    def one_row(row, count):
        def one_chunk(chunk, count):
            jobs_ref[count] = row * 32 + chunk
            return count + 1

        return lax.fori_loop(0, (offs_ref[27, row] + 127) // 128, one_chunk, count)

    return lax.fori_loop(0, 16, one_row, 0)


def pack_rows(offs_ref, row, get, put, width):
    lane = lax.broadcasted_iota(jnp.int32, (width, 128), 1)

    def slot_step(slot, held):
        begin = offs_ref[slot, row]
        end = offs_ref[slot + 1, row]
        turned = get(slot)
        merged = jnp.where(lane >= begin % 128, turned, held)
        put(begin // 128, merged)
        return jnp.where(jnp.broadcast_to(end // 128 > begin // 128, (width, 128)), turned, merged)

    return lax.fori_loop(0, 27, slot_step, get(0), unroll=3)


def density_kernel(
    req_ref, lists_ref, counts_ref, active_ref, near_ref, shift_ref, energy_ref, old_ref,
    fresh_ref, mine_ref, edge_ref, pack_ref, index_ref, offs_out_ref,
    table_ref, mask_ref, offs_ref, jobs_ref, x_ref, y_ref, z_ref, inv_ref, sum_ref, local_sem,
):
    cells = old_ref.shape[0]
    first = lax.axis_index("dom") * cells
    lane = lax.broadcasted_iota(jnp.int32, (1, 128), 1)
    lanes = lax.broadcasted_iota(jnp.int32, (16, 128), 1)
    on_diagonal = lax.broadcasted_iota(jnp.int32, (16, 128), 0) == lanes

    lows, highs = [], []
    for axis in range(3):
        own = rows_of(near_ref, 13, 1 + axis)
        lows.append(jnp.min(own, axis=1, keepdims=True))
        highs.append(jnp.max(own, axis=1, keepdims=True))
    widest = jnp.max(rows_of(near_ref, 13, 7), axis=1, keepdims=True)

    def mask_step(slot, carry):
        away = jnp.zeros((16, 128), jnp.float32)
        for axis, step in enumerate((slot // 9, slot // 3 % 3, slot % 3)):
            at = rows_of(near_ref, slot, 1 + axis) + (step - 1).astype(jnp.float32)
            out = jnp.maximum(jnp.maximum(lows[axis] - at, at - highs[axis]), 0.0)
            away = away + out * out
        reach = jnp.maximum(rows_of(near_ref, slot, 7), widest)
        chosen = (rows_of(near_ref, slot, 0) > 0.0) & (away <= reach * reach * 1.0001)
        mask_ref[pl.ds(slot * 16, 16), :] = jnp.where(chosen, 1.0, 0.0)
        return carry

    lax.fori_loop(0, 27, mask_step, 0, unroll=3)
    high = lax.broadcasted_iota(jnp.int32, (128, 256), 0)
    wide = lax.broadcasted_iota(jnp.int32, (128, 256), 1)
    counter = jnp.where((wide >= 128) | (high <= wide), 1.0, 0.0).astype(jnp.bfloat16)

    def rank_step(slot, begin):
        chosen = mask_ref[pl.ds(slot * 16, 16), :].astype(jnp.bfloat16)
        ranks = jnp.dot(chosen, counter, preferred_element_type=jnp.float32).astype(jnp.int32)
        order = ranks[:, 0:128]
        wanted = (lanes - begin) & 127
        index = jnp.zeros((16, 128), jnp.int32)
        for step in (64, 32, 16, 8, 4, 2, 1):
            index = index + jnp.where(pick(order, index + (step - 1)) <= wanted, step, 0)
        index_ref[pl.ds(slot * 16, 16), :] = index
        offs_out_ref[pl.ds(slot, 1), :] = jnp.sum(jnp.where(on_diagonal, begin, 0), axis=0, keepdims=True)
        return begin + ranks[:, 128:256]

    total = lax.fori_loop(0, 27, rank_step, jnp.zeros((16, 128), jnp.int32), unroll=3)
    offs_out_ref[27:28, :] = jnp.sum(jnp.where(on_diagonal, total, 0), axis=0, keepdims=True)
    offs_out_ref[28:32, :] = jnp.zeros((4, 128), jnp.int32)
    moved = pltpu.make_async_copy(offs_out_ref, offs_ref, local_sem)
    moved.start()
    table_ref[...] = GAS * energy_ref[...] / old_ref[...]

    def own_step(row, carry):
        own = near_ref[pl.ds(1664 + row * 8, 8), :]
        at = pl.ds(row * 128, 128)
        x_ref[at, :] = column(own[1:2])
        y_ref[at, :] = column(own[2:3])
        z_ref[at, :] = column(own[3:4])
        inv_ref[at, :] = column(1.0 / own[7:8])
        sum_ref[at, :] = jnp.zeros((128, 128), jnp.float32)
        return carry

    lax.fori_loop(0, 16, own_step, 0)
    moved.wait()

    def pack_step(row, carry):
        def get(slot):
            tile = near_ref[pl.ds((slot * 16 + row) * 8, 8), :] + shift_ref[slot]
            index = index_ref[pl.ds(slot * 16 + row, 1), :]
            return pick(tile, jnp.broadcast_to(index, (8, 128)))

        def put(chunk, tile):
            pack_ref[row * 28 + chunk] = tile

        held = pack_rows(offs_ref, row, get, put, 8)
        total = offs_ref[27, row]
        wide = lax.broadcasted_iota(jnp.int32, (8, 128), 1)
        deep = lax.broadcasted_iota(jnp.int32, (8, 128), 0)
        put(total // 128, jnp.where((deep == 0) & (wide >= total % 128), 0.0, held))
        return carry

    lax.fori_loop(0, 16, pack_step, 0)
    count = list_jobs(offs_ref, jobs_ref)

    def job_step(job, carry):
        code = jobs_ref[job]
        row = code // 32
        tile = pack_ref[row * 28 + code % 32]
        mass, near_x, near_y, near_z = [jnp.broadcast_to(tile[f : f + 1], (8, 128)) for f in range(4)]
        for part in range(16):
            at = pl.ds(row * 128 + part * 8, 8)
            gap_x = x_ref[at, :] - near_x
            gap_y = y_ref[at, :] - near_y
            gap_z = z_ref[at, :] - near_z
            square = jnp.maximum(gap_x * gap_x + gap_y * gap_y + gap_z * gap_z, TINY)
            ratio = square * lax.rsqrt(square) * inv_ref[at, :]
            outer = 1.0 - jnp.minimum(ratio, 1.0)
            inner = 1.0 - jnp.minimum(ratio + ratio, 1.0)
            weight = (outer + outer) * (outer * outer) - inner * (inner * inner)
            sum_ref[at, :] = sum_ref[at, :] + weight * mass
        return carry

    lax.fori_loop(0, count, job_step, 0)

    def end_step(row, carry):
        own = near_ref[pl.ds(1664 + row * 8, 8), :]
        inverse = 1.0 / own[7:8]
        total = row_sums(sum_ref[pl.ds(row * 128, 128), :])
        cell = active_ref[row] - first
        fresh = jnp.where(
            lane < counts_ref[cell], total * (NORM * inverse * inverse * inverse), old_ref[pl.ds(cell, 1), :]
        )
        fresh_ref[row] = fresh
        table_ref[pl.ds(cell, 1), :] = GAS * energy_ref[pl.ds(cell, 1), :] / fresh
        return carry

    lax.fori_loop(0, 16, end_step, 0)

    def collect(entry, carry):
        for block in HOME:
            mine_ref[block * 48 + entry] = table_ref[pl.ds(req_ref[block, entry] - first, 1), :]
        for place, block in WIDE:
            mine_ref[block * 48 + entry] = table_ref[pl.ds(lists_ref[place, block, entry] - first, 1), :]
        return carry

    lax.fori_loop(0, SPAN, collect, 0)
    for number, (place, block) in enumerate(EDGE):
        mine_ref[block * 48 + SPAN] = jnp.zeros((1, 128), jnp.float32)
        edge_ref[number] = table_ref[pl.ds(lists_ref[place, block, SPAN] - first, 1), :]


def pass_kernel(devices, mine_ref, edge_ref, near_ref, send_sem, recv_sem, local_sem):
    me = lax.axis_index("dom")
    greet(me, devices)
    copies = []

    def requester(place):
        return (lax.rem(me + devices - STEPS[place], devices),)

    for number, (place, block) in enumerate(WIDE):
        rows = pl.ds(block * 48, SPAN)
        copies.append(
            pltpu.make_async_remote_copy(
                mine_ref.at[rows], near_ref.at[rows], send_sem.at[number], recv_sem.at[number],
                device_id=requester(place), device_id_type=MESH,
            )
        )
    for number, (place, block) in enumerate(EDGE):
        copies.append(
            pltpu.make_async_remote_copy(
                edge_ref.at[number], near_ref.at[block * 48 + SPAN], send_sem.at[5 + number], recv_sem.at[5 + number],
                device_id=requester(place), device_id_type=MESH,
            )
        )
    for number, block in enumerate(HOME):
        rows = pl.ds(block * 48, SPAN)
        copies.append(pltpu.make_async_copy(mine_ref.at[rows], near_ref.at[rows], local_sem.at[number]))
    for copy in copies:
        copy.start()
    for copy in copies:
        copy.wait()


def slope(ratio):
    low = jnp.minimum(ratio, 1.0)
    high = jnp.minimum(ratio + ratio, 1.0)
    return (high - low) * (2.0 - (low + high))


def force_kernel(
    counts_ref, active_ref, offs_ref, near_ref, press_ref, pack_ref, index_ref, fresh_ref,
    hydro_ref, turned_ref, chunk_ref, jobs_ref, x_ref, y_ref, z_ref, vx_ref, vy_ref, vz_ref, inv_ref, own_ref,
    ax_ref, ay_ref, az_ref, rate_ref,
):
    cells = counts_ref.shape[0]
    first = lax.axis_index("dom") * cells
    lane = lax.broadcasted_iota(jnp.int32, (1, 128), 1)

    def turn_step(slot, carry):
        at = pl.ds(slot * 16, 16)
        turned_ref[at, :] = pick(press_ref[at, :], index_ref[at, :])
        return carry

    lax.fori_loop(0, 27, turn_step, 0, unroll=3)

    def own_step(row, carry):
        own = near_ref[pl.ds(1664 + row * 8, 8), :]
        at = pl.ds(row * 128, 128)
        inverse = 1.0 / own[7:8]
        inv_sq = inverse * inverse
        for ref, value in (
            (x_ref, own[1:2]), (y_ref, own[2:3]), (z_ref, own[3:4]),
            (vx_ref, own[4:5]), (vy_ref, own[5:6]), (vz_ref, own[6:7]),
            (inv_ref, inverse), (own_ref, (6.0 * NORM) * (inv_sq * inv_sq) * press_ref[pl.ds(208 + row, 1), :]),
        ):
            ref[at, :] = column(value)
        for ref in (ax_ref, ay_ref, az_ref, rate_ref):
            ref[at, :] = jnp.zeros((128, 128), jnp.float32)

        def get(slot):
            return turned_ref[pl.ds(slot * 16 + row, 1), :]

        def put(chunk, value):
            chunk_ref[pl.ds(row * 28 + chunk, 1), :] = value

        held = pack_rows(offs_ref, row, get, put, 1)
        put(offs_ref[27, row] // 128, held)
        return carry

    lax.fori_loop(0, 16, own_step, 0)
    count = list_jobs(offs_ref, jobs_ref)

    def job_step(job, carry):
        code = jobs_ref[job]
        row = code // 32
        place = row * 28 + code % 32
        tile = pack_ref[place]
        near_inv = 1.0 / tile[7:8]
        near_sq = near_inv * near_inv
        push = (6.0 * NORM) * tile[0:1] * (near_sq * near_sq) * chunk_ref[pl.ds(place, 1), :]
        mass, near_x, near_y, near_z, near_vx, near_vy, near_vz = [
            jnp.broadcast_to(tile[f : f + 1], (8, 128)) for f in range(7)
        ]
        near_inv = jnp.broadcast_to(near_inv, (8, 128))
        push = jnp.broadcast_to(push, (8, 128))
        for part in range(16):
            at = pl.ds(row * 128 + part * 8, 8)
            gap_x = x_ref[at, :] - near_x
            gap_y = y_ref[at, :] - near_y
            gap_z = z_ref[at, :] - near_z
            square = jnp.maximum(gap_x * gap_x + gap_y * gap_y + gap_z * gap_z, TINY)
            root = lax.rsqrt(square)
            gap = square * root
            pull = slope(gap * inv_ref[at, :]) * root * mass
            both = own_ref[at, :] * pull + slope(gap * near_inv) * push * root
            work = (vx_ref[at, :] - near_vx) * gap_x + (vy_ref[at, :] - near_vy) * gap_y + (vz_ref[at, :] - near_vz) * gap_z
            ax_ref[at, :] = ax_ref[at, :] + both * gap_x
            ay_ref[at, :] = ay_ref[at, :] + both * gap_y
            az_ref[at, :] = az_ref[at, :] + both * gap_z
            rate_ref[at, :] = rate_ref[at, :] + pull * work
        return carry

    lax.fori_loop(0, count, job_step, 0)

    def end_step(row, carry):
        own = near_ref[pl.ds(1664 + row * 8, 8), :]
        inverse = 1.0 / own[7:8]
        inv_sq = inverse * inverse
        factor = (-6.0 * NORM) * (inv_sq * inv_sq) * press_ref[pl.ds(208 + row, 1), :]
        at = pl.ds(row * 128, 128)
        keep = lane < counts_ref[active_ref[row] - first]
        values = [fresh_ref[row]] + [row_sums(ref[at, :]) for ref in (ax_ref, ay_ref, az_ref)]
        values.append(factor * row_sums(rate_ref[at, :]))
        for number, value in enumerate(values):
            hydro_ref[number, pl.ds(row, 1), :] = jnp.where(keep, value, 0.0)
        return carry

    lax.fori_loop(0, 16, end_step, 0)


def specs(kinds):
    return [pl.BlockSpec(memory_space=pltpu.SMEM if kind == "s" else pltpu.VMEM) for kind in kinds]


def floats(*shape):
    return jax.ShapeDtypeStruct(shape, jnp.float32)


def density_call(*args):
    square = pltpu.VMEM((2048, 128), jnp.float32)
    return pl.pallas_call(
        density_kernel,
        out_shape=(
            floats(16, 1, 128), floats(432, 1, 128), floats(9, 1, 128), floats(448, 8, 128),
            jax.ShapeDtypeStruct((432, 128), jnp.int32), jax.ShapeDtypeStruct((32, 128), jnp.int32),
        ),
        in_specs=specs("ssssvvvv"),
        out_specs=tuple(specs("vvvvvv")),
        scratch_shapes=[
            pltpu.VMEM((1600, 128), jnp.float32), pltpu.VMEM((432, 128), jnp.float32),
            pltpu.SMEM((32, 128), jnp.int32), pltpu.SMEM((448,), jnp.int32),
        ] + [square] * 5 + [pltpu.SemaphoreType.DMA],
        compiler_params=pltpu.CompilerParams(vmem_limit_bytes=LIMIT),
        name="density",
    )(*args)


def force_call(*args):
    square = pltpu.VMEM((2048, 128), jnp.float32)
    return pl.pallas_call(
        force_kernel,
        out_shape=floats(5, 16, 128),
        in_specs=specs("sssvvvvv"),
        out_specs=specs("v")[0],
        scratch_shapes=[
            pltpu.VMEM((432, 128), jnp.float32), pltpu.VMEM((448, 128), jnp.float32), pltpu.SMEM((448,), jnp.int32),
        ] + [square] * 12,
        compiler_params=pltpu.CompilerParams(vmem_limit_bytes=LIMIT),
        name="force",
    )(*args)


def shards(positions, velocity, mass, smoothing, energy, density_old, counts, active, neighbours):
    devices = lax.axis_size("dom")
    vmem = pl.BlockSpec(memory_space=pltpu.VMEM)
    smem = pl.BlockSpec(memory_space=pltpu.SMEM)
    pos = jnp.transpose(positions, (1, 0, 2))
    vel = jnp.transpose(velocity, (1, 0, 2))
    requests = jnp.pad(neighbours.T.reshape(9, 48), ((0, 7), (0, 80)))
    shifts = jnp.asarray(shift_tiles())
    f32 = jnp.float32

    near, asked = pl.pallas_call(
        lambda *refs: gather_kernel(devices, *refs),
        out_shape=(jax.ShapeDtypeStruct((432, 8, 128), f32), jax.ShapeDtypeStruct((7, 16, 128), jnp.int32)),
        in_specs=[smem, vmem, smem, vmem, vmem, vmem, vmem],
        out_specs=(vmem, vmem),
        scratch_shapes=[
            pltpu.VMEM((432, 8, 128), f32),
            pltpu.VMEM((9, 8, 128), f32),
            pltpu.SMEM((7, 16, 128), jnp.int32),
            pltpu.SemaphoreType.DMA((7,)),
            pltpu.SemaphoreType.DMA((7,)),
            pltpu.SemaphoreType.DMA((14,)),
            pltpu.SemaphoreType.DMA((14,)),
            pltpu.SemaphoreType.DMA,
        ],
        compiler_params=pltpu.CompilerParams(collective_id=0, has_side_effects=True, vmem_limit_bytes=LIMIT),
    )(requests, requests, counts, pos, vel, mass, smoothing)

    flat = near.reshape(3456, 128)
    fresh, mine, edge, packed, index, offs = density_call(
        requests, asked, counts, active, flat, shifts, energy, density_old
    )

    press = pl.pallas_call(
        lambda *refs: pass_kernel(devices, *refs),
        out_shape=jax.ShapeDtypeStruct((432, 1, 128), f32),
        in_specs=[vmem, vmem],
        out_specs=vmem,
        scratch_shapes=[
            pltpu.SemaphoreType.DMA((14,)),
            pltpu.SemaphoreType.DMA((14,)),
            pltpu.SemaphoreType.DMA((4,)),
        ],
        compiler_params=pltpu.CompilerParams(collective_id=1, has_side_effects=True, vmem_limit_bytes=LIMIT),
    )(mine, edge)

    hydro = force_call(counts, active, offs, flat, press.reshape(432, 128), packed, index, fresh)
    return jnp.transpose(hydro, (1, 0, 2))


def solution(mesh):
    placed = (
        P("dom", None, None),
        P("dom", None, None),
        P("dom", None),
        P("dom", None),
        P("dom", None),
        P("dom", None),
        P("dom"),
        P("dom"),
        P("dom", None),
    )
    return jax.shard_map(
        shards, mesh=mesh, in_specs=placed, out_specs=P("dom", None, None), check_vma=False
    )
```

time: 215 us -> 133 us (0.62)
  Pallas kernels: 211 us -> 131 us
    pallas_call x2, Pallas kernels: 156 us -> 75.4 us  [the longest x1 39.5 us: density_call(): pl.pallas_call(density_kernel, out_shape=(floats(16, 1, 128), floats(432,...]
where the time goes in v2:
time: 133 us
  Pallas kernels  131 us (98%)
  local copies, waits for them, and re-layouts  1.46 us (1%)
    pallas_call x1, Pallas kernels, shards(): pl.pallas_call(lambda *refs: gather_kernel(devices, *refs), out_shape=(ja...  40.5 us
    pallas_call x1, Pallas kernels, density_call(): pl.pallas_call(density_kernel, out_shape=(floats(16, 1, 128), floats(432,...  39.5 us
    pallas_call x1, Pallas kernels, force_call(): pl.pallas_call(force_kernel, out_shape=floats(5, 16, 128), in_specs=specs...  35.9 us
    pallas_call x1, Pallas kernels, shards(): pl.pallas_call(lambda *refs: pass_kernel(devices, *refs), out_shape=jax.S...  15.5 us

profile of v2, /device:TPU:1, one launch (start us, length us, event | category | flops | bytes accessed | tf_op | source)
XLA Modules:
  0.0 132.9 jit_solution(15474431227573188202)
XLA Ops:
  0.0 0.8 copy.12
  0.8 0.1 reshape.9
  0.9 0.6 pad.4.refs_0_.refs_1_.req_ref
  1.5 40.5 %shard_map.100 = (f32[432,8,128]{2,1,0:T(8,128)}, s32[7,16,128]{2,1,0:T(8,128)}) custom-call(s32[16,128]{1,0:T(8,128)} %pad.4.refs_0_.refs_1_.req_ref, s32[16,128]{1,0:T(8,128)} %pad.4.refs_0_.refs_1_.req_ref, s32[1600]{0:T(1024)} %counts_ref.3, f32[3,1600,128]{2,1,0:T(8,128)} %bitcast.8, f32[3,1600,128]{2,1,0:T(8,128)} %bitcast.9, f32[1600,128]{1,0:T(8,128)} %refs_5_.1, ...), custom_call_target="tpu_custom_call" | custom-call | tf_op jit(solution)/shard_map/pallas_call | solution.py:474
  42.0 39.5 %density.1 = (f32[16,1,128]{2,1,0:T(1,128)}, f32[432,1,128]{2,1,0:T(1,128)}, f32[9,1,128]{2,1,0:T(1,128)}, f32[448,8,128]{2,1,0:T(8,128)}, s32[432,128]{1,0:T(8,128)}, /*index=5*/s32[32,128]{1,0:T(8,128)}) custom-call(s32[16,128]{1,0:T(8,128)} %pad.4.refs_0_.refs_1_.req_ref, s32[7,16,128]{2,1,0:T(8,128)} %get-tuple-element.13.lists_ref, s32[1600]{0:T(1024)} %counts_ref.3, ...), custom_call_target="tpu_custom_call" | custom-call | tf_op jit(solution)/shard_map/density/pallas_call | solution.py:432
  81.5 15.5 %shard_map.101 = f32[432,1,128]{2,1,0:T(1,128)} custom-call(f32[432,1,128]{2,1,0:T(1,128)} %get-tuple-element.16.refs_0_, f32[9,1,128]{2,1,0:T(1,128)} %get-tuple-element.17.refs_1_), custom_call_target="tpu_custom_call" | custom-call | tf_op jit(solution)/shard_map/pallas_call | solution.py:497
  97.0 35.9 %force.1 = f32[5,16,128]{2,1,0:T(8,128)} custom-call(s32[1600]{0:T(1024)} %counts_ref.3, s32[16]{0:T(128)} %active_ref.3, s32[32,128]{1,0:T(8,128)} %get-tuple-element.15.offs_ref, f32[3456,128]{1,0:T(8,128)} %bitcast.7, f32[432,128]{1,0:T(8,128)} %bitcast.10, f32[448,8,128]{2,1,0:T(8,128)} %get-tuple-element.18.pack_ref, ...), custom_call_target="tpu_custom_call" | custom-call | tf_op jit(solution)/shard_map/force/pallas_call | solution.py:451

commit v3 on v2

--- a/solution.py
+++ b/solution.py
@@ -15,7 +15,7 @@
 LIMIT = 56 * 1024 * 1024
 
 STEPS = (16, 4, 20, 1, 5, 17, 21)
-WIDE = ((2, 8), (0, 6), (0, 7), (1, 2), (1, 5))
+WIDE = ((0, 6), (0, 7), (1, 2), (1, 5), (2, 8))
 EDGE = ((6, 8), (5, 6), (5, 7), (4, 2), (4, 5), (3, 0), (3, 1), (3, 3), (3, 4))
 HOME = (0, 1, 3, 4)
 SPAN = 47
@@ -54,7 +54,7 @@
         for axis in range(3):
             dst[place, 1 + axis : 2 + axis, :] = pos_ref[axis, pl.ds(cell, 1), :]
             dst[place, 4 + axis : 5 + axis, :] = vel_ref[axis, pl.ds(cell, 1), :]
-        dst[place, 7:8, :] = smooth_ref[pl.ds(cell, 1), :]
+        dst[place, 7:8, :] = 1.0 / smooth_ref[pl.ds(cell, 1), :]
 
     greet(me, devices)
     asks = []
@@ -72,12 +72,13 @@
         return carry
 
     lax.fori_loop(0, SPAN, home_step, 0)
-    for ask in asks:
-        ask.wait()
-    listed = pltpu.make_async_copy(asked_ref, lists_ref, local_sem)
-    listed.start()
-    listed.wait()
     copies = []
+
+    def hear(place):
+        asks[place].wait_recv()
+        listed = pltpu.make_async_copy(asked_ref.at[place], lists_ref.at[place], local_sem.at[place])
+        listed.start()
+        listed.wait()
 
     def requester(place):
         return (lax.rem(me + devices - STEPS[place], devices),)
@@ -98,8 +99,14 @@
             copy.start()
             copies.append(copy)
 
-    serve(WIDE[:3], 0)
-    serve(WIDE[3:], 3)
+    hear(0)
+    serve(WIDE[0:2], 0)
+    hear(1)
+    serve(WIDE[2:4], 2)
+    hear(2)
+    serve(WIDE[4:5], 4)
+    for place in (3, 4, 5, 6):
+        hear(place)
     for number, (place, block) in enumerate(EDGE):
         fill(edge_ref, number, lists_ref[place, block, SPAN])
         copy = pltpu.make_async_remote_copy(
@@ -110,6 +117,8 @@
         copies.append(copy)
     for copy in copies:
         copy.wait()
+    for ask in asks:
+        ask.wait_send()
 
 
 def rows_of(ref, slot, feature):
@@ -133,15 +142,47 @@
     return jnp.sum(jnp.where(eye(), total, 0.0), axis=0, keepdims=True)
 
 
-def list_jobs(offs_ref, jobs_ref):
-    def one_row(row, count):
-        def one_chunk(chunk, count):
-            jobs_ref[count] = row * 32 + chunk
-            return count + 1
-
-        return lax.fori_loop(0, (offs_ref[27, row] + 127) // 128, one_chunk, count)
-
-    return lax.fori_loop(0, 16, one_row, 0)
+def list_jobs(offs_ref, counts_ref, active_ref, first, order_ref, jobs_ref):
+    place = jnp.int32(0)
+    ends = []
+    for low, high in ((0, 80), (80, 96), (96, 112), (112, 128)):
+        for row in range(16):
+            own = counts_ref[active_ref[row] - first]
+            order_ref[place] = row
+            place = place + ((own > low) & (own <= high)).astype(jnp.int32)
+        ends.append(place)
+    count = jnp.int32(0)
+    begin = jnp.int32(0)
+    jobs_ref[512] = count
+    for number, end in enumerate(ends):
+        def one_row(place, count):
+            row = order_ref[place]
+            chunks = (offs_ref[27, row] + 127) // 128
+            for chunk in range(10):
+                jobs_ref[count + chunk] = row * 32 + chunk
+
+            def one_chunk(chunk, carry):
+                jobs_ref[count + chunk] = row * 32 + chunk
+                return carry
+
+            lax.fori_loop(10, chunks, one_chunk, 0)
+            return count + chunks
+
+        count = lax.fori_loop(begin, end, one_row, count)
+        jobs_ref[count] = 31
+        count = count + count % 2
+        jobs_ref[513 + number] = count
+        begin = end
+
+
+def run_jobs(jobs_ref, step):
+    for number, parts in enumerate((10, 12, 14, 16)):
+        def two(pair, carry):
+            step(2 * pair, parts)
+            step(2 * pair + 1, parts)
+            return carry
+
+        lax.fori_loop(jobs_ref[512 + number] // 2, jobs_ref[513 + number] // 2, two, 0)
 
 
 def pack_rows(offs_ref, row, get, put, width):
@@ -155,13 +196,13 @@
         put(begin // 128, merged)
         return jnp.where(jnp.broadcast_to(end // 128 > begin // 128, (width, 128)), turned, merged)
 
-    return lax.fori_loop(0, 27, slot_step, get(0), unroll=3)
+    return lax.fori_loop(0, 27, slot_step, get(0), unroll=27)
 
 
 def density_kernel(
     req_ref, lists_ref, counts_ref, active_ref, near_ref, shift_ref, energy_ref, old_ref,
-    fresh_ref, mine_ref, edge_ref, pack_ref, index_ref, offs_out_ref,
-    table_ref, mask_ref, offs_ref, jobs_ref, x_ref, y_ref, z_ref, inv_ref, sum_ref, local_sem,
+    fresh_ref, mine_ref, edge_ref, pack_ref, index_ref, offs_out_ref, jobs_ref,
+    table_ref, mask_ref, offs_ref, order_ref, x_ref, y_ref, z_ref, inv_ref, sum_ref, local_sem,
 ):
     cells = old_ref.shape[0]
     first = lax.axis_index("dom") * cells
@@ -174,7 +215,7 @@
         own = rows_of(near_ref, 13, 1 + axis)
         lows.append(jnp.min(own, axis=1, keepdims=True))
         highs.append(jnp.max(own, axis=1, keepdims=True))
-    widest = jnp.max(rows_of(near_ref, 13, 7), axis=1, keepdims=True)
+    widest = jnp.min(rows_of(near_ref, 13, 7), axis=1, keepdims=True)
 
     def mask_step(slot, carry):
         away = jnp.zeros((16, 128), jnp.float32)
@@ -182,12 +223,12 @@
             at = rows_of(near_ref, slot, 1 + axis) + (step - 1).astype(jnp.float32)
             out = jnp.maximum(jnp.maximum(lows[axis] - at, at - highs[axis]), 0.0)
             away = away + out * out
-        reach = jnp.maximum(rows_of(near_ref, slot, 7), widest)
-        chosen = (rows_of(near_ref, slot, 0) > 0.0) & (away <= reach * reach * 1.0001)
+        reach = jnp.minimum(rows_of(near_ref, slot, 7), widest)
+        chosen = (rows_of(near_ref, slot, 0) > 0.0) & (away * (reach * reach) <= 1.0001)
         mask_ref[pl.ds(slot * 16, 16), :] = jnp.where(chosen, 1.0, 0.0)
         return carry
 
-    lax.fori_loop(0, 27, mask_step, 0, unroll=3)
+    lax.fori_loop(0, 27, mask_step, 0, unroll=27)
     high = lax.broadcasted_iota(jnp.int32, (128, 256), 0)
     wide = lax.broadcasted_iota(jnp.int32, (128, 256), 1)
     counter = jnp.where((wide >= 128) | (high <= wide), 1.0, 0.0).astype(jnp.bfloat16)
@@ -204,7 +245,7 @@
         offs_out_ref[pl.ds(slot, 1), :] = jnp.sum(jnp.where(on_diagonal, begin, 0), axis=0, keepdims=True)
         return begin + ranks[:, 128:256]
 
-    total = lax.fori_loop(0, 27, rank_step, jnp.zeros((16, 128), jnp.int32), unroll=3)
+    total = lax.fori_loop(0, 27, rank_step, jnp.zeros((16, 128), jnp.int32), unroll=27)
     offs_out_ref[27:28, :] = jnp.sum(jnp.where(on_diagonal, total, 0), axis=0, keepdims=True)
     offs_out_ref[28:32, :] = jnp.zeros((4, 128), jnp.int32)
     moved = pltpu.make_async_copy(offs_out_ref, offs_ref, local_sem)
@@ -213,12 +254,9 @@
 
     def own_step(row, carry):
         own = near_ref[pl.ds(1664 + row * 8, 8), :]
-        at = pl.ds(row * 128, 128)
-        x_ref[at, :] = column(own[1:2])
-        y_ref[at, :] = column(own[2:3])
-        z_ref[at, :] = column(own[3:4])
-        inv_ref[at, :] = column(1.0 / own[7:8])
-        sum_ref[at, :] = jnp.zeros((128, 128), jnp.float32)
+        for ref, feature in ((x_ref, 1), (y_ref, 2), (z_ref, 3), (inv_ref, 7)):
+            ref[pl.ds(row * 128, 128), :] = column(own[feature : feature + 1])
+        sum_ref[pl.ds(row * 128, 128), :] = jnp.zeros((128, 128), jnp.float32)
         return carry
 
     lax.fori_loop(0, 16, own_step, 0)
@@ -231,24 +269,25 @@
             return pick(tile, jnp.broadcast_to(index, (8, 128)))
 
         def put(chunk, tile):
-            pack_ref[row * 28 + chunk] = tile
+            pack_ref[row * 32 + chunk] = tile
 
         held = pack_rows(offs_ref, row, get, put, 8)
         total = offs_ref[27, row]
         wide = lax.broadcasted_iota(jnp.int32, (8, 128), 1)
         deep = lax.broadcasted_iota(jnp.int32, (8, 128), 0)
         put(total // 128, jnp.where((deep == 0) & (wide >= total % 128), 0.0, held))
+        put(31, jnp.where(deep == 0, 0.0, held))
         return carry
 
     lax.fori_loop(0, 16, pack_step, 0)
-    count = list_jobs(offs_ref, jobs_ref)
-
-    def job_step(job, carry):
+    list_jobs(offs_ref, counts_ref, active_ref, first, order_ref, jobs_ref)
+
+    def job_step(job, parts):
         code = jobs_ref[job]
         row = code // 32
-        tile = pack_ref[row * 28 + code % 32]
+        tile = pack_ref[code]
         mass, near_x, near_y, near_z = [jnp.broadcast_to(tile[f : f + 1], (8, 128)) for f in range(4)]
-        for part in range(16):
+        for part in range(parts):
             at = pl.ds(row * 128 + part * 8, 8)
             gap_x = x_ref[at, :] - near_x
             gap_y = y_ref[at, :] - near_y
@@ -259,13 +298,12 @@
             inner = 1.0 - jnp.minimum(ratio + ratio, 1.0)
             weight = (outer + outer) * (outer * outer) - inner * (inner * inner)
             sum_ref[at, :] = sum_ref[at, :] + weight * mass
-        return carry
-
-    lax.fori_loop(0, count, job_step, 0)
+
+    run_jobs(jobs_ref, job_step)
 
     def end_step(row, carry):
         own = near_ref[pl.ds(1664 + row * 8, 8), :]
-        inverse = 1.0 / own[7:8]
+        inverse = own[7:8]
         total = row_sums(sum_ref[pl.ds(row * 128, 128), :])
         cell = active_ref[row] - first
         fresh = jnp.where(
@@ -329,25 +367,29 @@
 
 
 def force_kernel(
-    counts_ref, active_ref, offs_ref, near_ref, press_ref, pack_ref, index_ref, fresh_ref,
-    hydro_ref, turned_ref, chunk_ref, jobs_ref, x_ref, y_ref, z_ref, vx_ref, vy_ref, vz_ref, inv_ref, own_ref,
-    ax_ref, ay_ref, az_ref, rate_ref,
+    counts_ref, active_ref, offs_ref, jobs_ref, all_ref, press_ref, pack_ref, index_ref, fresh_ref,
+    hydro_ref, near_ref, turned_ref, chunk_ref, x_ref, y_ref, z_ref, vx_ref, vy_ref, vz_ref, inv_ref, own_ref,
+    ax_ref, ay_ref, az_ref, rate_ref, own_sem,
 ):
     cells = counts_ref.shape[0]
     first = lax.axis_index("dom") * cells
     lane = lax.broadcasted_iota(jnp.int32, (1, 128), 1)
 
+    own_copy = pltpu.make_async_copy(all_ref.at[pl.ds(1664, 128)], near_ref, own_sem)
+    own_copy.start()
+
     def turn_step(slot, carry):
         at = pl.ds(slot * 16, 16)
         turned_ref[at, :] = pick(press_ref[at, :], index_ref[at, :])
         return carry
 
-    lax.fori_loop(0, 27, turn_step, 0, unroll=3)
+    lax.fori_loop(0, 27, turn_step, 0, unroll=9)
+    own_copy.wait()
 
     def own_step(row, carry):
-        own = near_ref[pl.ds(1664 + row * 8, 8), :]
+        own = near_ref[pl.ds(row * 8, 8), :]
         at = pl.ds(row * 128, 128)
-        inverse = 1.0 / own[7:8]
+        inverse = own[7:8]
         inv_sq = inverse * inverse
         for ref, value in (
             (x_ref, own[1:2]), (y_ref, own[2:3]), (z_ref, own[3:4]),
@@ -362,21 +404,20 @@
             return turned_ref[pl.ds(slot * 16 + row, 1), :]
 
         def put(chunk, value):
-            chunk_ref[pl.ds(row * 28 + chunk, 1), :] = value
+            chunk_ref[pl.ds(row * 32 + chunk, 1), :] = value
 
         held = pack_rows(offs_ref, row, get, put, 1)
         put(offs_ref[27, row] // 128, held)
+        put(31, held)
         return carry
 
     lax.fori_loop(0, 16, own_step, 0)
-    count = list_jobs(offs_ref, jobs_ref)
-
-    def job_step(job, carry):
-        code = jobs_ref[job]
-        row = code // 32
-        place = row * 28 + code % 32
+
+    def job_step(job, parts):
+        place = jobs_ref[job]
+        row = place // 32
         tile = pack_ref[place]
-        near_inv = 1.0 / tile[7:8]
+        near_inv = tile[7:8]
         near_sq = near_inv * near_inv
         push = (6.0 * NORM) * tile[0:1] * (near_sq * near_sq) * chunk_ref[pl.ds(place, 1), :]
         mass, near_x, near_y, near_z, near_vx, near_vy, near_vz = [
@@ -384,7 +425,7 @@
         ]
         near_inv = jnp.broadcast_to(near_inv, (8, 128))
         push = jnp.broadcast_to(push, (8, 128))
-        for part in range(16):
+        for part in range(parts):
             at = pl.ds(row * 128 + part * 8, 8)
             gap_x = x_ref[at, :] - near_x
             gap_y = y_ref[at, :] - near_y
@@ -399,13 +440,12 @@
             ay_ref[at, :] = ay_ref[at, :] + both * gap_y
             az_ref[at, :] = az_ref[at, :] + both * gap_z
             rate_ref[at, :] = rate_ref[at, :] + pull * work
-        return carry
-
-    lax.fori_loop(0, count, job_step, 0)
+
+    run_jobs(jobs_ref, job_step)
 
     def end_step(row, carry):
-        own = near_ref[pl.ds(1664 + row * 8, 8), :]
-        inverse = 1.0 / own[7:8]
+        own = near_ref[pl.ds(row * 8, 8), :]
+        inverse = own[7:8]
         inv_sq = inverse * inverse
         factor = (-6.0 * NORM) * (inv_sq * inv_sq) * press_ref[pl.ds(208 + row, 1), :]
         at = pl.ds(row * 128, 128)
@@ -432,14 +472,15 @@
     return pl.pallas_call(
         density_kernel,
         out_shape=(
-            floats(16, 1, 128), floats(432, 1, 128), floats(9, 1, 128), floats(448, 8, 128),
+            floats(16, 1, 128), floats(432, 1, 128), floats(9, 1, 128), floats(512, 8, 128),
             jax.ShapeDtypeStruct((432, 128), jnp.int32), jax.ShapeDtypeStruct((32, 128), jnp.int32),
+            jax.ShapeDtypeStruct((640,), jnp.int32),
         ),
         in_specs=specs("ssssvvvv"),
-        out_specs=tuple(specs("vvvvvv")),
+        out_specs=tuple(specs("vvvvvvs")),
         scratch_shapes=[
             pltpu.VMEM((1600, 128), jnp.float32), pltpu.VMEM((432, 128), jnp.float32),
-            pltpu.SMEM((32, 128), jnp.int32), pltpu.SMEM((448,), jnp.int32),
+            pltpu.SMEM((32, 128), jnp.int32), pltpu.SMEM((32,), jnp.int32),
         ] + [square] * 5 + [pltpu.SemaphoreType.DMA],
         compiler_params=pltpu.CompilerParams(vmem_limit_bytes=LIMIT),
         name="density",
@@ -451,11 +492,12 @@
     return pl.pallas_call(
         force_kernel,
         out_shape=floats(5, 16, 128),
-        in_specs=specs("sssvvvvv"),
+        in_specs=specs("ssss") + [pl.BlockSpec(memory_space=pl.ANY)] + specs("vvvv"),
         out_specs=specs("v")[0],
         scratch_shapes=[
-            pltpu.VMEM((432, 128), jnp.float32), pltpu.VMEM((448, 128), jnp.float32), pltpu.SMEM((448,), jnp.int32),
-        ] + [square] * 12,
+            pltpu.VMEM((128, 128), jnp.float32), pltpu.VMEM((432, 128), jnp.float32),
+            pltpu.VMEM((512, 128), jnp.float32),
+        ] + [square] * 12 + [pltpu.SemaphoreType.DMA],
         compiler_params=pltpu.CompilerParams(vmem_limit_bytes=LIMIT),
         name="force",
     )(*args)
@@ -484,13 +526,13 @@
             pltpu.SemaphoreType.DMA((7,)),
             pltpu.SemaphoreType.DMA((14,)),
             pltpu.SemaphoreType.DMA((14,)),
-            pltpu.SemaphoreType.DMA,
+            pltpu.SemaphoreType.DMA((7,)),
         ],
         compiler_params=pltpu.CompilerParams(collective_id=0, has_side_effects=True, vmem_limit_bytes=LIMIT),
     )(requests, requests, counts, pos, vel, mass, smoothing)
 
     flat = near.reshape(3456, 128)
-    fresh, mine, edge, packed, index, offs = density_call(
+    fresh, mine, edge, packed, index, offs, jobs = density_call(
         requests, asked, counts, active, flat, shifts, energy, density_old
     )
 
@@ -507,7 +549,7 @@
         compiler_params=pltpu.CompilerParams(collective_id=1, has_side_effects=True, vmem_limit_bytes=LIMIT),
     )(mine, edge)
 
-    hydro = force_call(counts, active, offs, flat, press.reshape(432, 128), packed, index, fresh)
+    hydro = force_call(counts, active, offs, jobs, flat, press.reshape(432, 128), packed, index, fresh)
     return jnp.transpose(hydro, (1, 0, 2))
 
 

time: 133 us -> 107 us (0.80)
  Pallas kernels: 131 us -> 105 us
    pallas_call x1, Pallas kernels: 39.5 us -> 24.1 us  [density_call(): pl.pallas_call(density_kernel, out_shape=(floats(16, 1, 128), floats(432,...]
    pallas_call x1, Pallas kernels: 35.9 us -> 26.4 us  [force_call(): pl.pallas_call(force_kernel, out_shape=floats(5, 16, 128), in_specs=specs...]
where the time goes in v3:
time: 107 us; the launch traced here: 106 us
  Pallas kernels  105 us (98%)
  local copies, waits for them, and re-layouts  1.46 us (1%)
    pallas_call x1, Pallas kernels, shards(): pl.pallas_call(lambda *refs: gather_kernel(devices, *refs), out_shape=(ja...  39.9 us
    pallas_call x1, Pallas kernels, force_call(): pl.pallas_call(force_kernel, out_shape=floats(5, 16, 128), in_specs=specs...  26.4 us
    pallas_call x1, Pallas kernels, density_call(): pl.pallas_call(density_kernel, out_shape=(floats(16, 1, 128), floats(432,...  24.1 us
    pallas_call x1, Pallas kernels, shards(): pl.pallas_call(lambda *refs: pass_kernel(devices, *refs), out_shape=jax.S...  14.4 us

profile of v3, /device:TPU:1, one launch (start us, length us, event | category | flops | bytes accessed | tf_op | source)
XLA Modules:
  0.0 106.3 jit_solution(8183605694728883007)
XLA Ops:
  0.0 0.8 copy.12
  0.8 0.1 reshape.9
  0.9 0.6 pad.4.refs_0_.refs_1_.req_ref
  1.5 39.9 %shard_map.100 = (f32[432,8,128]{2,1,0:T(8,128)}, s32[7,16,128]{2,1,0:T(8,128)}) custom-call(s32[16,128]{1,0:T(8,128)} %pad.4.refs_0_.refs_1_.req_ref, s32[16,128]{1,0:T(8,128)} %pad.4.refs_0_.refs_1_.req_ref, s32[1600]{0:T(1024)} %counts_ref.3, f32[3,1600,128]{2,1,0:T(8,128)} %bitcast.8, f32[3,1600,128]{2,1,0:T(8,128)} %bitcast.9, f32[1600,128]{1,0:T(8,128)} %refs_5_.1, ...), custom_call_target="tpu_custom_call" | custom-call | tf_op jit(solution)/shard_map/pallas_call | solution.py:516
  41.4 24.1 %density.1 = (f32[16,1,128]{2,1,0:T(1,128)}, f32[432,1,128]{2,1,0:T(1,128)}, f32[9,1,128]{2,1,0:T(1,128)}, f32[512,8,128]{2,1,0:T(8,128)}, s32[432,128]{1,0:T(8,128)}, /*index=5*/s32[32,128]{1,0:T(8,128)}, s32[640]{0:T(1024)}) custom-call(s32[16,128]{1,0:T(8,128)} %pad.4.refs_0_.refs_1_.req_ref, s32[7,16,128]{2,1,0:T(8,128)} %get-tuple-element.14.lists_ref, ...), custom_call_target="tpu_custom_call" | custom-call | tf_op jit(solution)/shard_map/density/pallas_call | solution.py:472
  65.5 14.4 %shard_map.101 = f32[432,1,128]{2,1,0:T(1,128)} custom-call(f32[432,1,128]{2,1,0:T(1,128)} %get-tuple-element.18.refs_0_, f32[9,1,128]{2,1,0:T(1,128)} %get-tuple-element.19.refs_1_), custom_call_target="tpu_custom_call" | custom-call | tf_op jit(solution)/shard_map/pallas_call | solution.py:539
  79.9 26.4 %force.1 = f32[5,16,128]{2,1,0:T(8,128)} custom-call(s32[1600]{0:T(1024)} %counts_ref.3, s32[16]{0:T(128)} %active_ref.3, s32[32,128]{1,0:T(8,128)} %get-tuple-element.16.offs_ref, s32[640]{0:T(1024)} %get-tuple-element.17.jobs_ref, f32[3456,128]{1,0:T(8,128)} %bitcast.7, f32[432,128]{1,0:T(8,128)} %bitcast.10, f32[512,8,128]{2,1,0:T(8,128)} %get-tuple-element.20.pack_ref, ...), custom_call_target="tpu_custom_call" | custom-call | tf_op jit(solution)/shard_map/force/pallas_call | solution.py:492

commit v4 on v3

--- a/solution.py
+++ b/solution.py
@@ -15,18 +15,32 @@
 LIMIT = 56 * 1024 * 1024
 
 STEPS = (16, 4, 20, 1, 5, 17, 21)
-WIDE = ((0, 6), (0, 7), (1, 2), (1, 5), (2, 8))
-EDGE = ((6, 8), (5, 6), (5, 7), (4, 2), (4, 5), (3, 0), (3, 1), (3, 3), (3, 4))
-HOME = (0, 1, 3, 4)
+BLOCKS = (0, 1, 3, 4, 2, 5, 6, 7, 8)
+WIDE = ((1, 4), (1, 5), (0, 6), (0, 7), (2, 8))
+EDGE = ((6, 8), (5, 6), (5, 7), (4, 4), (4, 5), (3, 0), (3, 1), (3, 2), (3, 3))
+HOME = (0, 1, 2, 3)
 SPAN = 47
+NEAR_SLOTS = 12
+FAR_SLOTS = 15
+OWN = 10
+SPARE = 15
+
+
+def near_slot(place):
+    return place + 3 * (place // 6)
+
+
+def far_slot(place):
+    return place + jnp.where(place < 3, 6, 12)
 
 
 def shift_tiles():
     tiles = np.zeros((27, 8, 128), np.float32)
-    for slot in range(27):
-        tiles[slot, 1] = slot // 9 - 1
-        tiles[slot, 2] = slot // 3 % 3 - 1
-        tiles[slot, 3] = slot % 3 - 1
+    for place in range(27):
+        slot = 3 * BLOCKS[place // 3] + place % 3
+        tiles[place, 1] = slot // 9 - 1
+        tiles[place, 2] = slot // 3 % 3 - 1
+        tiles[place, 3] = slot % 3 - 1
     return tiles
 
 
@@ -40,7 +54,7 @@
 
 def gather_kernel(
     devices, req_ref, req_send, counts_ref, pos_ref, vel_ref, mass_ref, smooth_ref,
-    near_ref, asked_ref, send_ref, edge_ref, lists_ref, ask_out, ask_in, send_sem, recv_sem, local_sem,
+    near_ref, asked_ref, x_ref, y_ref, xy_ref, far_edge_ref, edge_ref, lists_ref, ask_out, ask_in, send_sem, recv_sem, local_sem,
 ):
     me = lax.axis_index("dom")
     cells = mass_ref.shape[0]
@@ -83,38 +97,31 @@
     def requester(place):
         return (lax.rem(me + devices - STEPS[place], devices),)
 
-    def serve(group, start):
+    def serve(dst, group):
         def step(entry, carry):
-            for place, block in group:
-                fill(send_ref, block * 48 + entry, lists_ref[place, block, entry])
+            for number, (place, block) in enumerate(group):
+                fill(dst, number * SPAN + entry, lists_ref[place, block, entry])
             return carry
 
         lax.fori_loop(0, SPAN, step, 0)
-        for number, (place, block) in enumerate(group):
-            rows = pl.ds(block * 48, SPAN)
-            copy = pltpu.make_async_remote_copy(
-                send_ref.at[rows], near_ref.at[rows], send_sem.at[start + number], recv_sem.at[start + number],
-                device_id=requester(place), device_id_type=MESH,
-            )
-            copy.start()
-            copies.append(copy)
-
-    hear(0)
-    serve(WIDE[0:2], 0)
-    hear(1)
-    serve(WIDE[2:4], 2)
-    hear(2)
-    serve(WIDE[4:5], 4)
+
     for place in (3, 4, 5, 6):
         hear(place)
     for number, (place, block) in enumerate(EDGE):
         fill(edge_ref, number, lists_ref[place, block, SPAN])
+        target = near_ref.at[block * 48 + SPAN] if block < 4 else far_edge_ref.at[block - 4]
         copy = pltpu.make_async_remote_copy(
-            edge_ref.at[number], near_ref.at[block * 48 + SPAN], send_sem.at[5 + number], recv_sem.at[5 + number],
+            edge_ref.at[number], target, send_sem.at[number], recv_sem.at[number],
             device_id=requester(place), device_id_type=MESH,
         )
         copy.start()
         copies.append(copy)
+    hear(0)
+    serve(x_ref, WIDE[2:4])
+    hear(1)
+    serve(y_ref, WIDE[0:2])
+    hear(2)
+    serve(xy_ref, WIDE[4:5])
     for copy in copies:
         copy.wait()
     for ask in asks:
@@ -142,7 +149,7 @@
     return jnp.sum(jnp.where(eye(), total, 0.0), axis=0, keepdims=True)
 
 
-def list_jobs(offs_ref, counts_ref, active_ref, first, order_ref, jobs_ref):
+def list_jobs(sources, counts_ref, active_ref, first, order_ref, jobs_ref):
     place = jnp.int32(0)
     ends = []
     for low, high in ((0, 80), (80, 96), (96, 112), (112, 128)):
@@ -157,19 +164,22 @@
     for number, end in enumerate(ends):
         def one_row(place, count):
             row = order_ref[place]
-            chunks = (offs_ref[27, row] + 127) // 128
-            for chunk in range(10):
-                jobs_ref[count + chunk] = row * 32 + chunk
-
-            def one_chunk(chunk, carry):
-                jobs_ref[count + chunk] = row * 32 + chunk
-                return carry
-
-            lax.fori_loop(10, chunks, one_chunk, 0)
-            return count + chunks
+            for offs_ref, slots, base in sources:
+                chunks = (offs_ref[slots, row] + 127) // 128
+                code = row * 16 + base
+                for chunk in range(6):
+                    jobs_ref[count + chunk] = code + chunk
+
+                def one_chunk(chunk, carry):
+                    jobs_ref[count + chunk] = code + chunk
+                    return carry
+
+                lax.fori_loop(6, chunks, one_chunk, 0)
+                count = count + chunks
+            return count
 
         count = lax.fori_loop(begin, end, one_row, count)
-        jobs_ref[count] = 31
+        jobs_ref[count] = SPARE
         count = count + count % 2
         jobs_ref[513 + number] = count
         begin = end
@@ -185,7 +195,7 @@
         lax.fori_loop(jobs_ref[512 + number] // 2, jobs_ref[513 + number] // 2, two, 0)
 
 
-def pack_rows(offs_ref, row, get, put, width):
+def pack_rows(offs_ref, slots, row, get, put, width):
     lane = lax.broadcasted_iota(jnp.int32, (width, 128), 1)
 
     def slot_step(slot, held):
@@ -196,95 +206,96 @@
         put(begin // 128, merged)
         return jnp.where(jnp.broadcast_to(end // 128 > begin // 128, (width, 128)), turned, merged)
 
-    return lax.fori_loop(0, 27, slot_step, get(0), unroll=27)
-
-
-def density_kernel(
-    req_ref, lists_ref, counts_ref, active_ref, near_ref, shift_ref, energy_ref, old_ref,
-    fresh_ref, mine_ref, edge_ref, pack_ref, index_ref, offs_out_ref, jobs_ref,
-    table_ref, mask_ref, offs_ref, order_ref, x_ref, y_ref, z_ref, inv_ref, sum_ref, local_sem,
+    return lax.fori_loop(0, slots, slot_step, get(0), unroll=slots)
+
+
+def pack_part(
+    slots, slot_of, near_ref, own_ref, own_place, shift_ref, pack_ref, index_ref, offs_out_ref, mask_ref, offs_ref, local_sem,
+    meanwhile,
 ):
-    cells = old_ref.shape[0]
-    first = lax.axis_index("dom") * cells
-    lane = lax.broadcasted_iota(jnp.int32, (1, 128), 1)
     lanes = lax.broadcasted_iota(jnp.int32, (16, 128), 1)
     on_diagonal = lax.broadcasted_iota(jnp.int32, (16, 128), 0) == lanes
-
     lows, highs = [], []
     for axis in range(3):
-        own = rows_of(near_ref, 13, 1 + axis)
+        own = rows_of(own_ref, own_place, 1 + axis)
         lows.append(jnp.min(own, axis=1, keepdims=True))
         highs.append(jnp.max(own, axis=1, keepdims=True))
-    widest = jnp.min(rows_of(near_ref, 13, 7), axis=1, keepdims=True)
-
-    def mask_step(slot, carry):
+    widest = jnp.min(rows_of(own_ref, own_place, 7), axis=1, keepdims=True)
+
+    def mask_step(place, carry):
+        slot = slot_of(place)
         away = jnp.zeros((16, 128), jnp.float32)
         for axis, step in enumerate((slot // 9, slot // 3 % 3, slot % 3)):
-            at = rows_of(near_ref, slot, 1 + axis) + (step - 1).astype(jnp.float32)
+            at = rows_of(near_ref, place, 1 + axis) + (step - 1).astype(jnp.float32)
             out = jnp.maximum(jnp.maximum(lows[axis] - at, at - highs[axis]), 0.0)
             away = away + out * out
-        reach = jnp.minimum(rows_of(near_ref, slot, 7), widest)
-        chosen = (rows_of(near_ref, slot, 0) > 0.0) & (away * (reach * reach) <= 1.0001)
-        mask_ref[pl.ds(slot * 16, 16), :] = jnp.where(chosen, 1.0, 0.0)
-        return carry
-
-    lax.fori_loop(0, 27, mask_step, 0, unroll=27)
+        reach = jnp.minimum(rows_of(near_ref, place, 7), widest)
+        chosen = (rows_of(near_ref, place, 0) > 0.0) & (away * (reach * reach) <= 1.0001)
+        mask_ref[pl.ds(place * 16, 16), :] = jnp.where(chosen, 1.0, 0.0)
+        return carry
+
+    lax.fori_loop(0, slots, mask_step, 0, unroll=slots)
     high = lax.broadcasted_iota(jnp.int32, (128, 256), 0)
     wide = lax.broadcasted_iota(jnp.int32, (128, 256), 1)
     counter = jnp.where((wide >= 128) | (high <= wide), 1.0, 0.0).astype(jnp.bfloat16)
 
-    def rank_step(slot, begin):
-        chosen = mask_ref[pl.ds(slot * 16, 16), :].astype(jnp.bfloat16)
+    def rank_step(place, begin):
+        chosen = mask_ref[pl.ds(place * 16, 16), :].astype(jnp.bfloat16)
         ranks = jnp.dot(chosen, counter, preferred_element_type=jnp.float32).astype(jnp.int32)
         order = ranks[:, 0:128]
         wanted = (lanes - begin) & 127
         index = jnp.zeros((16, 128), jnp.int32)
         for step in (64, 32, 16, 8, 4, 2, 1):
             index = index + jnp.where(pick(order, index + (step - 1)) <= wanted, step, 0)
-        index_ref[pl.ds(slot * 16, 16), :] = index
-        offs_out_ref[pl.ds(slot, 1), :] = jnp.sum(jnp.where(on_diagonal, begin, 0), axis=0, keepdims=True)
+        index_ref[pl.ds(place * 16, 16), :] = index
+        offs_out_ref[pl.ds(place, 1), :] = jnp.sum(jnp.where(on_diagonal, begin, 0), axis=0, keepdims=True)
         return begin + ranks[:, 128:256]
 
-    total = lax.fori_loop(0, 27, rank_step, jnp.zeros((16, 128), jnp.int32), unroll=27)
-    offs_out_ref[27:28, :] = jnp.sum(jnp.where(on_diagonal, total, 0), axis=0, keepdims=True)
-    offs_out_ref[28:32, :] = jnp.zeros((4, 128), jnp.int32)
+    total = lax.fori_loop(0, slots, rank_step, jnp.zeros((16, 128), jnp.int32), unroll=slots)
+    for place in range(slots, 16):
+        offs_out_ref[place : place + 1, :] = jnp.sum(jnp.where(on_diagonal, total, 0), axis=0, keepdims=True)
     moved = pltpu.make_async_copy(offs_out_ref, offs_ref, local_sem)
     moved.start()
-    table_ref[...] = GAS * energy_ref[...] / old_ref[...]
-
+    meanwhile()
+    moved.wait()
+    deep = lax.broadcasted_iota(jnp.int32, (8, 128), 0)
+    wide = lax.broadcasted_iota(jnp.int32, (8, 128), 1)
+
+    def pack_step(row, carry):
+        def get(place):
+            tile = near_ref[pl.ds((place * 16 + row) * 8, 8), :] + shift_ref[place]
+            index = index_ref[pl.ds(place * 16 + row, 1), :]
+            return pick(tile, jnp.broadcast_to(index, (8, 128)))
+
+        def put(chunk, tile):
+            pack_ref[row * 16 + chunk] = tile
+
+        held = pack_rows(offs_ref, slots, row, get, put, 8)
+        total = offs_ref[slots, row]
+        put(total // 128, jnp.where((deep == 0) & (wide >= total % 128), 0.0, held))
+        put(SPARE, jnp.where(deep == 0, 0.0, held))
+        return carry
+
+    lax.fori_loop(0, 16, pack_step, 0)
+
+
+def own_columns(own_ref, own_place, pairs, sums):
     def own_step(row, carry):
-        own = near_ref[pl.ds(1664 + row * 8, 8), :]
-        for ref, feature in ((x_ref, 1), (y_ref, 2), (z_ref, 3), (inv_ref, 7)):
-            ref[pl.ds(row * 128, 128), :] = column(own[feature : feature + 1])
-        sum_ref[pl.ds(row * 128, 128), :] = jnp.zeros((128, 128), jnp.float32)
+        own = own_ref[pl.ds(own_place * 128 + row * 8, 8), :]
+        at = pl.ds(row * 128, 128)
+        for ref, feature in pairs:
+            ref[at, :] = column(own[feature : feature + 1])
+        for ref in sums:
+            ref[at, :] = jnp.zeros((128, 128), jnp.float32)
         return carry
 
     lax.fori_loop(0, 16, own_step, 0)
-    moved.wait()
-
-    def pack_step(row, carry):
-        def get(slot):
-            tile = near_ref[pl.ds((slot * 16 + row) * 8, 8), :] + shift_ref[slot]
-            index = index_ref[pl.ds(slot * 16 + row, 1), :]
-            return pick(tile, jnp.broadcast_to(index, (8, 128)))
-
-        def put(chunk, tile):
-            pack_ref[row * 32 + chunk] = tile
-
-        held = pack_rows(offs_ref, row, get, put, 8)
-        total = offs_ref[27, row]
-        wide = lax.broadcasted_iota(jnp.int32, (8, 128), 1)
-        deep = lax.broadcasted_iota(jnp.int32, (8, 128), 0)
-        put(total // 128, jnp.where((deep == 0) & (wide >= total % 128), 0.0, held))
-        put(31, jnp.where(deep == 0, 0.0, held))
-        return carry
-
-    lax.fori_loop(0, 16, pack_step, 0)
-    list_jobs(offs_ref, counts_ref, active_ref, first, order_ref, jobs_ref)
-
+
+
+def sum_weights(jobs_ref, pack_ref, x_ref, y_ref, z_ref, inv_ref, sum_ref):
     def job_step(job, parts):
         code = jobs_ref[job]
-        row = code // 32
+        row = code // 16
         tile = pack_ref[code]
         mass, near_x, near_y, near_z = [jnp.broadcast_to(tile[f : f + 1], (8, 128)) for f in range(4)]
         for part in range(parts):
@@ -301,10 +312,68 @@
 
     run_jobs(jobs_ref, job_step)
 
+
+def near_kernel(
+    counts_ref, active_ref, near_ref, shift_ref,
+    part_ref, pack_ref, index_ref, offs_out_ref,
+    mask_ref, offs_ref, order_ref, jobs_ref, x_ref, y_ref, z_ref, inv_ref, sum_ref, local_sem,
+):
+    first = lax.axis_index("dom") * counts_ref.shape[0]
+
+    def meanwhile():
+        own_columns(near_ref, OWN, ((x_ref, 1), (y_ref, 2), (z_ref, 3), (inv_ref, 7)), (sum_ref,))
+
+    pack_part(
+        NEAR_SLOTS, near_slot, near_ref, near_ref, OWN, shift_ref, pack_ref, index_ref, offs_out_ref, mask_ref, offs_ref,
+        local_sem, meanwhile,
+    )
+    list_jobs(((offs_ref, NEAR_SLOTS, 0),), counts_ref, active_ref, first, order_ref, jobs_ref)
+    sum_weights(jobs_ref, pack_ref, x_ref, y_ref, z_ref, inv_ref, sum_ref)
+
     def end_step(row, carry):
-        own = near_ref[pl.ds(1664 + row * 8, 8), :]
-        inverse = own[7:8]
-        total = row_sums(sum_ref[pl.ds(row * 128, 128), :])
+        part_ref[row] = row_sums(sum_ref[pl.ds(row * 128, 128), :])
+        return carry
+
+    lax.fori_loop(0, 16, end_step, 0)
+
+
+def far_kernel(
+    req_ref, lists_ref, counts_ref, active_ref, near_offs_ref, near_ref, x_got_ref, y_got_ref, xy_got_ref, far_edge_ref,
+    shift_ref, energy_ref, old_ref, part_ref,
+    fresh_ref, mine_ref, edge_ref, pack_ref, index_ref, offs_out_ref, all_jobs_ref,
+    far_ref, own_ref, table_ref, mask_ref, offs_ref, order_ref, jobs_ref, x_ref, y_ref, z_ref, inv_ref, sum_ref,
+    local_sem, load_sem,
+):
+    cells = old_ref.shape[0]
+    first = lax.axis_index("dom") * cells
+    lane = lax.broadcasted_iota(jnp.int32, (1, 128), 1)
+    loads = [(near_ref.at[pl.ds(OWN * 128, 128)], own_ref)]
+    for number, (source, block) in enumerate(((y_got_ref, 0), (y_got_ref, 1), (x_got_ref, 0), (x_got_ref, 1), (xy_got_ref, 0))):
+        loads.append((source.at[pl.ds(block * SPAN * 8, SPAN * 8)], far_ref.at[pl.ds(number * 384, SPAN * 8)]))
+        loads.append((far_edge_ref.at[pl.ds(number * 8, 8)], far_ref.at[pl.ds(number * 384 + SPAN * 8, 8)]))
+    loads = [pltpu.make_async_copy(source, target, load_sem.at[number]) for number, (source, target) in enumerate(loads)]
+    for load in loads:
+        load.start()
+    table_ref[...] = GAS * energy_ref[...] / old_ref[...]
+    for load in loads:
+        load.wait()
+
+    def meanwhile():
+        own_columns(own_ref, 0, ((x_ref, 1), (y_ref, 2), (z_ref, 3), (inv_ref, 7)), (sum_ref,))
+
+    pack_part(
+        FAR_SLOTS, far_slot, far_ref, own_ref, 0, shift_ref, pack_ref, index_ref, offs_out_ref, mask_ref, offs_ref,
+        local_sem, meanwhile,
+    )
+    list_jobs(((offs_ref, FAR_SLOTS, 0),), counts_ref, active_ref, first, order_ref, jobs_ref)
+    list_jobs(
+        ((near_offs_ref, NEAR_SLOTS, 0), (offs_ref, FAR_SLOTS, 256)), counts_ref, active_ref, first, order_ref, all_jobs_ref
+    )
+    sum_weights(jobs_ref, pack_ref, x_ref, y_ref, z_ref, inv_ref, sum_ref)
+
+    def end_step(row, carry):
+        inverse = own_ref[pl.ds(row * 8 + 7, 1), :]
+        total = part_ref[row] + row_sums(sum_ref[pl.ds(row * 128, 128), :])
         cell = active_ref[row] - first
         fresh = jnp.where(
             lane < counts_ref[cell], total * (NORM * inverse * inverse * inverse), old_ref[pl.ds(cell, 1), :]
@@ -367,24 +436,26 @@
 
 
 def force_kernel(
-    counts_ref, active_ref, offs_ref, jobs_ref, all_ref, press_ref, pack_ref, index_ref, fresh_ref,
-    hydro_ref, near_ref, turned_ref, chunk_ref, x_ref, y_ref, z_ref, vx_ref, vy_ref, vz_ref, inv_ref, own_ref,
+    counts_ref, active_ref, near_offs_ref, far_offs_ref, jobs_ref, all_ref, near_pack_ref, far_pack_ref,
+    near_index_ref, far_index_ref, press_ref, fresh_ref,
+    hydro_ref, pack_ref, near_ref, turned_ref, chunk_ref, x_ref, y_ref, z_ref, vx_ref, vy_ref, vz_ref, inv_ref, own_ref,
     ax_ref, ay_ref, az_ref, rate_ref, own_sem,
 ):
     cells = counts_ref.shape[0]
     first = lax.axis_index("dom") * cells
     lane = lax.broadcasted_iota(jnp.int32, (1, 128), 1)
-
-    own_copy = pltpu.make_async_copy(all_ref.at[pl.ds(1664, 128)], near_ref, own_sem)
-    own_copy.start()
-
-    def turn_step(slot, carry):
-        at = pl.ds(slot * 16, 16)
-        turned_ref[at, :] = pick(press_ref[at, :], index_ref[at, :])
-        return carry
-
-    lax.fori_loop(0, 27, turn_step, 0, unroll=9)
-    own_copy.wait()
+    loads = [
+        pltpu.make_async_copy(all_ref.at[pl.ds(OWN * 128, 128)], near_ref, own_sem.at[0]),
+        pltpu.make_async_copy(near_pack_ref, pack_ref.at[pl.ds(0, 256)], own_sem.at[1]),
+        pltpu.make_async_copy(far_pack_ref, pack_ref.at[pl.ds(256, 256)], own_sem.at[2]),
+    ]
+    for load in loads:
+        load.start()
+    for index_ref, slots, begin in ((near_index_ref, NEAR_SLOTS, 0), (far_index_ref, FAR_SLOTS, NEAR_SLOTS)):
+        for place in range(slots):
+            at = pl.ds((begin + place) * 16, 16)
+            turned_ref[at, :] = pick(press_ref[at, :], index_ref[place * 16 : place * 16 + 16, :])
+    loads[0].wait()
 
     def own_step(row, carry):
         own = near_ref[pl.ds(row * 8, 8), :]
@@ -394,28 +465,33 @@
         for ref, value in (
             (x_ref, own[1:2]), (y_ref, own[2:3]), (z_ref, own[3:4]),
             (vx_ref, own[4:5]), (vy_ref, own[5:6]), (vz_ref, own[6:7]),
-            (inv_ref, inverse), (own_ref, (6.0 * NORM) * (inv_sq * inv_sq) * press_ref[pl.ds(208 + row, 1), :]),
+            (inv_ref, inverse), (own_ref, (6.0 * NORM) * (inv_sq * inv_sq) * press_ref[pl.ds(OWN * 16 + row, 1), :]),
         ):
             ref[at, :] = column(value)
         for ref in (ax_ref, ay_ref, az_ref, rate_ref):
             ref[at, :] = jnp.zeros((128, 128), jnp.float32)
 
-        def get(slot):
-            return turned_ref[pl.ds(slot * 16 + row, 1), :]
-
-        def put(chunk, value):
-            chunk_ref[pl.ds(row * 32 + chunk, 1), :] = value
-
-        held = pack_rows(offs_ref, row, get, put, 1)
-        put(offs_ref[27, row] // 128, held)
-        put(31, held)
+        for offs_ref, slots, begin, base in (
+            (near_offs_ref, NEAR_SLOTS, 0, 0), (far_offs_ref, FAR_SLOTS, NEAR_SLOTS, 256)
+        ):
+            def get(place):
+                return turned_ref[pl.ds((begin + place) * 16 + row, 1), :]
+
+            def put(chunk, value):
+                chunk_ref[pl.ds(base + row * 16 + chunk, 1), :] = value
+
+            held = pack_rows(offs_ref, slots, row, get, put, 1)
+            put(offs_ref[slots, row] // 128, held)
+            put(SPARE, held)
         return carry
 
     lax.fori_loop(0, 16, own_step, 0)
+    loads[1].wait()
+    loads[2].wait()
 
     def job_step(job, parts):
         place = jobs_ref[job]
-        row = place // 32
+        row = place % 256 // 16
         tile = pack_ref[place]
         near_inv = tile[7:8]
         near_sq = near_inv * near_inv
@@ -447,7 +523,7 @@
         own = near_ref[pl.ds(row * 8, 8), :]
         inverse = own[7:8]
         inv_sq = inverse * inverse
-        factor = (-6.0 * NORM) * (inv_sq * inv_sq) * press_ref[pl.ds(208 + row, 1), :]
+        factor = (-6.0 * NORM) * (inv_sq * inv_sq) * press_ref[pl.ds(OWN * 16 + row, 1), :]
         at = pl.ds(row * 128, 128)
         keep = lane < counts_ref[active_ref[row] - first]
         values = [fresh_ref[row]] + [row_sums(ref[at, :]) for ref in (ax_ref, ay_ref, az_ref)]
@@ -467,37 +543,58 @@
     return jax.ShapeDtypeStruct(shape, jnp.float32)
 
 
-def density_call(*args):
-    square = pltpu.VMEM((2048, 128), jnp.float32)
+def ints(*shape):
+    return jax.ShapeDtypeStruct(shape, jnp.int32)
+
+
+SQUARE = pltpu.VMEM((2048, 128), jnp.float32)
+
+
+def near_call(*args):
     return pl.pallas_call(
-        density_kernel,
+        near_kernel,
+        out_shape=(floats(16, 1, 128), floats(256, 8, 128), ints(192, 128), ints(16, 128)),
+        in_specs=specs("ssvv"),
+        out_specs=tuple(specs("vvvv")),
+        scratch_shapes=[
+            pltpu.VMEM((192, 128), jnp.float32), pltpu.SMEM((16, 128), jnp.int32),
+            pltpu.SMEM((32,), jnp.int32), pltpu.SMEM((640,), jnp.int32),
+        ] + [SQUARE] * 5 + [pltpu.SemaphoreType.DMA],
+        compiler_params=pltpu.CompilerParams(vmem_limit_bytes=LIMIT),
+        cost_estimate=pl.CostEstimate(flops=100_000_000, bytes_accessed=45_000_000, transcendentals=0),
+        name="near_density",
+    )(*args)
+
+
+def far_call(*args):
+    return pl.pallas_call(
+        far_kernel,
         out_shape=(
-            floats(16, 1, 128), floats(432, 1, 128), floats(9, 1, 128), floats(512, 8, 128),
-            jax.ShapeDtypeStruct((432, 128), jnp.int32), jax.ShapeDtypeStruct((32, 128), jnp.int32),
-            jax.ShapeDtypeStruct((640,), jnp.int32),
+            floats(16, 1, 128), floats(432, 1, 128), floats(9, 1, 128), floats(256, 8, 128),
+            ints(240, 128), ints(16, 128), ints(640),
         ),
-        in_specs=specs("ssssvvvv"),
+        in_specs=specs("sssss") + [pl.BlockSpec(memory_space=pl.ANY)] * 5 + specs("vvvv"),
         out_specs=tuple(specs("vvvvvvs")),
         scratch_shapes=[
-            pltpu.VMEM((1600, 128), jnp.float32), pltpu.VMEM((432, 128), jnp.float32),
-            pltpu.SMEM((32, 128), jnp.int32), pltpu.SMEM((32,), jnp.int32),
-        ] + [square] * 5 + [pltpu.SemaphoreType.DMA],
+            pltpu.VMEM((1920, 128), jnp.float32), pltpu.VMEM((128, 128), jnp.float32),
+            pltpu.VMEM((1600, 128), jnp.float32), pltpu.VMEM((240, 128), jnp.float32),
+            pltpu.SMEM((16, 128), jnp.int32), pltpu.SMEM((32,), jnp.int32), pltpu.SMEM((640,), jnp.int32),
+        ] + [SQUARE] * 5 + [pltpu.SemaphoreType.DMA, pltpu.SemaphoreType.DMA((11,))],
         compiler_params=pltpu.CompilerParams(vmem_limit_bytes=LIMIT),
-        name="density",
+        name="far_density",
     )(*args)
 
 
 def force_call(*args):
-    square = pltpu.VMEM((2048, 128), jnp.float32)
     return pl.pallas_call(
         force_kernel,
         out_shape=floats(5, 16, 128),
-        in_specs=specs("ssss") + [pl.BlockSpec(memory_space=pl.ANY)] + specs("vvvv"),
+        in_specs=specs("sssss") + [pl.BlockSpec(memory_space=pl.ANY)] * 3 + specs("vvvv"),
         out_specs=specs("v")[0],
         scratch_shapes=[
-            pltpu.VMEM((128, 128), jnp.float32), pltpu.VMEM((432, 128), jnp.float32),
-            pltpu.VMEM((512, 128), jnp.float32),
-        ] + [square] * 12 + [pltpu.SemaphoreType.DMA],
+            pltpu.VMEM((512, 8, 128), jnp.float32), pltpu.VMEM((128, 128), jnp.float32),
+            pltpu.VMEM((432, 128), jnp.float32), pltpu.VMEM((512, 128), jnp.float32),
+        ] + [SQUARE] * 12 + [pltpu.SemaphoreType.DMA((3,))],
         compiler_params=pltpu.CompilerParams(vmem_limit_bytes=LIMIT),
         name="force",
     )(*args)
@@ -509,31 +606,43 @@
     smem = pl.BlockSpec(memory_space=pltpu.SMEM)
     pos = jnp.transpose(positions, (1, 0, 2))
     vel = jnp.transpose(velocity, (1, 0, 2))
-    requests = jnp.pad(neighbours.T.reshape(9, 48), ((0, 7), (0, 80)))
-    shifts = jnp.asarray(shift_tiles())
+    blocks = neighbours.T.reshape(9, 48)
+    requests = jnp.pad(
+        jnp.concatenate([blocks[0:2], blocks[3:5], blocks[2:3], blocks[5:9]], axis=0), ((0, 7), (0, 80))
+    )
+    shifts = shift_tiles()
     f32 = jnp.float32
 
-    near, asked = pl.pallas_call(
+    near, asked, for_x, for_y, for_xy, far_edge = pl.pallas_call(
         lambda *refs: gather_kernel(devices, *refs),
-        out_shape=(jax.ShapeDtypeStruct((432, 8, 128), f32), jax.ShapeDtypeStruct((7, 16, 128), jnp.int32)),
+        out_shape=(
+            floats(192, 8, 128), ints(7, 16, 128), floats(94, 8, 128), floats(94, 8, 128), floats(47, 8, 128), floats(5, 8, 128)
+        ),
         in_specs=[smem, vmem, smem, vmem, vmem, vmem, vmem],
-        out_specs=(vmem, vmem),
+        out_specs=(vmem,) * 6,
         scratch_shapes=[
-            pltpu.VMEM((432, 8, 128), f32),
             pltpu.VMEM((9, 8, 128), f32),
             pltpu.SMEM((7, 16, 128), jnp.int32),
             pltpu.SemaphoreType.DMA((7,)),
             pltpu.SemaphoreType.DMA((7,)),
-            pltpu.SemaphoreType.DMA((14,)),
-            pltpu.SemaphoreType.DMA((14,)),
+            pltpu.SemaphoreType.DMA((9,)),
+            pltpu.SemaphoreType.DMA((9,)),
             pltpu.SemaphoreType.DMA((7,)),
         ],
         compiler_params=pltpu.CompilerParams(collective_id=0, has_side_effects=True, vmem_limit_bytes=LIMIT),
+        name="gather",
     )(requests, requests, counts, pos, vel, mass, smoothing)
 
-    flat = near.reshape(3456, 128)
-    fresh, mine, edge, packed, index, offs, jobs = density_call(
-        requests, asked, counts, active, flat, shifts, energy, density_old
+    def fetched(value, steps):
+        pairs = [(source, (source - steps) % devices) for source in range(devices)]
+        return lax.ppermute(value, "dom", pairs).reshape(-1, 128)
+
+    x_got, y_got, xy_got = fetched(for_x, 16), fetched(for_y, 4), fetched(for_xy, 20)
+    flat = near.reshape(1536, 128)
+    part, near_pack, near_index, near_offs = near_call(counts, active, flat, jnp.asarray(shifts[:12]))
+    fresh, mine, edge, far_pack, far_index, far_offs, jobs = far_call(
+        requests, asked, counts, active, near_offs, flat, x_got, y_got, xy_got, far_edge.reshape(40, 128),
+        jnp.asarray(shifts[12:]), energy, density_old, part,
     )
 
     press = pl.pallas_call(
@@ -547,9 +656,13 @@
             pltpu.SemaphoreType.DMA((4,)),
         ],
         compiler_params=pltpu.CompilerParams(collective_id=1, has_side_effects=True, vmem_limit_bytes=LIMIT),
+        name="exchange",
     )(mine, edge)
 
-    hydro = force_call(counts, active, offs, jobs, flat, press.reshape(432, 128), packed, index, fresh)
+    hydro = force_call(
+        counts, active, near_offs, far_offs, jobs, flat, near_pack, far_pack, near_index, far_index,
+        press.reshape(432, 128), fresh,
+    )
     return jnp.transpose(hydro, (1, 0, 2))
 
 

time: 107 us -> 113 us (1.056)
  Pallas kernels: 105 us -> 96.6 us
  starting transfers between devices: 0 us -> 5.46 us
  waiting for transfers between devices: 0 us -> 4.96 us
  local copies, waits for them, and re-layouts: 1.46 us -> 4.39 us
    pallas_call x2 -> x3, Pallas kernels: 64 us -> 56.8 us  [the longest x1 24.4 us: shards(): pl.pallas_call(lambda *refs: gather_kernel(devices, *refs), out_shape=(fl...]
    ppermute x0 -> x3, starting transfers between devices: none -> 5.46 us  [fetched(): return lax.ppermute(value, 'dom', pairs).reshape(-1, 128)]
    ppermute x0 -> x3, waiting for transfers between devices: none -> 4.96 us  [fetched(): return lax.ppermute(value, 'dom', pairs).reshape(-1, 128)]
    slice x0 -> x11, local copies, waits for them, and re-layouts: none -> 3.02 us  [the longest x3 1 us: shards(): blocks[0:2]]
    pallas_call x1, Pallas kernels: 26.4 us -> 25.2 us  [force_call(): pl.pallas_call(force_kernel, out_shape=floats(5, 16, 128), in_specs=specs...]
  transfers between devices with their start and end apart: 0 -> 3, of which waited for: 0 -> 1; matrix products, arithmetic and copies ran while one was open for 0% -> 0% of each run, Pallas kernels for 0% -> 12%
where the time goes in v4:
time: 113 us; the launch traced here: 111 us
  Pallas kernels  96.6 us (85%)
  starting transfers between devices  5.46 us (5%)
  waiting for transfers between devices  4.96 us (4%)
  local copies, waits for them, and re-layouts  4.39 us (4%)
    pallas_call x1, Pallas kernels, force_call(): pl.pallas_call(force_kernel, out_shape=floats(5, 16, 128), in_specs=specs...  25.2 us
    pallas_call x1, Pallas kernels, shards(): pl.pallas_call(lambda *refs: gather_kernel(devices, *refs), out_shape=(fl...  24.4 us
    pallas_call x1, Pallas kernels, far_call(): pl.pallas_call(far_kernel, out_shape=(floats(16, 1, 128), floats(432, 1,...  19 us
    pallas_call x1, Pallas kernels, shards(): pl.pallas_call(lambda *refs: pass_kernel(devices, *refs), out_shape=jax.S...  14.6 us
    pallas_call x1, Pallas kernels, near_call(): pl.pallas_call(near_kernel, out_shape=(floats(16, 1, 128), floats(256, 8,...  13.4 us
    ppermute x3, starting transfers between devices, fetched(): return lax.ppermute(value, 'dom', pairs).reshape(-1, 128)  5.46 us
    ppermute x3, waiting for transfers between devices, fetched(): return lax.ppermute(value, 'dom', pairs).reshape(-1, 128)  4.96 us
  transfers between devices with their start and end apart: 3, of which 1 were waited for; matrix products, arithmetic and copies ran while one was open for 0% of the time, Pallas kernels for 12%

profile of v4, /device:TPU:1, one launch (start us, length us, event | category | flops | bytes accessed | tf_op | source)
XLA Modules:
  0.0 111.5 jit_solution(15506911349783378466)
XLA Ops:
  0.0 0.8 slice.34
  0.8 0.8 slice.35
  1.5 0.8 fusion
  2.4 0.1 copy.14
  2.5 0.1 slice.29
  2.5 0.1 copy.15
  2.6 0.1 slice.31
  2.7 0.1 copy.12
  2.8 0.1 slice.25
  2.9 0.1 copy.13
  2.9 0.1 slice.27
  3.1 0.6 pad.4.refs_0_.refs_1_.req_ref
  3.7 24.4 %gather.1 = (f32[192,8,128]{2,1,0:T(8,128)}, s32[7,16,128]{2,1,0:T(8,128)}, f32[94,8,128]{2,1,0:T(8,128)}, f32[94,8,128]{2,1,0:T(8,128)}, f32[47,8,128]{2,1,0:T(8,128)}, /*index=5*/f32[5,8,128]{2,1,0:T(8,128)}) custom-call(s32[16,128]{1,0:T(8,128)} %pad.4.refs_0_.refs_1_.req_ref, s32[16,128]{1,0:T(8,128)} %pad.4.refs_0_.refs_1_.req_ref, s32[1600]{0:T(1024)} %counts_ref.5, ...), custom_call_target="tpu_custom_call" | custom-call | tf_op jit(solution)/shard_map/gather/pallas_call | solution.py:616
  28.0 2.7 %collective-permute-start = (f32[94,8,128]{2,1,0:T(8,128)}, f32[94,8,128]{2,1,0:T(8,128)S(1)}, u32[]{:S(2)}, u32[]{:S(2)}) collective-permute-start(f32[94,8,128]{2,1,0:T(8,128)} %get-tuple-element.25), channel_id=1, source_target_pairs={{0,112},{1,113},{2,114},{3,115},{4,116},{5,117},{6,118},{7,119},{8... | collective-permute-start | bytes 1155080 | tf_op jit(solution)/shard_map/ppermute | solution.py:638
  30.7 2.4 %collective-permute-start.1 = (f32[94,8,128]{2,1,0:T(8,128)}, f32[94,8,128]{2,1,0:T(8,128)S(1)}, u32[]{:S(2)}, u32[]{:S(2)}) collective-permute-start(f32[94,8,128]{2,1,0:T(8,128)} %get-tuple-element.26), channel_id=1, source_target_pairs={{0,124},{1,125},{2,126},{3,127},{4,0},{5,1},{6,2},{7,3},{8,4},{9,5... | collective-permute-start | bytes 1155080 | tf_op jit(solution)/shard_map/ppermute | solution.py:638
  33.1 0.4 collective-permute-start.2
  33.5 13.4 %near_density.1 = (f32[16,1,128]{2,1,0:T(1,128)}, f32[256,8,128]{2,1,0:T(8,128)}, s32[192,128]{1,0:T(8,128)}, s32[16,128]{1,0:T(8,128)}) custom-call(s32[1600]{0:T(1024)} %counts_ref.5, s32[16]{0:T(128)} %active_ref.5, f32[1536,128]{1,0:T(8,128)} %bitcast.10, f32[12,8,128]{2,1,0:T(8,128)} %constant.6.clone.shift_ref), custom_call_target="tpu_custom_call" | custom-call | flops 100000000 | bytes 45000000 | tf_op jit(solution)/shard_map/near_density/pallas_call | solution.py:554
  46.9 0.0 collective-permute-done.2
  47.0 0.0 copy-start.2
  47.0 0.0 collective-permute-done
  47.0 0.0 copy-start
  47.0 5.0 %collective-permute-done.1 = f32[94,8,128]{2,1,0:T(8,128)S(1)} collective-permute-done((f32[94,8,128]{2,1,0:T(8,128)}, f32[94,8,128]{2,1,0:T(8,128)S(1)}, u32[]{:S(2)}, u32[]{:S(2)}) %collective-permute-start.1) | collective-permute-done | bytes 385056 | tf_op jit(solution)/shard_map/ppermute | solution.py:638
  51.9 0.0 copy-start.1
  51.9 0.0 copy-done.2
  51.9 0.0 copy-done
  51.9 0.7 copy-done.1
  52.7 19.0 %far_density.1 = (f32[16,1,128]{2,1,0:T(1,128)}, f32[432,1,128]{2,1,0:T(1,128)}, f32[9,1,128]{2,1,0:T(1,128)}, f32[256,8,128]{2,1,0:T(8,128)}, s32[240,128]{1,0:...) custom-call(s32[16,128]{1,0:T(8,128)} %pad.4.refs_0_.refs_1_.req_ref, s32[7,16,128]{2,1,0:T(8,128)} %get-tuple-element.24.lists_ref, ...), custom_call_target="tpu_custom_call" | custom-call | tf_op jit(solution)/shard_map/far_density/pallas_call | solution.py:570
  71.7 14.6 %exchange.1 = f32[432,1,128]{2,1,0:T(1,128)} custom-call(f32[432,1,128]{2,1,0:T(1,128)} %get-tuple-element.36.refs_0_, f32[9,1,128]{2,1,0:T(1,128)} %get-tuple-element.37.refs_1_), custom_call_target="tpu_custom_call" | custom-call | tf_op jit(solution)/shard_map/exchange/pallas_call | solution.py:648
  86.3 25.2 %force.1 = f32[5,16,128]{2,1,0:T(8,128)} custom-call(s32[1600]{0:T(1024)} %counts_ref.5, s32[16]{0:T(128)} %active_ref.5, s32[16,128]{1,0:T(8,128)} %get-tuple-element.23.near_offs_ref, s32[16,128]{1,0:T(8,128)} %get-tuple-element.30.far_offs_ref, s32[640]{0:T(1024)} %get-tuple-element.31.jobs_ref, f32[1536,128]{1,0:T(8,128)} %bitcast.12, ...), custom_call_target="tpu_custom_call" | custom-call | tf_op jit(solution)/shard_map/force/pallas_call | solution.py:589
  (1 shorter events, 0.0 us)
Async XLA Ops:
  28.0 18.9 %collective-permute-start = (f32[94,8,128]{2,1,0:T(8,128)}, f32[94,8,128]{2,1,0:T(8,128)S(1)}, u32[]{:S(2)}, u32[]{:S(2)}) collective-permute-start(f32[94,8,128]{2,1,0:T(8,128)} %get-tuple-element.25), channel_id=1, source_target_pairs={{0,112},{1,113},{2,114},{3,115},{4,116},{5,117},{6,118},{7,119},{8... | collective-permute-start | bytes 1155080 | tf_op jit(solution)/shard_map/ppermute | solution.py:638
  30.7 21.2 %collective-permute-start.1 = (f32[94,8,128]{2,1,0:T(8,128)}, f32[94,8,128]{2,1,0:T(8,128)S(1)}, u32[]{:S(2)}, u32[]{:S(2)}) collective-permute-start(f32[94,8,128]{2,1,0:T(8,128)} %get-tuple-element.26), channel_id=1, source_target_pairs={{0,124},{1,125},{2,126},{3,127},{4,0},{5,1},{6,2},{7,3},{8,4},{9,5... | collective-permute-start | bytes 1155080 | tf_op jit(solution)/shard_map/ppermute | solution.py:638
  33.1 13.8 %collective-permute-start.2 = (f32[47,8,128]{2,1,0:T(8,128)}, f32[47,8,128]{2,1,0:T(8,128)S(1)}, u32[]{:S(2)}, u32[]{:S(2)}) collective-permute-start(f32[47,8,128]{2,1,0:T(8,128)} %get-tuple-element.27), channel_id=1, source_target_pairs={{0,108},{1,109},{2,110},{3,111},{4,112},{5,113},{6,114},{7,115},{8... | collective-permute-start | bytes 577544 | tf_op jit(solution)/shard_map/ppermute | solution.py:638
  47.0 5.0 %copy-start.2 = (f32[47,8,128]{2,1,0:T(8,128)}, f32[47,8,128]{2,1,0:T(8,128)S(1)}, u32[]{:S(2)}) copy-start(f32[47,8,128]{2,1,0:T(8,128)S(1)} %collective-permute-done.2) | copy-start | bytes 577540
  47.0 5.0 %copy-start = (f32[94,8,128]{2,1,0:T(8,128)}, f32[94,8,128]{2,1,0:T(8,128)S(1)}, u32[]{:S(2)}) copy-start(f32[94,8,128]{2,1,0:T(8,128)S(1)} %collective-permute-done) | copy-start | bytes 1155076
  51.9 0.8 copy-start.1

commit v5 on v3

--- a/solution.py
+++ b/solution.py
@@ -19,6 +19,7 @@
 EDGE = ((6, 8), (5, 6), (5, 7), (4, 2), (4, 5), (3, 0), (3, 1), (3, 3), (3, 4))
 HOME = (0, 1, 3, 4)
 SPAN = 47
+COLUMNS = (1, 2, 3, 7, 4, 5, 6)
 
 
 def shift_tiles():
@@ -39,11 +40,20 @@
 
 
 def gather_kernel(
-    devices, req_ref, req_send, counts_ref, pos_ref, vel_ref, mass_ref, smooth_ref,
-    near_ref, asked_ref, send_ref, edge_ref, lists_ref, ask_out, ask_in, send_sem, recv_sem, local_sem,
+    devices, req_ref, req_send, counts_ref, pos_all, vel_all, mass_all, smooth_all,
+    near_ref, asked_ref, columns_ref, pos_ref, vel_ref, mass_ref, smooth_ref, square_ref, send_ref, edge_ref, lists_ref,
+    ask_out, ask_in, send_sem, recv_sem, local_sem, table_sem, column_sem,
 ):
     me = lax.axis_index("dom")
     cells = mass_ref.shape[0]
+    tables = [
+        pltpu.make_async_copy(source, target, table_sem.at[number])
+        for number, (source, target) in enumerate(
+            ((pos_all, pos_ref), (vel_all, vel_ref), (mass_all, mass_ref), (smooth_all, smooth_ref))
+        )
+    ]
+    for table in tables:
+        table.start()
     first = me * cells
     lane = lax.broadcasted_iota(jnp.int32, (1, 128), 1)
 
@@ -66,6 +76,9 @@
         ask.start()
         asks.append(ask)
 
+    for table in tables:
+        table.wait()
+
     def home_step(entry, carry):
         for block in HOME:
             fill(near_ref, block * 48 + entry, req_ref[block, entry])
@@ -73,12 +86,11 @@
 
     lax.fori_loop(0, SPAN, home_step, 0)
     copies = []
-
-    def hear(place):
-        asks[place].wait_recv()
-        listed = pltpu.make_async_copy(asked_ref.at[place], lists_ref.at[place], local_sem.at[place])
-        listed.start()
-        listed.wait()
+    lists = []
+    for place, ask in enumerate(asks):
+        ask.wait_recv()
+        lists.append(pltpu.make_async_copy(asked_ref.at[place], lists_ref.at[place], local_sem.at[place]))
+        lists[-1].start()
 
     def requester(place):
         return (lax.rem(me + devices - STEPS[place], devices),)
@@ -99,14 +111,14 @@
             copy.start()
             copies.append(copy)
 
-    hear(0)
+    lists[0].wait()
     serve(WIDE[0:2], 0)
-    hear(1)
+    lists[1].wait()
     serve(WIDE[2:4], 2)
-    hear(2)
+    lists[2].wait()
     serve(WIDE[4:5], 4)
     for place in (3, 4, 5, 6):
-        hear(place)
+        lists[place].wait()
     for number, (place, block) in enumerate(EDGE):
         fill(edge_ref, number, lists_ref[place, block, SPAN])
         copy = pltpu.make_async_remote_copy(
@@ -115,10 +127,20 @@
         )
         copy.start()
         copies.append(copy)
+
+    def own_step(row, carry):
+        for number, feature in enumerate(COLUMNS):
+            square_ref[number, pl.ds(row * 128, 128), :] = column(near_ref[208 + row, feature : feature + 1, :])
+        return carry
+
+    lax.fori_loop(0, 16, own_step, 0)
+    stored = pltpu.make_async_copy(square_ref, columns_ref, column_sem)
+    stored.start()
     for copy in copies:
         copy.wait()
     for ask in asks:
         ask.wait_send()
+    stored.wait()
 
 
 def rows_of(ref, slot, feature):
@@ -157,7 +179,7 @@
     for number, end in enumerate(ends):
         def one_row(place, count):
             row = order_ref[place]
-            chunks = (offs_ref[27, row] + 127) // 128
+            chunks = (offs_ref[27, row] + 127) >> 7
             for chunk in range(10):
                 jobs_ref[count + chunk] = row * 32 + chunk
 
@@ -170,7 +192,7 @@
 
         count = lax.fori_loop(begin, end, one_row, count)
         jobs_ref[count] = 31
-        count = count + count % 2
+        count = count + (count & 1)
         jobs_ref[513 + number] = count
         begin = end
 
@@ -182,7 +204,7 @@
             step(2 * pair + 1, parts)
             return carry
 
-        lax.fori_loop(jobs_ref[512 + number] // 2, jobs_ref[513 + number] // 2, two, 0)
+        lax.fori_loop(jobs_ref[512 + number] >> 1, jobs_ref[513 + number] >> 1, two, 0)
 
 
 def pack_rows(offs_ref, row, get, put, width):
@@ -192,23 +214,29 @@
         begin = offs_ref[slot, row]
         end = offs_ref[slot + 1, row]
         turned = get(slot)
-        merged = jnp.where(lane >= begin % 128, turned, held)
-        put(begin // 128, merged)
-        return jnp.where(jnp.broadcast_to(end // 128 > begin // 128, (width, 128)), turned, merged)
+        merged = jnp.where(lane >= (begin & 127), turned, held)
+        put(begin >> 7, merged)
+        return jnp.where(jnp.broadcast_to((end >> 7) > (begin >> 7), (width, 128)), turned, merged)
 
     return lax.fori_loop(0, 27, slot_step, get(0), unroll=27)
 
 
 def density_kernel(
-    req_ref, lists_ref, counts_ref, active_ref, near_ref, shift_ref, energy_ref, old_ref,
+    req_ref, lists_ref, counts_ref, active_ref, near_ref, columns_ref, shift_ref, energy_ref, old_ref,
     fresh_ref, mine_ref, edge_ref, pack_ref, index_ref, offs_out_ref, jobs_ref,
-    table_ref, mask_ref, offs_ref, order_ref, x_ref, y_ref, z_ref, inv_ref, sum_ref, local_sem,
+    table_ref, mask_ref, offs_ref, order_ref, x_ref, y_ref, z_ref, inv_ref, sum_ref, local_sem, column_sem,
 ):
     cells = old_ref.shape[0]
     first = lax.axis_index("dom") * cells
     lane = lax.broadcasted_iota(jnp.int32, (1, 128), 1)
     lanes = lax.broadcasted_iota(jnp.int32, (16, 128), 1)
     on_diagonal = lax.broadcasted_iota(jnp.int32, (16, 128), 0) == lanes
+    loads = [
+        pltpu.make_async_copy(columns_ref.at[number], ref, column_sem.at[number])
+        for number, ref in enumerate((x_ref, y_ref, z_ref, inv_ref))
+    ]
+    for load in loads:
+        load.start()
 
     lows, highs = [], []
     for axis in range(3):
@@ -253,9 +281,6 @@
     table_ref[...] = GAS * energy_ref[...] / old_ref[...]
 
     def own_step(row, carry):
-        own = near_ref[pl.ds(1664 + row * 8, 8), :]
-        for ref, feature in ((x_ref, 1), (y_ref, 2), (z_ref, 3), (inv_ref, 7)):
-            ref[pl.ds(row * 128, 128), :] = column(own[feature : feature + 1])
         sum_ref[pl.ds(row * 128, 128), :] = jnp.zeros((128, 128), jnp.float32)
         return carry
 
@@ -275,16 +300,18 @@
         total = offs_ref[27, row]
         wide = lax.broadcasted_iota(jnp.int32, (8, 128), 1)
         deep = lax.broadcasted_iota(jnp.int32, (8, 128), 0)
-        put(total // 128, jnp.where((deep == 0) & (wide >= total % 128), 0.0, held))
+        put(total >> 7, jnp.where((deep == 0) & (wide >= (total & 127)), 0.0, held))
         put(31, jnp.where(deep == 0, 0.0, held))
         return carry
 
     lax.fori_loop(0, 16, pack_step, 0)
     list_jobs(offs_ref, counts_ref, active_ref, first, order_ref, jobs_ref)
+    for load in loads:
+        load.wait()
 
     def job_step(job, parts):
         code = jobs_ref[job]
-        row = code // 32
+        row = code >> 5
         tile = pack_ref[code]
         mass, near_x, near_y, near_z = [jnp.broadcast_to(tile[f : f + 1], (8, 128)) for f in range(4)]
         for part in range(parts):
@@ -294,8 +321,8 @@
             gap_z = z_ref[at, :] - near_z
             square = jnp.maximum(gap_x * gap_x + gap_y * gap_y + gap_z * gap_z, TINY)
             ratio = square * lax.rsqrt(square) * inv_ref[at, :]
-            outer = 1.0 - jnp.minimum(ratio, 1.0)
-            inner = 1.0 - jnp.minimum(ratio + ratio, 1.0)
+            outer = jnp.maximum(1.0 - ratio, 0.0)
+            inner = jnp.maximum(outer - ratio, 0.0)
             weight = (outer + outer) * (outer * outer) - inner * (inner * inner)
             sum_ref[at, :] = sum_ref[at, :] + weight * mass
 
@@ -361,15 +388,15 @@
 
 
 def slope(ratio):
-    low = jnp.minimum(ratio, 1.0)
-    high = jnp.minimum(ratio + ratio, 1.0)
-    return (high - low) * (2.0 - (low + high))
+    outer = jnp.maximum(1.0 - ratio, 0.0)
+    low = jnp.minimum(outer, ratio)
+    return low * ((outer + outer) - low)
 
 
 def force_kernel(
-    counts_ref, active_ref, offs_ref, jobs_ref, all_ref, press_ref, pack_ref, index_ref, fresh_ref,
+    counts_ref, active_ref, offs_ref, jobs_ref, all_ref, columns_ref, press_ref, pack_ref, index_ref, fresh_ref,
     hydro_ref, near_ref, turned_ref, chunk_ref, x_ref, y_ref, z_ref, vx_ref, vy_ref, vz_ref, inv_ref, own_ref,
-    ax_ref, ay_ref, az_ref, rate_ref, own_sem,
+    ax_ref, ay_ref, az_ref, rate_ref, own_sem, column_sem,
 ):
     cells = counts_ref.shape[0]
     first = lax.axis_index("dom") * cells
@@ -377,6 +404,12 @@
 
     own_copy = pltpu.make_async_copy(all_ref.at[pl.ds(1664, 128)], near_ref, own_sem)
     own_copy.start()
+    loads = [
+        pltpu.make_async_copy(columns_ref.at[number], ref, column_sem.at[number])
+        for number, ref in enumerate((x_ref, y_ref, z_ref, inv_ref, vx_ref, vy_ref, vz_ref))
+    ]
+    for load in loads:
+        load.start()
 
     def turn_step(slot, carry):
         at = pl.ds(slot * 16, 16)
@@ -391,12 +424,7 @@
         at = pl.ds(row * 128, 128)
         inverse = own[7:8]
         inv_sq = inverse * inverse
-        for ref, value in (
-            (x_ref, own[1:2]), (y_ref, own[2:3]), (z_ref, own[3:4]),
-            (vx_ref, own[4:5]), (vy_ref, own[5:6]), (vz_ref, own[6:7]),
-            (inv_ref, inverse), (own_ref, (6.0 * NORM) * (inv_sq * inv_sq) * press_ref[pl.ds(208 + row, 1), :]),
-        ):
-            ref[at, :] = column(value)
+        own_ref[at, :] = column((6.0 * NORM) * (inv_sq * inv_sq) * press_ref[pl.ds(208 + row, 1), :])
         for ref in (ax_ref, ay_ref, az_ref, rate_ref):
             ref[at, :] = jnp.zeros((128, 128), jnp.float32)
 
@@ -407,15 +435,17 @@
             chunk_ref[pl.ds(row * 32 + chunk, 1), :] = value
 
         held = pack_rows(offs_ref, row, get, put, 1)
-        put(offs_ref[27, row] // 128, held)
+        put(offs_ref[27, row] >> 7, held)
         put(31, held)
         return carry
 
     lax.fori_loop(0, 16, own_step, 0)
+    for load in loads:
+        load.wait()
 
     def job_step(job, parts):
         place = jobs_ref[job]
-        row = place // 32
+        row = place >> 5
         tile = pack_ref[place]
         near_inv = tile[7:8]
         near_sq = near_inv * near_inv
@@ -476,12 +506,12 @@
             jax.ShapeDtypeStruct((432, 128), jnp.int32), jax.ShapeDtypeStruct((32, 128), jnp.int32),
             jax.ShapeDtypeStruct((640,), jnp.int32),
         ),
-        in_specs=specs("ssssvvvv"),
+        in_specs=specs("ssssv") + [pl.BlockSpec(memory_space=pl.ANY)] + specs("vvv"),
         out_specs=tuple(specs("vvvvvvs")),
         scratch_shapes=[
             pltpu.VMEM((1600, 128), jnp.float32), pltpu.VMEM((432, 128), jnp.float32),
             pltpu.SMEM((32, 128), jnp.int32), pltpu.SMEM((32,), jnp.int32),
-        ] + [square] * 5 + [pltpu.SemaphoreType.DMA],
+        ] + [square] * 5 + [pltpu.SemaphoreType.DMA, pltpu.SemaphoreType.DMA((4,))],
         compiler_params=pltpu.CompilerParams(vmem_limit_bytes=LIMIT),
         name="density",
     )(*args)
@@ -492,12 +522,12 @@
     return pl.pallas_call(
         force_kernel,
         out_shape=floats(5, 16, 128),
-        in_specs=specs("ssss") + [pl.BlockSpec(memory_space=pl.ANY)] + specs("vvvv"),
+        in_specs=specs("ssss") + [pl.BlockSpec(memory_space=pl.ANY)] * 2 + specs("vvvv"),
         out_specs=specs("v")[0],
         scratch_shapes=[
             pltpu.VMEM((128, 128), jnp.float32), pltpu.VMEM((432, 128), jnp.float32),
             pltpu.VMEM((512, 128), jnp.float32),
-        ] + [square] * 12 + [pltpu.SemaphoreType.DMA],
+        ] + [square] * 12 + [pltpu.SemaphoreType.DMA, pltpu.SemaphoreType.DMA((7,))],
         compiler_params=pltpu.CompilerParams(vmem_limit_bytes=LIMIT),
         name="force",
     )(*args)
@@ -513,12 +543,18 @@
     shifts = jnp.asarray(shift_tiles())
     f32 = jnp.float32
 
-    near, asked = pl.pallas_call(
+    anywhere = pl.BlockSpec(memory_space=pl.ANY)
+    near, asked, columns = pl.pallas_call(
         lambda *refs: gather_kernel(devices, *refs),
-        out_shape=(jax.ShapeDtypeStruct((432, 8, 128), f32), jax.ShapeDtypeStruct((7, 16, 128), jnp.int32)),
-        in_specs=[smem, vmem, smem, vmem, vmem, vmem, vmem],
-        out_specs=(vmem, vmem),
+        out_shape=(floats(432, 8, 128), jax.ShapeDtypeStruct((7, 16, 128), jnp.int32), floats(7, 2048, 128)),
+        in_specs=[smem, vmem, smem, anywhere, anywhere, anywhere, anywhere],
+        out_specs=(vmem, vmem, anywhere),
         scratch_shapes=[
+            pltpu.VMEM((3, 1600, 128), f32),
+            pltpu.VMEM((3, 1600, 128), f32),
+            pltpu.VMEM((1600, 128), f32),
+            pltpu.VMEM((1600, 128), f32),
+            pltpu.VMEM((7, 2048, 128), f32),
             pltpu.VMEM((432, 8, 128), f32),
             pltpu.VMEM((9, 8, 128), f32),
             pltpu.SMEM((7, 16, 128), jnp.int32),
@@ -527,13 +563,15 @@
             pltpu.SemaphoreType.DMA((14,)),
             pltpu.SemaphoreType.DMA((14,)),
             pltpu.SemaphoreType.DMA((7,)),
+            pltpu.SemaphoreType.DMA((4,)),
+            pltpu.SemaphoreType.DMA,
         ],
         compiler_params=pltpu.CompilerParams(collective_id=0, has_side_effects=True, vmem_limit_bytes=LIMIT),
     )(requests, requests, counts, pos, vel, mass, smoothing)
 
     flat = near.reshape(3456, 128)
     fresh, mine, edge, packed, index, offs, jobs = density_call(
-        requests, asked, counts, active, flat, shifts, energy, density_old
+        requests, asked, counts, active, flat, columns, shifts, energy, density_old
     )
 
     press = pl.pallas_call(
@@ -549,7 +587,7 @@
         compiler_params=pltpu.CompilerParams(collective_id=1, has_side_effects=True, vmem_limit_bytes=LIMIT),
     )(mine, edge)
 
-    hydro = force_call(counts, active, offs, jobs, flat, press.reshape(432, 128), packed, index, fresh)
+    hydro = force_call(counts, active, offs, jobs, flat, columns, press.reshape(432, 128), packed, index, fresh)
     return jnp.transpose(hydro, (1, 0, 2))
 
 

time: 107 us -> 93.8 us (0.88)
  Pallas kernels: 105 us -> 91 us
    pallas_call x1, Pallas kernels: 24.1 us -> 16.9 us  [density_call(): pl.pallas_call(density_kernel, out_shape=(floats(16, 1, 128), floats(432,...]
    pallas_call x1, Pallas kernels: 26.4 us -> 20.3 us  [force_call(): pl.pallas_call(force_kernel, out_shape=floats(5, 16, 128), in_specs=specs...]
    pallas_call x1, Pallas kernels: 39.9 us -> 38.6 us  [shards(): pl.pallas_call(lambda *refs: gather_kernel(devices, *refs), out_shape=(fl...]
where the time goes in v5:
time: 93.8 us; the launch traced here: 92.5 us
  Pallas kernels  91 us (97%)
  local copies, waits for them, and re-layouts  1.46 us (2%)
    pallas_call x1, Pallas kernels, shards(): pl.pallas_call(lambda *refs: gather_kernel(devices, *refs), out_shape=(fl...  38.6 us
    pallas_call x1, Pallas kernels, force_call(): pl.pallas_call(force_kernel, out_shape=floats(5, 16, 128), in_specs=specs...  20.3 us
    pallas_call x1, Pallas kernels, density_call(): pl.pallas_call(density_kernel, out_shape=(floats(16, 1, 128), floats(432,...  16.9 us
    pallas_call x1, Pallas kernels, shards(): pl.pallas_call(lambda *refs: pass_kernel(devices, *refs), out_shape=jax.S...  15.2 us

profile of v5, /device:TPU:1, one launch (start us, length us, event | category | flops | bytes accessed | tf_op | source)
XLA Modules:
  0.0 92.5 jit_solution(16347570346132605648)
XLA Ops:
  0.0 0.8 copy.12
  0.8 0.1 reshape.9
  0.9 0.6 pad.4.refs_0_.refs_1_.req_ref
  1.5 38.6 %shard_map.100 = (f32[432,8,128]{2,1,0:T(8,128)}, s32[7,16,128]{2,1,0:T(8,128)}, f32[7,2048,128]{2,1,0:T(8,128)}) custom-call(s32[16,128]{1,0:T(8,128)} %pad.4.refs_0_.refs_1_.req_ref, s32[16,128]{1,0:T(8,128)} %pad.4.refs_0_.refs_1_.req_ref, s32[1600]{0:T(1024)} %counts_ref.3, f32[3,1600,128]{2,1,0:T(8,128)} %bitcast.8, f32[3,1600,128]{2,1,0:T(8,128)} %bitcast.9, ...), custom_call_target="tpu_custom_call" | custom-call | tf_op jit(solution)/shard_map/pallas_call | solution.py:547
  40.0 16.9 %density.1 = (f32[16,1,128]{2,1,0:T(1,128)}, f32[432,1,128]{2,1,0:T(1,128)}, f32[9,1,128]{2,1,0:T(1,128)}, f32[512,8,128]{2,1,0:T(8,128)}, s32[432,128]{1,0:T(8,128)}, /*index=5*/s32[32,128]{1,0:T(8,128)}, s32[640]{0:T(1024)}) custom-call(s32[16,128]{1,0:T(8,128)} %pad.4.refs_0_.refs_1_.req_ref, s32[7,16,128]{2,1,0:T(8,128)} %get-tuple-element.15.lists_ref, ...), custom_call_target="tpu_custom_call" | custom-call | tf_op jit(solution)/shard_map/density/pallas_call | solution.py:502
  57.0 15.2 %shard_map.101 = f32[432,1,128]{2,1,0:T(1,128)} custom-call(f32[432,1,128]{2,1,0:T(1,128)} %get-tuple-element.20.refs_0_, f32[9,1,128]{2,1,0:T(1,128)} %get-tuple-element.21.refs_1_), custom_call_target="tpu_custom_call" | custom-call | tf_op jit(solution)/shard_map/pallas_call | solution.py:577
  72.2 20.3 %force.1 = f32[5,16,128]{2,1,0:T(8,128)} custom-call(s32[1600]{0:T(1024)} %counts_ref.3, s32[16]{0:T(128)} %active_ref.3, s32[32,128]{1,0:T(8,128)} %get-tuple-element.18.offs_ref, s32[640]{0:T(1024)} %get-tuple-element.19.jobs_ref, f32[3456,128]{1,0:T(8,128)} %bitcast.7, f32[7,2048,128]{2,1,0:T(8,128)} %get-tuple-element.17.columns_ref, ...), custom_call_target="tpu_custom_call" | custom-call | tf_op jit(solution)/shard_map/force/pallas_call | solution.py:522

commit v6 on v5

v6 whole, which is shorter than its diff:
```python
import math

import jax
import jax.numpy as jnp
import numpy as np
from jax import lax
from jax.experimental import pallas as pl
from jax.experimental.pallas import tpu as pltpu
from jax.sharding import PartitionSpec as P

MESH = pl.DeviceIdType.MESH
NORM = 8.0 / math.pi
GAS = 2.0 / 3.0
TINY = 1e-14
LIMIT = 56 * 1024 * 1024

STEPS = (16, 4, 20, 1, 5, 17, 21)
WIDE = ((0, 6), (0, 7), (1, 2), (1, 5), (2, 8))
EDGE = ((6, 8), (5, 6), (5, 7), (4, 2), (4, 5), (3, 0), (3, 1), (3, 3), (3, 4))
HOME = (0, 1, 3, 4)
SPAN = 47
COLUMNS = (1, 2, 3, 7, 4, 5, 6)


def shift_tiles():
    tiles = np.zeros((27, 8, 128), np.float32)
    for slot in range(27):
        tiles[slot, 1] = slot // 9 - 1
        tiles[slot, 2] = slot // 3 % 3 - 1
        tiles[slot, 3] = slot % 3 - 1
    return tiles


def greet(me, devices):
    barrier = pltpu.get_barrier_semaphore()
    for steps in STEPS:
        for other in (me + steps, me + devices - steps):
            pl.semaphore_signal(barrier, inc=1, device_id=(lax.rem(other, devices),), device_id_type=MESH)
    pl.semaphore_wait(barrier, 2 * len(STEPS))


def gather_kernel(
    devices, req_ref, req_send, counts_ref, active_ref, pos_all, vel_all, mass_all, smooth_all, energy_all, old_all,
    near_ref, press_ref, fresh_ref, columns_ref,
    pos_ref, vel_ref, mass_ref, smooth_ref, energy_ref, old_ref, asked_ref, square_ref, sum_ref, table_ref, own_ref,
    send_ref, edge_ref, give_ref, give_edge_ref, lists_ref,
    ask_out, ask_in, send_sem, recv_sem, give_out, give_in, local_sem, table_sem, column_sem,
):
    me = lax.axis_index("dom")
    cells = mass_ref.shape[0]
    tables = [
        pltpu.make_async_copy(source, target, table_sem.at[number])
        for number, (source, target) in enumerate(
            (
                (pos_all, pos_ref), (vel_all, vel_ref), (mass_all, mass_ref), (smooth_all, smooth_ref),
                (energy_all, energy_ref), (old_all, old_ref),
            )
        )
    ]
    for table in tables:
        table.start()
    first = me * cells
    lane = lax.broadcasted_iota(jnp.int32, (1, 128), 1)

    def local(cell):
        return jnp.clip(cell - first, 0, cells - 1)

    def fill(dst, place, cell):
        cell = local(cell)
        keep = lane < counts_ref[cell]
        dst[place, 0:1, :] = jnp.where(keep, mass_ref[pl.ds(cell, 1), :], 0.0)
        for axis in range(3):
            dst[place, 1 + axis : 2 + axis, :] = pos_ref[axis, pl.ds(cell, 1), :]
            dst[place, 4 + axis : 5 + axis, :] = vel_ref[axis, pl.ds(cell, 1), :]
        dst[place, 7:8, :] = 1.0 / smooth_ref[pl.ds(cell, 1), :]

    greet(me, devices)
    asks = []
    for place, steps in enumerate(STEPS):
        ask = pltpu.make_async_remote_copy(
            req_send, asked_ref.at[place], ask_out.at[place], ask_in.at[place],
            device_id=(lax.rem(me + steps, devices),), device_id_type=MESH,
        )
        ask.start()
        asks.append(ask)

    for table in tables:
        table.wait()

    def home_step(entry, carry):
        for block in HOME:
            fill(near_ref, block * 48 + entry, req_ref[block, entry])
        return carry

    lax.fori_loop(0, SPAN, home_step, 0)
    copies = []
    lists = []
    for place, ask in enumerate(asks):
        ask.wait_recv()
        lists.append(pltpu.make_async_copy(asked_ref.at[place], lists_ref.at[place], local_sem.at[place]))
        lists[-1].start()

    def requester(place):
        return (lax.rem(me + devices - STEPS[place], devices),)

    def serve(group, start):
        def step(entry, carry):
            for place, block in group:
                fill(send_ref, block * 48 + entry, lists_ref[place, block, entry])
            return carry

        lax.fori_loop(0, SPAN, step, 0)
        for number, (place, block) in enumerate(group):
            rows = pl.ds(block * 48, SPAN)
            copy = pltpu.make_async_remote_copy(
                send_ref.at[rows], near_ref.at[rows], send_sem.at[start + number], recv_sem.at[start + number],
                device_id=requester(place), device_id_type=MESH,
            )
            copy.start()
            copies.append(copy)

    lists[0].wait()
    serve(WIDE[0:2], 0)
    lists[1].wait()
    serve(WIDE[2:4], 2)
    lists[2].wait()
    serve(WIDE[4:5], 4)
    for place in (3, 4, 5, 6):
        lists[place].wait()
    for number, (place, block) in enumerate(EDGE):
        fill(edge_ref, number, lists_ref[place, block, SPAN])
        copy = pltpu.make_async_remote_copy(
            edge_ref.at[number], near_ref.at[block * 48 + SPAN], send_sem.at[5 + number], recv_sem.at[5 + number],
            device_id=requester(place), device_id_type=MESH,
        )
        copy.start()
        copies.append(copy)

    def own_step(row, carry):
        for number, feature in enumerate(COLUMNS):
            square_ref[number, pl.ds(row * 128, 128), :] = column(near_ref[208 + row, feature : feature + 1, :])
        return carry

    lax.fori_loop(0, 16, own_step, 0)
    stored = pltpu.make_async_copy(square_ref, columns_ref, column_sem)
    stored.start()
    sum_ref[...] = jnp.zeros((2048, 128), jnp.float32)

    def add_tiles(row, tiles):
        near = []
        for index, *shift in tiles:
            tile = near_ref[index]
            near.append([tile[0:1]] + [tile[1 + axis : 2 + axis] + shift[axis] for axis in range(3)])
        for part in range(4):
            at = pl.ds(row * 128 + part * 32, 32)
            own_x, own_y, own_z, own_inv = [square_ref[number, at, :] for number in range(4)]
            total = sum_ref[at, :]
            for mass, near_x, near_y, near_z in near:
                gap_x = own_x - near_x
                gap_y = own_y - near_y
                gap_z = own_z - near_z
                square = jnp.maximum(gap_x * gap_x + gap_y * gap_y + gap_z * gap_z, TINY)
                ratio = square * lax.rsqrt(square) * own_inv
                outer = jnp.maximum(1.0 - ratio, 0.0)
                inner = jnp.maximum(outer - ratio, 0.0)
                total = total + ((outer + outer) * (outer * outer) - inner * (inner * inner)) * mass
            sum_ref[at, :] = total

    def add_blocks(blocks):
        def step(entry, carry):
            high = (entry // 16 - 1).astype(jnp.float32)
            add_tiles(entry % 16, [(block * 48 + entry, block // 3 - 1.0, block % 3 - 1.0, high) for block in blocks])
            return carry

        lax.fori_loop(0, SPAN, step, 0)

    add_blocks(HOME)
    for blocks, numbers in (((6, 7), (0, 1)), ((2, 5), (2, 3)), ((8,), (4,))):
        for number in numbers:
            copies[number].wait_recv()
        add_blocks(blocks)
    for copy in copies[5:]:
        copy.wait_recv()
    for begin in (0, 3, 6):
        add_tiles(15, [(block * 48 + SPAN, block // 3 - 1.0, block % 3 - 1.0, 1.0) for block in range(begin, begin + 3)])

    def fresh_step(row, carry):
        inverse = near_ref[208 + row, 7:8, :]
        cell = local(active_ref[row])
        fresh = jnp.where(
            lane < counts_ref[cell],
            row_sums(sum_ref[pl.ds(row * 128, 128), :]) * (NORM * inverse * inverse * inverse),
            old_ref[pl.ds(cell, 1), :],
        )
        fresh_ref[row] = fresh
        own_ref[row] = GAS * energy_ref[pl.ds(cell, 1), :] / fresh
        return carry

    lax.fori_loop(0, 16, fresh_step, 0)
    deep = lax.broadcasted_iota(jnp.int32, (32, 128), 0)
    own_cells = [local(active_ref[row]) for row in range(16)]

    def table_step(part, carry):
        at = pl.ds(part * 32, 32)
        value = GAS * energy_ref[at, :] / old_ref[at, :]
        for row in range(16):
            value = jnp.where(deep == own_cells[row] - part * 32, own_ref[row], value)
        table_ref[at, :] = value
        return carry

    lax.fori_loop(0, cells // 32, table_step, 0)

    def give_step(entry, carry):
        for place, block in WIDE:
            give_ref[block * 48 + entry] = table_ref[pl.ds(local(lists_ref[place, block, entry]), 1), :]
        return carry

    lax.fori_loop(0, SPAN, give_step, 0)
    gives = []
    for number, (place, block) in enumerate(WIDE):
        rows = pl.ds(block * 48, SPAN)
        gives.append((place, give_ref.at[rows], press_ref.at[rows]))
    for number, (place, block) in enumerate(EDGE):
        give_edge_ref[number] = table_ref[pl.ds(local(lists_ref[place, block, SPAN]), 1), :]
        gives.append((place, give_edge_ref.at[number], press_ref.at[block * 48 + SPAN]))
    gives = [
        pltpu.make_async_remote_copy(
            source, target, give_out.at[number], give_in.at[number], device_id=requester(place), device_id_type=MESH
        )
        for number, (place, source, target) in enumerate(gives)
    ]
    for give in gives:
        give.start()

    def keep_step(entry, carry):
        for block in HOME:
            press_ref[block * 48 + entry] = table_ref[pl.ds(local(req_ref[block, entry]), 1), :]
        return carry

    lax.fori_loop(0, SPAN, keep_step, 0)
    for ask in asks:
        ask.wait_send()
    for copy in copies:
        copy.wait_send()
    stored.wait()
    for give in gives:
        give.wait()


def rows_of(ref, slot, feature):
    return ref[pl.ds(slot * 128 + feature, 16, stride=8), :]


def pick(values, index):
    return jnp.take_along_axis(values, index, axis=1, mode="promise_in_bounds")


def eye():
    return lax.broadcasted_iota(jnp.int32, (128, 128), 0) == lax.broadcasted_iota(jnp.int32, (128, 128), 1)


def column(row):
    return jnp.broadcast_to(jnp.sum(jnp.where(eye(), row, 0.0), axis=1, keepdims=True), (128, 128))


def row_sums(pairs):
    total = jnp.sum(pairs, axis=1, keepdims=True)
    return jnp.sum(jnp.where(eye(), total, 0.0), axis=0, keepdims=True)


def list_jobs(offs_ref, counts_ref, active_ref, first, order_ref, jobs_ref):
    place = jnp.int32(0)
    ends = []
    for low, high in ((0, 80), (80, 96), (96, 112), (112, 128)):
        for row in range(16):
            own = counts_ref[active_ref[row] - first]
            order_ref[place] = row
            place = place + ((own > low) & (own <= high)).astype(jnp.int32)
        ends.append(place)
    count = jnp.int32(0)
    begin = jnp.int32(0)
    jobs_ref[512] = count
    for number, end in enumerate(ends):
        def one_row(place, count):
            row = order_ref[place]
            chunks = (offs_ref[27, row] + 127) >> 7
            for chunk in range(10):
                jobs_ref[count + chunk] = row * 32 + chunk

            def one_chunk(chunk, carry):
                jobs_ref[count + chunk] = row * 32 + chunk
                return carry

            lax.fori_loop(10, chunks, one_chunk, 0)
            return count + chunks

        count = lax.fori_loop(begin, end, one_row, count)
        jobs_ref[count] = 31
        count = count + (count & 1)
        jobs_ref[513 + number] = count
        begin = end


def run_jobs(jobs_ref, step):
    for number, parts in enumerate((10, 12, 14, 16)):
        def two(pair, carry):
            step(2 * pair, parts)
            step(2 * pair + 1, parts)
            return carry

        lax.fori_loop(jobs_ref[512 + number] >> 1, jobs_ref[513 + number] >> 1, two, 0)


def slope(ratio):
    outer = jnp.maximum(1.0 - ratio, 0.0)
    low = jnp.minimum(outer, ratio)
    return low * ((outer + outer) - low)


def force_kernel(
    counts_ref, active_ref, columns_ref, near_ref, press_ref, shift_ref, fresh_ref,
    hydro_ref, pack_ref, chunk_ref, index_ref, mask_ref, offs_out_ref, turned_ref, offs_ref, order_ref, jobs_ref,
    x_ref, y_ref, z_ref, vx_ref, vy_ref, vz_ref, inv_ref, own_ref, ax_ref, ay_ref, az_ref, rate_ref, local_sem, column_sem,
):
    cells = counts_ref.shape[0]
    first = lax.axis_index("dom") * cells
    lane = lax.broadcasted_iota(jnp.int32, (1, 128), 1)
    lanes = lax.broadcasted_iota(jnp.int32, (16, 128), 1)
    on_diagonal = lax.broadcasted_iota(jnp.int32, (16, 128), 0) == lanes
    loads = [
        pltpu.make_async_copy(columns_ref.at[number], ref, column_sem.at[number])
        for number, ref in enumerate((x_ref, y_ref, z_ref, inv_ref, vx_ref, vy_ref, vz_ref))
    ]
    for load in loads:
        load.start()
    lows, highs = [], []
    for axis in range(3):
        own = rows_of(near_ref, 13, 1 + axis)
        lows.append(jnp.min(own, axis=1, keepdims=True))
        highs.append(jnp.max(own, axis=1, keepdims=True))
    widest = jnp.min(rows_of(near_ref, 13, 7), axis=1, keepdims=True)

    for slot in range(27):
        away = jnp.zeros((16, 128), jnp.float32)
        for axis, step in enumerate((slot // 9, slot // 3 % 3, slot % 3)):
            at = rows_of(near_ref, slot, 1 + axis) + (step - 1.0)
            out = jnp.maximum(jnp.maximum(lows[axis] - at, at - highs[axis]), 0.0)
            away = away + out * out
        reach = jnp.minimum(rows_of(near_ref, slot, 7), widest)
        chosen = (rows_of(near_ref, slot, 0) > 0.0) & (away * (reach * reach) <= 1.0001)
        mask_ref[slot * 16 : slot * 16 + 16, :] = jnp.where(chosen, 1.0, 0.0)
    high = lax.broadcasted_iota(jnp.int32, (128, 256), 0)
    wide = lax.broadcasted_iota(jnp.int32, (128, 256), 1)
    counter = jnp.where((wide >= 128) | (high <= wide), 1.0, 0.0).astype(jnp.bfloat16)
    begin = jnp.zeros((16, 128), jnp.int32)
    for slot in range(27):
        at = pl.ds(slot * 16, 16)
        ranks = jnp.dot(mask_ref[at, :].astype(jnp.bfloat16), counter, preferred_element_type=jnp.float32)
        ranks = ranks.astype(jnp.int32)
        order = ranks[:, 0:128]
        wanted = (lanes - begin) & 127
        index = jnp.zeros((16, 128), jnp.int32)
        for step in (64, 32, 16, 8, 4, 2, 1):
            index = index + jnp.where(pick(order, index + (step - 1)) <= wanted, step, 0)
        index_ref[at, :] = index
        turned_ref[at, :] = pick(press_ref[at, :], index)
        offs_out_ref[slot : slot + 1, :] = jnp.sum(jnp.where(on_diagonal, begin, 0), axis=0, keepdims=True)
        begin = begin + ranks[:, 128:256]
    offs_out_ref[27:28, :] = jnp.sum(jnp.where(on_diagonal, begin, 0), axis=0, keepdims=True)
    offs_out_ref[28:32, :] = jnp.zeros((4, 128), jnp.int32)
    moved = pltpu.make_async_copy(offs_out_ref, offs_ref, local_sem)
    moved.start()

    def own_step(row, carry):
        own = near_ref[pl.ds(1664 + row * 8, 8), :]
        at = pl.ds(row * 128, 128)
        inv_sq = own[7:8] * own[7:8]
        own_ref[at, :] = column((6.0 * NORM) * (inv_sq * inv_sq) * press_ref[pl.ds(208 + row, 1), :])
        for ref in (ax_ref, ay_ref, az_ref, rate_ref):
            ref[at, :] = jnp.zeros((128, 128), jnp.float32)
        return carry

    lax.fori_loop(0, 16, own_step, 0)
    moved.wait()
    deep = lax.broadcasted_iota(jnp.int32, (8, 128), 0)
    across = lax.broadcasted_iota(jnp.int32, (8, 128), 1)

    def pack_step(row, carry):
        def put(chunk, tile, value):
            pack_ref[row * 32 + chunk] = tile
            chunk_ref[pl.ds(row * 32 + chunk, 1), :] = value

        def slot_step(slot, held):
            begin = offs_ref[slot, row]
            end = offs_ref[slot + 1, row]
            at = slot * 16 + row
            tile = near_ref[pl.ds(at * 8, 8), :] + shift_ref[slot]
            tile = pick(tile, jnp.broadcast_to(index_ref[pl.ds(at, 1), :], (8, 128)))
            value = turned_ref[pl.ds(at, 1), :]
            start = begin & 127
            merged = jnp.where(across >= start, tile, held[0])
            merged_value = jnp.where(lane >= start, value, held[1])
            put(begin >> 7, merged, merged_value)
            more = (end >> 7) > (begin >> 7)
            return (
                jnp.where(jnp.broadcast_to(more, (8, 128)), tile, merged),
                jnp.where(jnp.broadcast_to(more, (1, 128)), value, merged_value),
            )

        held = (near_ref[pl.ds(row * 8, 8), :], turned_ref[pl.ds(row, 1), :])
        held = lax.fori_loop(0, 27, slot_step, held, unroll=27)
        total = offs_ref[27, row]
        put(total >> 7, jnp.where((deep == 0) & (across >= (total & 127)), 0.0, held[0]), held[1])
        put(31, jnp.where(deep == 0, 0.0, held[0]), held[1])
        return carry

    lax.fori_loop(0, 16, pack_step, 0)
    list_jobs(offs_ref, counts_ref, active_ref, first, order_ref, jobs_ref)
    for load in loads:
        load.wait()

    def job_step(job, parts):
        place = jobs_ref[job]
        row = place >> 5
        tile = pack_ref[place]
        near_inv = tile[7:8]
        near_sq = near_inv * near_inv
        push = (6.0 * NORM) * tile[0:1] * (near_sq * near_sq) * chunk_ref[pl.ds(place, 1), :]
        mass, near_x, near_y, near_z, near_vx, near_vy, near_vz = [
            jnp.broadcast_to(tile[f : f + 1], (8, 128)) for f in range(7)
        ]
        near_inv = jnp.broadcast_to(near_inv, (8, 128))
        push = jnp.broadcast_to(push, (8, 128))
        for part in range(parts):
            at = pl.ds(row * 128 + part * 8, 8)
            gap_x = x_ref[at, :] - near_x
            gap_y = y_ref[at, :] - near_y
            gap_z = z_ref[at, :] - near_z
            square = jnp.maximum(gap_x * gap_x + gap_y * gap_y + gap_z * gap_z, TINY)
            root = lax.rsqrt(square)
            gap = square * root
            pull = slope(gap * inv_ref[at, :]) * root * mass
            both = own_ref[at, :] * pull + slope(gap * near_inv) * push * root
            work = (vx_ref[at, :] - near_vx) * gap_x + (vy_ref[at, :] - near_vy) * gap_y + (vz_ref[at, :] - near_vz) * gap_z
            ax_ref[at, :] = ax_ref[at, :] + both * gap_x
            ay_ref[at, :] = ay_ref[at, :] + both * gap_y
            az_ref[at, :] = az_ref[at, :] + both * gap_z
            rate_ref[at, :] = rate_ref[at, :] + pull * work

    run_jobs(jobs_ref, job_step)

    def end_step(row, carry):
        own = near_ref[pl.ds(1664 + row * 8, 8), :]
        inverse = own[7:8]
        inv_sq = inverse * inverse
        factor = (-6.0 * NORM) * (inv_sq * inv_sq) * press_ref[pl.ds(208 + row, 1), :]
        at = pl.ds(row * 128, 128)
        keep = lane < counts_ref[active_ref[row] - first]
        values = [fresh_ref[row]] + [row_sums(ref[at, :]) for ref in (ax_ref, ay_ref, az_ref)]
        values.append(factor * row_sums(rate_ref[at, :]))
        for number, value in enumerate(values):
            hydro_ref[number, pl.ds(row, 1), :] = jnp.where(keep, value, 0.0)
        return carry

    lax.fori_loop(0, 16, end_step, 0)


def specs(kinds):
    return [pl.BlockSpec(memory_space=pltpu.SMEM if kind == "s" else pltpu.VMEM) for kind in kinds]


def floats(*shape):
    return jax.ShapeDtypeStruct(shape, jnp.float32)


def force_call(*args):
    square = pltpu.VMEM((2048, 128), jnp.float32)
    return pl.pallas_call(
        force_kernel,
        out_shape=floats(5, 16, 128),
        in_specs=specs("ss") + [pl.BlockSpec(memory_space=pl.ANY)] + specs("vvvv"),
        out_specs=specs("v")[0],
        scratch_shapes=[
            pltpu.VMEM((512, 8, 128), jnp.float32), pltpu.VMEM((512, 128), jnp.float32),
            pltpu.VMEM((432, 128), jnp.int32), pltpu.VMEM((432, 128), jnp.float32), pltpu.VMEM((32, 128), jnp.int32),
            pltpu.VMEM((432, 128), jnp.float32), pltpu.SMEM((32, 128), jnp.int32), pltpu.SMEM((32,), jnp.int32),
            pltpu.SMEM((640,), jnp.int32),
        ] + [square] * 12 + [pltpu.SemaphoreType.DMA, pltpu.SemaphoreType.DMA((7,))],
        compiler_params=pltpu.CompilerParams(vmem_limit_bytes=LIMIT),
        name="force",
    )(*args)


def shards(positions, velocity, mass, smoothing, energy, density_old, counts, active, neighbours):
    devices = lax.axis_size("dom")
    vmem = pl.BlockSpec(memory_space=pltpu.VMEM)
    smem = pl.BlockSpec(memory_space=pltpu.SMEM)
    pos = jnp.transpose(positions, (1, 0, 2))
    vel = jnp.transpose(velocity, (1, 0, 2))
    requests = jnp.pad(neighbours.T.reshape(9, 48), ((0, 7), (0, 80)))
    shifts = jnp.asarray(shift_tiles())
    f32 = jnp.float32

    anywhere = pl.BlockSpec(memory_space=pl.ANY)
    near, press, fresh, columns = pl.pallas_call(
        lambda *refs: gather_kernel(devices, *refs),
        out_shape=(floats(432, 8, 128), floats(432, 1, 128), floats(16, 1, 128), floats(7, 2048, 128)),
        in_specs=[smem, vmem, smem, smem] + [anywhere] * 6,
        out_specs=(vmem, vmem, vmem, anywhere),
        scratch_shapes=[
            pltpu.VMEM((3, 1600, 128), f32),
            pltpu.VMEM((3, 1600, 128), f32),
            pltpu.VMEM((1600, 128), f32),
            pltpu.VMEM((1600, 128), f32),
            pltpu.VMEM((1600, 128), f32),
            pltpu.VMEM((1600, 128), f32),
            pltpu.VMEM((7, 16, 128), jnp.int32),
            pltpu.VMEM((7, 2048, 128), f32),
            pltpu.VMEM((2048, 128), f32),
            pltpu.VMEM((1600, 128), f32),
            pltpu.VMEM((16, 1, 128), f32),
            pltpu.VMEM((432, 8, 128), f32),
            pltpu.VMEM((9, 8, 128), f32),
            pltpu.VMEM((432, 1, 128), f32),
            pltpu.VMEM((9, 1, 128), f32),
            pltpu.SMEM((7, 16, 128), jnp.int32),
            pltpu.SemaphoreType.DMA((7,)),
            pltpu.SemaphoreType.DMA((7,)),
            pltpu.SemaphoreType.DMA((14,)),
            pltpu.SemaphoreType.DMA((14,)),
            pltpu.SemaphoreType.DMA((14,)),
            pltpu.SemaphoreType.DMA((14,)),
            pltpu.SemaphoreType.DMA((7,)),
            pltpu.SemaphoreType.DMA((6,)),
            pltpu.SemaphoreType.DMA,
        ],
        compiler_params=pltpu.CompilerParams(collective_id=0, has_side_effects=True, vmem_limit_bytes=LIMIT),
        name="cells",
    )(requests, requests, counts, active, pos, vel, mass, smoothing, energy, density_old)

    hydro = force_call(
        counts, active, columns, near.reshape(3456, 128), press.reshape(432, 128), shifts, fresh
    )
    return jnp.transpose(hydro, (1, 0, 2))


def solution(mesh):
    placed = (
        P("dom", None, None),
        P("dom", None, None),
        P("dom", None),
        P("dom", None),
        P("dom", None),
        P("dom", None),
        P("dom"),
        P("dom"),
        P("dom", None),
    )
    return jax.shard_map(
        shards, mesh=mesh, in_specs=placed, out_specs=P("dom", None, None), check_vma=False
    )
```

time: 93.8 us -> 86.8 us (0.925); the launches traced: 92.5 us -> 86.4 us
  Pallas kernels: 91 us -> 85 us
    pallas_call x2 -> x0, Pallas kernels: 32.1 us -> none  [the longest x1 16.9 us: density_call(): pl.pallas_call(density_kernel, out_shape=(floats(16, 1, 128), floats(432,...]
    pallas_call x1, Pallas kernels: 38.6 us -> 60.7 us  [shards(): pl.pallas_call(lambda *refs: gather_kernel(devices, *refs), out_shape=(fl...]
    pallas_call x1, Pallas kernels: 20.3 us -> 24.2 us  [force_call(): pl.pallas_call(force_kernel, out_shape=floats(5, 16, 128), in_specs=specs...]
where the time goes in v6:
time: 86.8 us; the launch traced here: 86.4 us
  Pallas kernels  85 us (98%)
  local copies, waits for them, and re-layouts  1.46 us (2%)
    pallas_call x1, Pallas kernels, shards(): pl.pallas_call(lambda *refs: gather_kernel(devices, *refs), out_shape=(fl...  60.7 us
    pallas_call x1, Pallas kernels, force_call(): pl.pallas_call(force_kernel, out_shape=floats(5, 16, 128), in_specs=specs...  24.2 us

profile of v6, /device:TPU:1, one launch (start us, length us, event | category | flops | bytes accessed | tf_op | source)
XLA Modules:
  0.0 86.4 jit_solution(11844667677961910545)
XLA Ops:
  0.0 0.8 copy.12
  0.8 0.1 reshape.9
  0.9 0.6 pad.4.refs_0_.refs_1_
  1.5 60.7 %cells.1 = (f32[432,8,128]{2,1,0:T(8,128)}, f32[432,1,128]{2,1,0:T(1,128)}, f32[16,1,128]{2,1,0:T(1,128)}, f32[7,2048,128]{2,1,0:T(8,128)}) custom-call(s32[16,128]{1,0:T(8,128)} %pad.4.refs_0_.refs_1_, s32[16,128]{1,0:T(8,128)} %pad.4.refs_0_.refs_1_, s32[1600]{0:T(1024)} %counts_ref.1, s32[16]{0:T(128)} %active_ref.1, f32[3,1600,128]{2,1,0:T(8,128)} %bitcast.6, ...), custom_call_target="tpu_custom_call" | custom-call | tf_op jit(solution)/shard_map/cells/pallas_call | solution.py:505
  62.2 24.2 %force.1 = f32[5,16,128]{2,1,0:T(8,128)} custom-call(s32[1600]{0:T(1024)} %counts_ref.1, s32[16]{0:T(128)} %active_ref.1, f32[7,2048,128]{2,1,0:T(8,128)} %get-tuple-element.9.columns_ref, f32[3456,128]{1,0:T(8,128)} %bitcast.8, f32[432,128]{1,0:T(8,128)} %bitcast.9, f32[27,8,128]{2,1,0:T(8,128)} %constant.4.clone.shift_ref, ...), custom_call_target="tpu_custom_call" | custom-call | tf_op jit(solution)/shard_map/force/pallas_call | solution.py:478

commit v7 on v6

--- a/solution.py
+++ b/solution.py
@@ -36,7 +36,6 @@
     for steps in STEPS:
         for other in (me + steps, me + devices - steps):
             pl.semaphore_signal(barrier, inc=1, device_id=(lax.rem(other, devices),), device_id_type=MESH)
-    pl.semaphore_wait(barrier, 2 * len(STEPS))
 
 
 def gather_kernel(
@@ -75,6 +74,7 @@
         dst[place, 7:8, :] = 1.0 / smooth_ref[pl.ds(cell, 1), :]
 
     greet(me, devices)
+    pl.semaphore_wait(pltpu.get_barrier_semaphore(), 2 * len(STEPS))
     asks = []
     for place, steps in enumerate(STEPS):
         ask = pltpu.make_async_remote_copy(
@@ -93,48 +93,6 @@
         return carry
 
     lax.fori_loop(0, SPAN, home_step, 0)
-    copies = []
-    lists = []
-    for place, ask in enumerate(asks):
-        ask.wait_recv()
-        lists.append(pltpu.make_async_copy(asked_ref.at[place], lists_ref.at[place], local_sem.at[place]))
-        lists[-1].start()
-
-    def requester(place):
-        return (lax.rem(me + devices - STEPS[place], devices),)
-
-    def serve(group, start):
-        def step(entry, carry):
-            for place, block in group:
-                fill(send_ref, block * 48 + entry, lists_ref[place, block, entry])
-            return carry
-
-        lax.fori_loop(0, SPAN, step, 0)
-        for number, (place, block) in enumerate(group):
-            rows = pl.ds(block * 48, SPAN)
-            copy = pltpu.make_async_remote_copy(
-                send_ref.at[rows], near_ref.at[rows], send_sem.at[start + number], recv_sem.at[start + number],
-                device_id=requester(place), device_id_type=MESH,
-            )
-            copy.start()
-            copies.append(copy)
-
-    lists[0].wait()
-    serve(WIDE[0:2], 0)
-    lists[1].wait()
-    serve(WIDE[2:4], 2)
-    lists[2].wait()
-    serve(WIDE[4:5], 4)
-    for place in (3, 4, 5, 6):
-        lists[place].wait()
-    for number, (place, block) in enumerate(EDGE):
-        fill(edge_ref, number, lists_ref[place, block, SPAN])
-        copy = pltpu.make_async_remote_copy(
-            edge_ref.at[number], near_ref.at[block * 48 + SPAN], send_sem.at[5 + number], recv_sem.at[5 + number],
-            device_id=requester(place), device_id_type=MESH,
-        )
-        copy.start()
-        copies.append(copy)
 
     def own_step(row, carry):
         for number, feature in enumerate(COLUMNS):
@@ -166,23 +124,83 @@
                 total = total + ((outer + outer) * (outer * outer) - inner * (inner * inner)) * mass
             sum_ref[at, :] = total
 
-    def add_blocks(blocks):
+    def add_blocks(blocks, begin, end):
         def step(entry, carry):
             high = (entry // 16 - 1).astype(jnp.float32)
             add_tiles(entry % 16, [(block * 48 + entry, block // 3 - 1.0, block % 3 - 1.0, high) for block in blocks])
             return carry
 
-        lax.fori_loop(0, SPAN, step, 0)
-
-    add_blocks(HOME)
-    for blocks, numbers in (((6, 7), (0, 1)), ((2, 5), (2, 3)), ((8,), (4,))):
-        for number in numbers:
-            copies[number].wait_recv()
-        add_blocks(blocks)
-    for copy in copies[5:]:
-        copy.wait_recv()
-    for begin in (0, 3, 6):
-        add_tiles(15, [(block * 48 + SPAN, block // 3 - 1.0, block % 3 - 1.0, 1.0) for block in range(begin, begin + 3)])
+        lax.fori_loop(begin, end, step, 0)
+
+    def hear(places):
+        lists = []
+        for place in places:
+            asks[place].wait_recv()
+            lists.append(pltpu.make_async_copy(asked_ref.at[place], lists_ref.at[place], local_sem.at[place]))
+            lists[-1].start()
+        for listed in lists:
+            listed.wait()
+
+    def requester(place):
+        return (lax.rem(me + devices - STEPS[place], devices),)
+
+    hear((0, 1, 2))
+    copies = []
+    edges = []
+
+    def serve(third):
+        size = 15 if third == 2 else 16
+
+        def serve_step(entry, carry):
+            entry = third * 16 + entry
+            for place, block in WIDE:
+                fill(send_ref, block * 48 + entry, lists_ref[place, block, entry])
+            return carry
+
+        lax.fori_loop(0, size, serve_step, 0)
+        for place, block in WIDE:
+            rows = pl.ds(block * 48 + third * 16, size)
+            copy = pltpu.make_async_remote_copy(
+                send_ref.at[rows], near_ref.at[rows], send_sem.at[len(copies)], recv_sem.at[len(copies)],
+                device_id=requester(place), device_id_type=MESH,
+            )
+            copy.start()
+            copies.append(copy)
+
+    serve(0)
+    hear((3, 4, 5, 6))
+    for number, (place, block) in enumerate(EDGE):
+        fill(edge_ref, number, lists_ref[place, block, SPAN])
+        copy = pltpu.make_async_remote_copy(
+            edge_ref.at[number], near_ref.at[block * 48 + SPAN], send_sem.at[15 + number], recv_sem.at[15 + number],
+            device_id=requester(place), device_id_type=MESH,
+        )
+        copy.start()
+        edges.append(copy)
+
+    serve(1)
+    add_blocks(HOME, 0, 16)
+    serve(2)
+    add_blocks(HOME, 16, 32)
+    add_blocks(HOME, 32, SPAN)
+
+    def table_step(part, carry):
+        at = pl.ds(part * 32, 32)
+        table_ref[at, :] = GAS * energy_ref[at, :] / old_ref[at, :]
+        return carry
+
+    lax.fori_loop(0, cells // 32, table_step, 0)
+    for third in range(3):
+        for copy in copies[5 * third : 5 * third + 5]:
+            copy.wait_recv()
+        if third == 2:
+            for copy in edges:
+                copy.wait_recv()
+            for begin in (0, 3, 6):
+                add_tiles(
+                    15, [(block * 48 + SPAN, block // 3 - 1.0, block % 3 - 1.0, 1.0) for block in range(begin, begin + 3)]
+                )
+        add_blocks((6, 7, 2, 5, 8), third * 16, min(third * 16 + 16, SPAN))
 
     def fresh_step(row, carry):
         inverse = near_ref[208 + row, 7:8, :]
@@ -196,19 +214,19 @@
         own_ref[row] = GAS * energy_ref[pl.ds(cell, 1), :] / fresh
         return carry
 
-    lax.fori_loop(0, 16, fresh_step, 0)
+    lax.fori_loop(0, 16, fresh_step, 0, unroll=4)
     deep = lax.broadcasted_iota(jnp.int32, (32, 128), 0)
     own_cells = [local(active_ref[row]) for row in range(16)]
 
-    def table_step(part, carry):
+    def patch_step(part, carry):
         at = pl.ds(part * 32, 32)
-        value = GAS * energy_ref[at, :] / old_ref[at, :]
+        value = table_ref[at, :]
         for row in range(16):
             value = jnp.where(deep == own_cells[row] - part * 32, own_ref[row], value)
         table_ref[at, :] = value
         return carry
 
-    lax.fori_loop(0, cells // 32, table_step, 0)
+    lax.fori_loop(0, cells // 32, patch_step, 0)
 
     def give_step(entry, carry):
         for place, block in WIDE:
@@ -240,7 +258,7 @@
     lax.fori_loop(0, SPAN, keep_step, 0)
     for ask in asks:
         ask.wait_send()
-    for copy in copies:
+    for copy in copies + edges:
         copy.wait_send()
     stored.wait()
     for give in gives:
@@ -526,8 +544,8 @@
             pltpu.SMEM((7, 16, 128), jnp.int32),
             pltpu.SemaphoreType.DMA((7,)),
             pltpu.SemaphoreType.DMA((7,)),
-            pltpu.SemaphoreType.DMA((14,)),
-            pltpu.SemaphoreType.DMA((14,)),
+            pltpu.SemaphoreType.DMA((24,)),
+            pltpu.SemaphoreType.DMA((24,)),
             pltpu.SemaphoreType.DMA((14,)),
             pltpu.SemaphoreType.DMA((14,)),
             pltpu.SemaphoreType.DMA((7,)),

time: 86.8 us -> 83.7 us (0.964)
  the two profiles are of different devices: /device:TPU:1 before, /device:TPU:27 now
where the time goes in v7:
time: 83.7 us; the launch traced here: 83.4 us
  Pallas kernels  81.9 us (98%)
  local copies, waits for them, and re-layouts  1.46 us (2%)
    pallas_call x1, Pallas kernels, shards(): pl.pallas_call(lambda *refs: gather_kernel(devices, *refs), out_shape=(fl...  56.6 us
    pallas_call x1, Pallas kernels, force_call(): pl.pallas_call(force_kernel, out_shape=floats(5, 16, 128), in_specs=specs...  25.4 us

profile of v7, /device:TPU:27, one launch (start us, length us, event | category | flops | bytes accessed | tf_op | source)
XLA Modules:
  0.0 83.4 jit_solution(8873842964996383422)
XLA Ops:
  0.0 0.8 copy.12
  0.8 0.1 reshape.9
  0.9 0.6 pad.4.refs_0_.refs_1_
  1.5 56.6 %cells.1 = (f32[432,8,128]{2,1,0:T(8,128)}, f32[432,1,128]{2,1,0:T(1,128)}, f32[16,1,128]{2,1,0:T(1,128)}, f32[7,2048,128]{2,1,0:T(8,128)}) custom-call(s32[16,128]{1,0:T(8,128)} %pad.4.refs_0_.refs_1_, s32[16,128]{1,0:T(8,128)} %pad.4.refs_0_.refs_1_, s32[1600]{0:T(1024)} %counts_ref.1, s32[16]{0:T(128)} %active_ref.1, f32[3,1600,128]{2,1,0:T(8,128)} %bitcast.6, ...), custom_call_target="tpu_custom_call" | custom-call | tf_op jit(solution)/shard_map/cells/pallas_call | solution.py:523
  58.0 25.4 %force.1 = f32[5,16,128]{2,1,0:T(8,128)} custom-call(s32[1600]{0:T(1024)} %counts_ref.1, s32[16]{0:T(128)} %active_ref.1, f32[7,2048,128]{2,1,0:T(8,128)} %get-tuple-element.9.columns_ref, f32[3456,128]{1,0:T(8,128)} %bitcast.8, f32[432,128]{1,0:T(8,128)} %bitcast.9, f32[27,8,128]{2,1,0:T(8,128)} %constant.4.clone.shift_ref, ...), custom_call_target="tpu_custom_call" | custom-call | tf_op jit(solution)/shard_map/force/pallas_call | solution.py:496

commit v8 on v7

--- a/solution.py
+++ b/solution.py
@@ -89,7 +89,7 @@
 
     def home_step(entry, carry):
         for block in HOME:
-            fill(near_ref, block * 48 + entry, req_ref[block, entry])
+            fill(near_ref, block * 48 + entry, req_ref[entry & 15, block * 3 + (entry >> 4)])
         return carry
 
     lax.fori_loop(0, SPAN, home_step, 0)
@@ -152,9 +152,8 @@
         size = 15 if third == 2 else 16
 
         def serve_step(entry, carry):
-            entry = third * 16 + entry
             for place, block in WIDE:
-                fill(send_ref, block * 48 + entry, lists_ref[place, block, entry])
+                fill(send_ref, block * 48 + third * 16 + entry, lists_ref[place, entry, block * 3 + third])
             return carry
 
         lax.fori_loop(0, size, serve_step, 0)
@@ -170,7 +169,7 @@
     serve(0)
     hear((3, 4, 5, 6))
     for number, (place, block) in enumerate(EDGE):
-        fill(edge_ref, number, lists_ref[place, block, SPAN])
+        fill(edge_ref, number, lists_ref[place, 15, block * 3 + 2])
         copy = pltpu.make_async_remote_copy(
             edge_ref.at[number], near_ref.at[block * 48 + SPAN], send_sem.at[15 + number], recv_sem.at[15 + number],
             device_id=requester(place), device_id_type=MESH,
@@ -230,29 +229,28 @@
 
     def give_step(entry, carry):
         for place, block in WIDE:
-            give_ref[block * 48 + entry] = table_ref[pl.ds(local(lists_ref[place, block, entry]), 1), :]
-        return carry
-
+            give_ref[block * 48 + entry] = table_ref[pl.ds(local(lists_ref[place, entry & 15, block * 3 + (entry >> 4)]), 1), :]
+        return carry
+
+    def send_give(number, place, source, target):
+        give = pltpu.make_async_remote_copy(
+            source, target, give_out.at[number], give_in.at[number], device_id=requester(place), device_id_type=MESH
+        )
+        give.start()
+        return give
+
+    gives = []
+    for number, (place, block) in enumerate(EDGE):
+        give_edge_ref[number] = table_ref[pl.ds(local(lists_ref[place, 15, block * 3 + 2]), 1), :]
+        gives.append(send_give(number, place, give_edge_ref.at[number], press_ref.at[block * 48 + SPAN]))
     lax.fori_loop(0, SPAN, give_step, 0)
-    gives = []
     for number, (place, block) in enumerate(WIDE):
         rows = pl.ds(block * 48, SPAN)
-        gives.append((place, give_ref.at[rows], press_ref.at[rows]))
-    for number, (place, block) in enumerate(EDGE):
-        give_edge_ref[number] = table_ref[pl.ds(local(lists_ref[place, block, SPAN]), 1), :]
-        gives.append((place, give_edge_ref.at[number], press_ref.at[block * 48 + SPAN]))
-    gives = [
-        pltpu.make_async_remote_copy(
-            source, target, give_out.at[number], give_in.at[number], device_id=requester(place), device_id_type=MESH
-        )
-        for number, (place, source, target) in enumerate(gives)
-    ]
-    for give in gives:
-        give.start()
+        gives.append(send_give(9 + number, place, give_ref.at[rows], press_ref.at[rows]))
 
     def keep_step(entry, carry):
         for block in HOME:
-            press_ref[block * 48 + entry] = table_ref[pl.ds(local(req_ref[block, entry]), 1), :]
+            press_ref[block * 48 + entry] = table_ref[pl.ds(local(req_ref[entry & 15, block * 3 + (entry >> 4)]), 1), :]
         return carry
 
     lax.fori_loop(0, SPAN, keep_step, 0)
@@ -432,7 +430,7 @@
         put(31, jnp.where(deep == 0, 0.0, held[0]), held[1])
         return carry
 
-    lax.fori_loop(0, 16, pack_step, 0)
+    lax.fori_loop(0, 16, pack_step, 0, unroll=2)
     list_jobs(offs_ref, counts_ref, active_ref, first, order_ref, jobs_ref)
     for load in loads:
         load.wait()
@@ -480,7 +478,7 @@
             hydro_ref[number, pl.ds(row, 1), :] = jnp.where(keep, value, 0.0)
         return carry
 
-    lax.fori_loop(0, 16, end_step, 0)
+    lax.fori_loop(0, 16, end_step, 0, unroll=2)
 
 
 def specs(kinds):
@@ -515,7 +513,7 @@
     smem = pl.BlockSpec(memory_space=pltpu.SMEM)
     pos = jnp.transpose(positions, (1, 0, 2))
     vel = jnp.transpose(velocity, (1, 0, 2))
-    requests = jnp.pad(neighbours.T.reshape(9, 48), ((0, 7), (0, 80)))
+    requests = jnp.pad(neighbours, ((0, 0), (0, 101)))
     shifts = jnp.asarray(shift_tiles())
     f32 = jnp.float32
 

time: 83.7 us -> 82.9 us (level)
  the two profiles are of different devices: /device:TPU:27 before, /device:TPU:18 now
where the time goes in v8:
time: 82.9 us; the launch traced here: 82.7 us
  Pallas kernels  81.4 us (98%)
  local copies, waits for them, and re-layouts  1.3 us (2%)
    pallas_call x1, Pallas kernels, shards(): pl.pallas_call(lambda *refs: gather_kernel(devices, *refs), out_shape=(fl...  56.4 us
    pallas_call x1, Pallas kernels, force_call(): pl.pallas_call(force_kernel, out_shape=floats(5, 16, 128), in_specs=specs...  25 us

profile of v8, /device:TPU:18, one launch (start us, length us, event | category | flops | bytes accessed | tf_op | source)
XLA Modules:
  0.0 82.7 jit_solution(15858306042921322590)
XLA Ops:
  0.0 1.3 %pad.4.refs_0_.refs_1_ = s32[16,128]{1,0:T(8,128)} pad(s32[16,27]{1,0:T(8,128)} %param.18, s32[]{:T(128)} %constant.1.clone.1), padding=0_0x0_101 | pad | bytes 9924 | tf_op jit(solution)/shard_map/jit(_pad)/pad | solution.py:516
  1.3 56.4 %cells.1 = (f32[432,8,128]{2,1,0:T(8,128)}, f32[432,1,128]{2,1,0:T(1,128)}, f32[16,1,128]{2,1,0:T(1,128)}, f32[7,2048,128]{2,1,0:T(8,128)}) custom-call(s32[16,128]{1,0:T(8,128)} %pad.4.refs_0_.refs_1_, s32[16,128]{1,0:T(8,128)} %pad.4.refs_0_.refs_1_, s32[1600]{0:T(1024)} %counts_ref.1, s32[16]{0:T(128)} %active_ref.1, f32[3,1600,128]{2,1,0:T(8,128)} %bitcast.5, ...), custom_call_target="tpu_custom_call" | custom-call | tf_op jit(solution)/shard_map/cells/pallas_call | solution.py:521
  57.7 25.0 %force.1 = f32[5,16,128]{2,1,0:T(8,128)} custom-call(s32[1600]{0:T(1024)} %counts_ref.1, s32[16]{0:T(128)} %active_ref.1, f32[7,2048,128]{2,1,0:T(8,128)} %get-tuple-element.9.columns_ref, f32[3456,128]{1,0:T(8,128)} %bitcast.7, f32[432,128]{1,0:T(8,128)} %bitcast.8, f32[27,8,128]{2,1,0:T(8,128)} %constant.4.clone.shift_ref, ...), custom_call_target="tpu_custom_call" | custom-call | tf_op jit(solution)/shard_map/force/pallas_call | solution.py:494

commit v9 on v8

--- a/solution.py
+++ b/solution.py
@@ -311,8 +311,9 @@
             return count + chunks
 
         count = lax.fori_loop(begin, end, one_row, count)
-        jobs_ref[count] = 31
-        count = count + (count & 1)
+        for extra in range(3):
+            jobs_ref[count + extra] = 31
+        count = (count + 3) & ~3
         jobs_ref[513 + number] = count
         begin = end
 
@@ -320,11 +321,11 @@
 def run_jobs(jobs_ref, step):
     for number, parts in enumerate((10, 12, 14, 16)):
         def two(pair, carry):
-            step(2 * pair, parts)
-            step(2 * pair + 1, parts)
+            for number in range(4):
+                step(4 * pair + number, parts)
             return carry
 
-        lax.fori_loop(jobs_ref[512 + number] >> 1, jobs_ref[513 + number] >> 1, two, 0)
+        lax.fori_loop(jobs_ref[512 + number] >> 2, jobs_ref[513 + number] >> 2, two, 0)
 
 
 def slope(ratio):

time: 82.9 us -> 82.8 us (level)
  the two profiles are of different devices: /device:TPU:18 before, /device:TPU:26 now
where the time goes in v9:
time: 82.8 us; the launch traced here: 81.7 us
  Pallas kernels  80.4 us (97%)
  local copies, waits for them, and re-layouts  1.3 us (2%)
    pallas_call x1, Pallas kernels, shards(): pl.pallas_call(lambda *refs: gather_kernel(devices, *refs), out_shape=(fl...  56.9 us
    pallas_call x1, Pallas kernels, force_call(): pl.pallas_call(force_kernel, out_shape=floats(5, 16, 128), in_specs=specs...  23.5 us

profile of v9, /device:TPU:26, one launch (start us, length us, event | category | flops | bytes accessed | tf_op | source)
XLA Modules:
  0.0 81.7 jit_solution(2902565972636105313)
XLA Ops:
  0.0 1.3 %pad.4.refs_0_.refs_1_ = s32[16,128]{1,0:T(8,128)} pad(s32[16,27]{1,0:T(8,128)} %param.18, s32[]{:T(128)} %constant.1.clone.1), padding=0_0x0_101 | pad | bytes 9924 | tf_op jit(solution)/shard_map/jit(_pad)/pad | solution.py:517
  1.3 56.9 %cells.1 = (f32[432,8,128]{2,1,0:T(8,128)}, f32[432,1,128]{2,1,0:T(1,128)}, f32[16,1,128]{2,1,0:T(1,128)}, f32[7,2048,128]{2,1,0:T(8,128)}) custom-call(s32[16,128]{1,0:T(8,128)} %pad.4.refs_0_.refs_1_, s32[16,128]{1,0:T(8,128)} %pad.4.refs_0_.refs_1_, s32[1600]{0:T(1024)} %counts_ref.1, s32[16]{0:T(128)} %active_ref.1, f32[3,1600,128]{2,1,0:T(8,128)} %bitcast.5, ...), custom_call_target="tpu_custom_call" | custom-call | tf_op jit(solution)/shard_map/cells/pallas_call | solution.py:522
  58.2 23.5 %force.1 = f32[5,16,128]{2,1,0:T(8,128)} custom-call(s32[1600]{0:T(1024)} %counts_ref.1, s32[16]{0:T(128)} %active_ref.1, f32[7,2048,128]{2,1,0:T(8,128)} %get-tuple-element.9.columns_ref, f32[3456,128]{1,0:T(8,128)} %bitcast.7, f32[432,128]{1,0:T(8,128)} %bitcast.8, f32[27,8,128]{2,1,0:T(8,128)} %constant.4.clone.shift_ref, ...), custom_call_target="tpu_custom_call" | custom-call | tf_op jit(solution)/shard_map/force/pallas_call | solution.py:495
